TPU v7x, 256 devices: a whole 4x4x8 slice. The times are simulated.
256 devices in a mesh: space: 16 (over x_hi, z), filt: 16 (over y, x_lo, core).
Axes of the slice: x: 4 (x_hi: 2, x_lo: 2; x = x_hi * 2 + x_lo), y: 4, z: 8, core: 2. Of those that a mesh axis runs over, the one named last changes fastest.
Arguments:
- volume: bfloat16 [1, 256, 64, 16, 128], P(None, 'filt', 'space'), may hold values from -6 to 6
- weight: bfloat16 [3, 3, 3, 256, 256], P(None, None, None, 'filt'), may hold values from -0.078125 to 0.078125
- cotangent: bfloat16 [1, 256, 64, 16, 128], P(None, 'filt', 'space'), may hold values from -6 to 6
Outputs:
- activated: bfloat16 [1, 256, 64, 16, 128], P(None, 'filt', 'space')
- input_grad: bfloat16 [1, 256, 64, 16, 128], P(None, 'filt', 'space')
- weight_grad: float32 [3, 3, 3, 256, 256], P(None, None, None, 'filt', 'space')
All inputs are finite; a program needn't handle non-finite values.
Results may differ from a plain program's by a relative error of at most 0.019.
Values may be sent and summed in bfloat16 or wider, within the bound.
No kernel may reach another device: no remote copies, remote signals or barrier semaphores. Data moves between devices by JAX's collectives and lax.ppermute only.
A program may use at most 128 MiB of HBM per device.

v0:
```python
import math

import jax
import jax.numpy as jnp
from jax import lax
from jax.sharding import PartitionSpec as P


def padded_2(cells, sides, width):
    for axis, dim in sides:
        count = lax.axis_size(axis)
        ends = count - 1
        head = lax.slice_in_dim(cells, 0, width, axis=dim)
        tail = lax.slice_in_dim(cells, cells.shape[dim] - width, cells.shape[dim], axis=dim)
        cells = jnp.concatenate(
            [
                lax.ppermute(tail, axis, [(i, (i + 1) % count) for i in range(ends)]),
                cells,
                lax.ppermute(head, axis, [((i + 1) % count, i) for i in range(ends)]),
            ],
            axis=dim,
        )
    return cells


def padded(field):
    return jnp.pad(field, ((0, 0), (0, 0), (0, 0), (1, 1), (1, 1)))


def stacked(field, planes):
    return jnp.concatenate([field[:, :, a : a + planes] for a in range(3)], axis=1)


def planar(product, channels, planes, height, breadth, flipped):
    lead = product.shape[0]
    parts = product.reshape(lead, 3, 3, channels, planes, height + 2, breadth + 2)
    summed = jnp.zeros((lead, channels, planes, height, breadth), jnp.float32)
    for b in range(3):
        for c in range(3):
            row_off = 2 - b if flipped else b
            col_off = 2 - c if flipped else c
            summed = (
                summed
                + parts[:, b, c, :, :, row_off : row_off + height, col_off : col_off + breadth]
            )
    return summed


def forward_part(matrix, shard_piece, channels, planes, height, breadth):
    columns = stacked(padded(shard_piece), planes)
    product = jnp.einsum("oc,bcdhw->bodhw", matrix, columns, preferred_element_type=jnp.float32)
    return planar(product, channels, planes, height, breadth, False)


def filter_part(grad_cols, shard_piece, planes, out_local):
    columns = stacked(padded(shard_piece), planes)
    summed = jnp.einsum("bodhw,bcdhw->co", grad_cols, columns, preferred_element_type=jnp.float32)
    return summed.reshape(3, shard_piece.shape[1], 3, 3, out_local)


def body(volume, weight, cotangent):
    batch, in_local, planes, height, breadth = volume.shape
    out_local = weight.shape[3]
    in_total = weight.shape[4]
    out_total = out_local * lax.axis_size("filt")
    grad_scale = 1.0 / math.sqrt(batch * planes * lax.axis_size("space") * height * breadth)
    reordered = jnp.transpose(weight, (1, 2, 3, 0, 4))
    haloed = padded_2(volume, (("space", 2),), 1)
    gathered = lax.all_gather(haloed, "filt", axis=1, tiled=True)
    pre = forward_part(
        reordered.reshape(9 * out_local, 3 * in_total), gathered, out_local, planes, height, breadth
    )
    activated = jax.nn.silu(pre).astype(jnp.bfloat16)
    sigma = jax.nn.sigmoid(pre)
    pre_grad = (cotangent.astype(jnp.float32) * sigma * (1.0 + pre * (1.0 - sigma))).astype(
        jnp.bfloat16
    )
    grad_cols = jnp.concatenate(
        [
            jnp.pad(pre_grad, ((0, 0), (0, 0), (0, 0), (b, 2 - b), (c, 2 - c)))
            for b in range(3)
            for c in range(3)
        ],
        axis=1,
    )
    filter_full = filter_part(grad_cols, gathered, planes, out_local)
    filter_local = jnp.transpose(filter_full, (0, 2, 3, 4, 1))
    weight_grad = (
        lax.psum_scatter(
            filter_local.astype(jnp.bfloat16), "space", scatter_dimension=4, tiled=True
        ).astype(jnp.float32)
        * grad_scale
    )
    grad_halo = padded_2(pre_grad, (("space", 2),), 1)
    by_output = jnp.transpose(weight, (0, 3, 1, 2, 4))
    weight_cols = lax.all_to_all(by_output, "filt", split_axis=4, concat_axis=1, tiled=True)
    grad_full = lax.all_gather(grad_halo, "filt", axis=1, tiled=True)
    flipped = weight_cols[::-1]
    matrix = jnp.transpose(flipped, (2, 3, 4, 0, 1)).reshape(9 * in_local, 3 * out_total)
    columns = stacked(padded(grad_full), planes)
    product = jnp.einsum("oc,bcdhw->bodhw", matrix, columns, preferred_element_type=jnp.float32)
    field_grad = planar(product, in_local, planes, height, breadth, True)
    return (activated, field_grad.astype(jnp.bfloat16), weight_grad)


def solution(mesh):
    in_specs = (
        P(None, "filt", "space", None, None),
        P(None, None, None, "filt", None),
        P(None, "filt", "space", None, None),
    )
    out_specs = (
        P(None, "filt", "space", None, None),
        P(None, "filt", "space", None, None),
        P(None, None, None, "filt", "space"),
    )
    return jax.shard_map(body, mesh=mesh, in_specs=in_specs, out_specs=out_specs, check_vma=False)
```

profile of v0, /device:TPU:1, one launch (start us, length us, event | category | flops | bytes accessed | tf_op | source)
XLA Modules:
  0.0 477.0 jit_solution(9113247387006721378)
XLA Ops:
  8.1 4.4 collective-permute-start
  13.8 3.9 collective-permute-done.1
  17.7 1.8 maximum_bitcast_fusion.4
  20.9 48.0 %all-gather.3.cloned.1.call-done = bf16[1,256,6,16,128]{4,3,2,0,1:T(8,128)(2,1)} async-done(((bf16[1,16,6,16,128]{4,3,2,0,1:T(8,128)(2,1)}), bf16[1,256,6,16,128]{4,3,2,0,1:T(8,128)(2,1)}) %all-gather.3.cloned.1.call-update) | async-done | bytes 6291472 | tf_op jit(solution)/shard_map/all_gather | solution.py:69
  68.9 9.2 %copy.73 = bf16[1,256,6,16,128]{1,4,3,2,0:T(8,128)(2,1)} copy(bf16[1,256,6,16,128]{4,3,2,0,1:T(8,128)(2,1)} %all-gather.3.cloned.1.call-done) | data formatting | bytes 12582912 | tf_op jit(solution)/shard_map/all_gather | solution.py:69
  78.1 11.5 %pad_slice_fusion.5 = (bf16[1,256,4,18,130]{1,4,3,2,0:T(8,128)(2,1)S(1)}, bf16[1,256,4,18,130]{1,4,3,2,0:T(8,128)(2,1)S(1)}, bf16[1,256,4,18,130]{1,4,3,2,0:T(8,128)(2,1)S(1)}) fusion(bf16[1,256,6,16,128]{1,4,3,2,0:T(8,128)(2,1)} %copy.73), kind=kLoop, calls=%fused_computation.16 | loop fusion | bytes 20668416 | tf_op jit(solution)/shard_map/slice | solution.py:31
  89.7 2.2 copy-done
  91.8 1.6 copy-done.1
  93.5 6.3 %pad_maximum_fusion = bf16[1,768,4,18,130]{1,4,3,2,0:T(8,128)(2,1)} fusion(bf16[1,256,4,18,130]{1,4,3,2,0:T(8,128)(2,1)S(1)} %get-tuple-element.22, bf16[1,256,4,18,130]{1,4,3,2,0:T(8,128)(2,1)S(1)} %get-tuple-element.21, bf16[1,256,4,18,130]{1,4,3,2,0:T(8,128)(2,1)S(1)} %get-tuple-element.20), kind=kLoop, calls=%fused_computation | loop fusion | flops 43130880 | bytes 28753920 | tf_op jit(solution)/shard_map/concatenate | solution.py:31
  99.8 9.1 %fusion.11 = f32[1,144,4,18,130]{1,4,3,2,0:T(8,128)} fusion(bf16[144,768,1,1]{1,0,2,3:T(8,128)(2,1)S(1)} %reshape.376, bf16[1,256,4,18,130]{1,4,3,2,0:T(8,128)(2,1)} %copy-done.1, bf16[1,256,4,18,130]{1,4,3,2,0:T(8,128)(2,1)} %copy-done, bf16[1,256,4,18,130]{1,4,3,2,0:T(8,128)(2,1)S(1)} %get-tuple-element.20), kind=kOutput, calls=%fused_computation.19 | convolution fusion | flops 2113413120 | bytes 19989504 | tf_op jit(solution)/shard_map/oc,bcdhw->bodhw/dot_general | solution.py:51
  108.9 12.3 %copy.75 = f32[1,144,4,18,130]{4,1,3,2,0:T(8,128)} copy(f32[1,144,4,18,130]{1,4,3,2,0:T(8,128)} %fusion.11) | data formatting | bytes 10782720 | tf_op jit(solution)/shard_map/oc,bcdhw->bodhw/transpose | solution.py:51
  121.2 4.2 multiply_convert_fusion
  134.7 27.1 %dot_general.21 = bf16[3,256,4,18,130]{1,0,4,3,2:T(4,128)(2,1)} reshape(bf16[1,768,4,18,130]{1,4,3,2,0:T(8,128)(2,1)} %pad_maximum_fusion) | data formatting | bytes 28753920 | tf_op jit(solution)/shard_map/bodhw,bcdhw->co/dot_general | solution.py:57
  161.8 12.0 %fusion.25 = bf16[3,3,3,16,256]{4,3,2,1,0:T(8,128)(2,1)} fusion(bf16[3,3,16,4,18,130]{5,2,1,0,4,3:T(8,128)(2,1)} %bitcast.19, bf16[3,256,4,18,130,1,1]{1,0,4,3,2,6,5:T(4,128)(2,1)} %bitcast.76), kind=kOutput, calls=%fused_computation.24 | convolution fusion | flops 2070392832 | bytes 17293824 | tf_op jit(solution)/shard_map/bodhw,bcdhw->co/dot_general | solution.py:57
  173.8 3.5 copy.93
  177.3 2.2 reshape.383
  179.5 3.2 collective-permute-start.2
  184.0 3.7 collective-permute-done.3
  188.7 3.3 copy.79
  192.0 2.5 bitcast_bitcast_fusion
  194.5 2.2 reshape.385
  196.6 13.2 %all_to_all.18 = bf16[16,2,3456]{2,1,0:T(2,128)(2,1)S(1)} all-to-all(bf16[16,2,3456]{2,1,0:T(2,128)(2,1)S(1)} %reshape.385), channel_id=1, replica_groups=mesh['space'=16,'filt'=16] {'filt'}, dimensions={0} | all-to-all | bytes 442368 | tf_op jit(solution)/shard_map/all_to_all | solution.py:96
  209.8 2.2 reshape.386
  212.0 2.7 copy.115
  214.8 2.8 all_to_all.16
  218.9 152.4 %reduce-scatter.4.cloned.1.call-done = bf16[16,432]{1,0:T(8,128)(2,1)} async-done(((bf16[256,432]{1,0:T(8,128)(2,1)}), bf16[16,432]{1,0:T(8,128)(2,1)}) %reduce-scatter.4.cloned.1.call-update) | async-done | bytes 13840
  373.0 48.7 %all-gather.5.cloned.1.call-done = bf16[1,256,6,16,128]{4,3,2,0,1:T(8,128)(2,1)} async-done(((bf16[1,16,6,16,128]{4,3,2,0,1:T(8,128)(2,1)}), bf16[1,256,6,16,128]{4,3,2,0,1:T(8,128)(2,1)}) %all-gather.5.cloned.1.call-update) | async-done | bytes 6291472 | tf_op jit(solution)/shard_map/all_gather | solution.py:97
  421.8 9.2 %copy.78 = bf16[1,256,6,16,128]{1,4,3,2,0:T(8,128)(2,1)} copy(bf16[1,256,6,16,128]{4,3,2,0,1:T(8,128)(2,1)} %all-gather.5.cloned.1.call-done) | data formatting | bytes 12582912 | tf_op jit(solution)/shard_map/all_gather | solution.py:97
  430.9 13.2 %pad_slice_fusion.2 = (bf16[1,256,4,18,130]{1,4,3,2,0:T(8,128)(2,1)S(1)}, bf16[1,256,4,18,130]{1,4,3,2,0:T(8,128)(2,1)}, bf16[1,256,4,18,130]{1,4,3,2,0:T(8,128)(2,1)}) fusion(bf16[1,256,6,16,128]{1,4,3,2,0:T(8,128)(2,1)} %copy.78), kind=kLoop, calls=%fused_computation.13 | loop fusion | bytes 20668416 | tf_op jit(solution)/shard_map/slice | solution.py:31
  444.1 9.2 %fusion.14 = f32[1,144,4,18,130]{1,4,3,2,0:T(8,128)} fusion(bf16[1,256,4,18,130]{1,4,3,2,0:T(8,128)(2,1)} %get-tuple-element.19, bf16[1,256,4,18,130]{1,4,3,2,0:T(8,128)(2,1)} %get-tuple-element.18, bf16[1,256,4,18,130]{1,4,3,2,0:T(8,128)(2,1)S(1)} %get-tuple-element.17, bf16[144,768,1,1]{1,0,2,3:T(8,128)(2,1)S(1)} %reshape.377), kind=kOutput, calls=%fused_computation.20 | convolution fusion | flops 2113413120 | bytes 19989504 | tf_op jit(solution)/shard_map/oc,bcdhw->bodhw/dot_general | solution.py:101
  453.2 12.3 %copy.82 = f32[1,144,4,18,130]{4,1,3,2,0:T(8,128)} copy(f32[1,144,4,18,130]{1,4,3,2,0:T(8,128)} %fusion.14) | data formatting | bytes 10782720 | tf_op jit(solution)/shard_map/oc,bcdhw->bodhw/transpose | solution.py:101
  465.5 4.2 fusion.32
  (40 shorter events, 19.0 us)
Async XLA Ops:
  7.2 61.7 %all-gather.3.cloned.1.call-start = ((), (), s32[]{:S(2)}) async-start(), calls=%async_computation.2 | async-start | bytes 6684672 | tf_op jit(solution)/shard_map/all_gather | solution.py:69
  8.1 5.7 %collective-permute-start = (bf16[1,16,1,16,128]{4,3,2,1,0:T(8,128)(2,1)S(1)}, bf16[1,16,1,16,128]{4,3,2,1,0:T(8,128)(2,1)S(1)}, u32[]{:S(2)}, u32[]{:S(2)}) collective-permute-start(bf16[1,16,1,16,128]{4,3,2,1,0:T(8,128)(2,1)S(1)} %get-tuple-element.25), channel_id=1, source_target_pairs={{0,16},{16,32},{32,48},{48,64},{64,80},{80,96},{96,112},{112,128},... | collective-permute-start | bytes 196616 | tf_op jit(solution)/shard_map/ppermute | solution.py:17
  12.5 5.2 %collective-permute-start.1 = (bf16[1,16,1,16,128]{4,3,2,1,0:T(8,128)(2,1)S(1)}, bf16[1,16,1,16,128]{4,3,2,1,0:T(8,128)(2,1)S(1)}, u32[]{:S(2)}, u32[]{:S(2)}) collective-permute-start(bf16[1,16,1,16,128]{4,3,2,1,0:T(8,128)(2,1)S(1)} %get-tuple-element.26), channel_id=1, source_target_pairs={{16,0},{32,16},{48,32},{64,48},{80,64},{96,80},{112,96},{128,112},... | collective-permute-start | bytes 196616 | tf_op jit(solution)/shard_map/ppermute | solution.py:19
  19.5 351.8 %reduce-scatter.4.cloned.1.call-start = ((), (), s32[]{:S(2)}) async-start(), calls=%async_computation.4 | async-start | bytes 278528
  89.6 2.2 copy-start
  89.7 3.8 copy-start.1
  108.9 12.3 %copy-start.3 = (bf16[1,16,4,16,128]{4,3,2,1,0:T(8,128)(2,1)S(1)}, bf16[1,16,4,16,128]{4,3,2,1,0:T(8,128)(2,1)}, u32[]{:S(2)}) copy-start(bf16[1,16,4,16,128]{4,3,2,1,0:T(8,128)(2,1)} %param.5) | copy-start | bytes 786436
  173.8 14.9 %copy-start.2 = (bf16[3,3,3,16,256]{4,3,2,1,0:T(8,128)(2,1)S(1)}, bf16[3,3,3,16,256]{4,3,2,1,0:T(8,128)(2,1)}, u32[]{:S(2)}) copy-start(bf16[3,3,3,16,256]{4,3,2,1,0:T(8,128)(2,1)} %param.4) | copy-start | bytes 663556
  179.5 242.3 %all-gather.5.cloned.1.call-start = ((), (), s32[]{:S(2)}) async-start(), calls=%async_computation.3 | async-start | bytes 6684672 | tf_op jit(solution)/shard_map/all_gather | solution.py:97
  179.5 4.5 collective-permute-start.2
  182.7 5.0 %collective-permute-start.3 = (bf16[1,16,1,16,128]{4,1,3,2,0:T(8,128)(2,1)S(1)}, bf16[1,16,1,16,128]{4,1,3,2,0:T(8,128)(2,1)S(1)}, u32[]{:S(2)}, u32[]{:S(2)}) collective-permute-start(bf16[1,16,1,16,128]{4,1,3,2,0:T(8,128)(2,1)S(1)} %get-tuple-element.24), channel_id=1, source_target_pairs={{16,0},{32,16},{48,32},{64,48},{80,64},{96,80},{112,96},{128,112},... | collective-permute-start | bytes 196616 | tf_op jit(solution)/shard_map/ppermute | solution.py:19
Sparse Core Ops, SparseCore 0:
  19.6 49.2 all-gather.2
  179.6 191.6 reduce-scatter.3
  373.3 48.3 all-gather.4
where the time goes:
time: 479 us; the launch traced here: 477 us
  waiting for transfers between devices  257 us (54%)
  local copies, waits for them, and re-layouts  135 us (28%)
  matrix products  30.3 us (6%)
  other arithmetic  17.3 us (4%)
  between operations  13.9 us (3%)
  blocking collectives  13.2 us (3%)
  starting transfers between devices  10.3 us (2%)
    unnamed x4, waiting for transfers between devices  152 us
    all_gather x1, waiting for transfers between devices, body(): grad_full = lax.all_gather(grad_halo, 'filt', axis=1, tiled=True)  48.7 us
    all_gather x1, waiting for transfers between devices, body(): gathered = lax.all_gather(haloed, 'filt', axis=1, tiled=True)  48 us
    unnamed x26, local copies, waits for them, and re-layouts  30.3 us
    dot_general x1, local copies, waits for them, and re-layouts, filter_part(): jnp.einsum('bodhw,bcdhw->co', grad_cols, columns, preferred_element_type=...  27.1 us
    slice x2, local copies, waits for them, and re-layouts, stacked(): field[:, :, a:a + planes]  24.7 us
    all_to_all x1, blocking collectives, body(): lax.all_to_all(by_output, 'filt', split_axis=4, concat_axis=1, tiled=True)  13.2 us
    transpose x1, local copies, waits for them, and re-layouts, forward_part(): jnp.einsum('oc,bcdhw->bodhw', matrix, columns, preferred_element_type=jnp...  12.3 us
  transfers between devices with their start and end apart: 7, of which 5 were waited for; matrix products, arithmetic and copies ran while one was open for 4% of the time, Pallas kernels for 0%

commit v1 on v0

v1 whole, which is shorter than its diff:
```python
import functools
import math

import jax
import jax.numpy as jnp
from jax import lax
from jax.experimental import pallas as pl
from jax.experimental.pallas import tpu as pltpu
from jax.sharding import Mesh, PartitionSpec as P

BREADTH = 128
GROUP = 4
VMEM_LIMIT = 40 * 1024 * 1024


def lane_shifted(value, by):
    if by == 0:
        return value
    lanes = value.shape[1]
    column = lax.broadcasted_iota(jnp.int32, value.shape, 1) % BREADTH
    moved = pltpu.roll(value, (-by) % lanes, 1)
    return jnp.where(column == (BREADTH - 1 if by > 0 else 0), 0.0, moved)


def row_shifted(value, by):
    if by == 0:
        return value
    gap = jnp.zeros((value.shape[0], BREADTH), value.dtype)
    if by > 0:
        return jnp.concatenate([value[:, BREADTH:], gap], axis=1)
    return jnp.concatenate([gap, value[:, :-BREADTH]], axis=1)


def folded(product, channels):
    total = None
    for c in range(3):
        column = None
        for b in range(3):
            at = (b * 3 + c) * channels
            part = row_shifted(product[at : at + channels], b - 1)
            column = part if column is None else column + part
        column = lane_shifted(column, c - 1)
        total = column if total is None else total + column
    return total


def partner(place_ref, axis, j):
    step = {"part": 1, "run": GROUP}[axis]
    return ((place_ref[0] // step) % GROUP) ^ j


def plane_of(space, part):
    return part ^ (part // 2) ^ ((space % 2) * (GROUP - 1))


def partner_plane(place_ref, j):
    return plane_of(place_ref[0] // GROUP**2, (place_ref[0] % GROUP) ^ j)


def at_end(place_ref, last):
    space, plane = place_ref[0] // GROUP**2, partner_plane(place_ref, 0)
    if last is None:
        return (space == 0) & (plane == 0)
    return (space == last) & (plane == GROUP - 1)


def unless(condition, value):
    return jnp.where(condition, jnp.zeros_like(value), value)


def block_rows(place_ref, axis, j, rows):
    return pl.ds(pl.multiple_of(partner(place_ref, axis, j) * rows, rows), rows)


def call(kernel, outputs, name, place, *operands, unread=(), scratch=()):
    def run(place_ref, *refs):
        kernel(place_ref, *refs[: len(operands)], *refs[len(operands) + len(unread) :])

    return pl.pallas_call(
        run,
        in_specs=[pl.BlockSpec(memory_space=pltpu.SMEM)]
        + [pl.BlockSpec(memory_space=pltpu.VMEM)] * len(operands)
        + [pl.BlockSpec(memory_space=pl.ANY)] * len(unread),
        out_specs=[pl.BlockSpec(memory_space=pltpu.VMEM)] * len(outputs),
        out_shape=[jax.ShapeDtypeStruct(shape, dtype) for shape, dtype in outputs],
        scratch_shapes=list(scratch),
        compiler_params=pltpu.CompilerParams(vmem_limit_bytes=VMEM_LIMIT),
        cost_estimate=pl.CostEstimate(flops=1, bytes_accessed=1, transcendentals=0),
        name=name,
    )(place, *operands, *unread)


def planes_kernel(place_ref, value_ref, out_ref):
    channels, planes, height, breadth = value_ref.shape
    for p in range(planes):
        value = value_ref[:, plane_of(place_ref[0] // GROUP**2, p)].astype(jnp.float32)
        out_ref[p] = value.reshape(channels, height * breadth).astype(out_ref.dtype)


def partner_planes_kernel(place_ref, value_ref, *outs):
    channels, _, height, breadth = value_ref.shape
    for j, out_ref in enumerate(outs):
        value = value_ref[:, partner_plane(place_ref, j)].astype(jnp.float32)
        out_ref[...] = value.reshape(channels, height * breadth).astype(out_ref.dtype)


def same_kernel(place_ref, value_ref, out_ref):
    del place_ref
    out_ref[...] = value_ref[...]


def halves_kernel(place_ref, value_ref, low_ref, high_ref):
    del place_ref
    half = low_ref.shape[0]
    low_ref[...] = value_ref[:half]
    high_ref[...] = value_ref[half:]


def edge_sums(place_ref, field_ref, matrices, out_ref, a):
    channels = out_ref.shape[0] // GROUP
    rows = 9 * channels
    for j, matrix_ref in enumerate(matrices):
        product = jnp.dot(
            matrix_ref[a * rows : (a + 1) * rows],
            field_ref[...],
            preferred_element_type=jnp.float32,
        )
        block = block_rows(place_ref, "part", j, channels)
        out_ref[block, :] = folded(product, channels).astype(out_ref.dtype)


def after_kernel(place_ref, *refs):
    halves, matrices = refs[: 2 * GROUP], refs[2 * GROUP : 3 * GROUP]
    field_ref, after_ref = refs[3 * GROUP :]
    for k, part_ref in enumerate(halves):
        half = part_ref.shape[0]
        start = partner(place_ref, "run", k // 2) * 2 * half + (k % 2) * half
        field_ref[pl.ds(pl.multiple_of(start, half), half), :] = part_ref[...]
    edge_sums(place_ref, field_ref, matrices, after_ref, 0)


def before_kernel(place_ref, field_ref, *refs):
    edge_sums(place_ref, field_ref, refs[:GROUP], refs[GROUP], 2)


def centre_kernel(place_ref, field_ref, *refs):
    edge_sums(place_ref, field_ref, refs[:GROUP], refs[GROUP], 1)


def gate_kernel(place_ref, same_ref, before_ref, after_ref, *refs, last):
    cotangents, active_ref, grad_ref = refs[:GROUP], refs[GROUP], refs[GROUP + 1]
    channels = cotangents[0].shape[0]
    for j, cotangent_ref in enumerate(cotangents):
        block = block_rows(place_ref, "part", j, channels)
        pre = (
            same_ref[block, :]
            + unless(at_end(place_ref, last), before_ref[block, :].astype(jnp.float32))
            + unless(at_end(place_ref, None), after_ref[block, :].astype(jnp.float32))
        )
        sigma = jax.nn.sigmoid(pre)
        active_ref[block, :] = (pre * sigma).astype(active_ref.dtype)
        grad_ref[block, :] = (
            cotangent_ref[...].astype(jnp.float32) * sigma * (1.0 + pre * (1.0 - sigma))
        ).astype(grad_ref.dtype)


def fill_moved(place_ref, moved_ref, grad_ref, low_ref, high_ref, last):
    plane = grad_ref.shape[1]
    stride = plane + 2 * BREADTH
    gap = jnp.zeros((grad_ref.shape[0], BREADTH), moved_ref.dtype)
    for p, ref in enumerate((low_ref, grad_ref, high_ref)):
        source = ref[...].astype(jnp.float32)
        if p != 1:
            source = unless(at_end(place_ref, last if p else None), source)
        for c in range(3):
            moved_ref[c, :, p * stride : p * stride + BREADTH] = gap
            moved_ref[c, :, p * stride + BREADTH : p * stride + BREADTH + plane] = lane_shifted(
                source, 1 - c
            ).astype(moved_ref.dtype)
            moved_ref[c, :, (p + 1) * stride - BREADTH : (p + 1) * stride] = gap


def tap_rows(moved_ref, block, plane):
    stride = plane + 2 * BREADTH
    parts = []
    for a in range(3):
        for b in range(3):
            for c in range(3):
                at = (2 - a) * stride + (2 - b) * BREADTH
                parts.append(moved_ref[c, block, at : at + plane])
    return jnp.concatenate(parts, axis=0)


def filter_kernel(place_ref, field_ref, grad_ref, low_ref, high_ref, *refs, last):
    outs, moved_ref = refs[:GROUP], refs[GROUP]
    rows, plane = grad_ref.shape
    fill_moved(place_ref, moved_ref, grad_ref, low_ref, high_ref, last)
    for j, out_ref in enumerate(outs):
        sums = lax.dot_general(
            field_ref[...],
            tap_rows(moved_ref, block_rows(place_ref, "part", j, rows // GROUP), plane),
            (((1,), (1,)), ((), ())),
            preferred_element_type=jnp.float32,
        )
        out_ref[...] = sums.astype(out_ref.dtype)


def input_kernel(place_ref, grad_ref, low_ref, high_ref, *refs, last):
    matrices, outs = refs[:GROUP], refs[GROUP : GROUP + 7]
    moved_ref, sum_ref = refs[GROUP + 7 :]
    rows, plane = grad_ref.shape
    fill_moved(place_ref, moved_ref, grad_ref, low_ref, high_ref, last)
    for j, matrix_ref in enumerate(matrices):
        part = lax.dot_general(
            matrix_ref[...],
            tap_rows(moved_ref, block_rows(place_ref, "part", j, rows // GROUP), plane),
            (((0,), (0,)), ((), ())),
            preferred_element_type=jnp.float32,
        )
        if j == 0:
            sum_ref[...] = part
        else:
            sum_ref[...] += part
    half = outs[1].shape[0]
    for out_ref, (j, start) in zip(outs, INPUT_CUTS):
        start = partner(place_ref, "run", j) * 2 * half + start * half
        block = pl.ds(pl.multiple_of(start, half), out_ref.shape[0])
        out_ref[...] = sum_ref[block, :].astype(out_ref.dtype)


INPUT_CUTS = ((0, 0), (2, 0), (2, 1), (1, 0), (3, 1), (1, 1), (3, 0))


def join_kernel(place_ref, near_ref, other_ref, high_ref, low_ref, near_out, other_out):
    del place_ref
    near_out[...] = (near_ref[...] + high_ref[...].astype(jnp.float32)).astype(near_out.dtype)
    other_out[...] = (other_ref[...] + low_ref[...].astype(jnp.float32)).astype(other_out.dtype)


def lift_kernel(place_ref, value_ref, other_ref, out_ref):
    del place_ref
    total = value_ref[...].astype(jnp.float32) + other_ref[...].astype(jnp.float32)
    out_ref[...] = total.astype(out_ref.dtype)


def merge_kernel(place_ref, *refs):
    del place_ref
    values, out_ref = refs[:-1], refs[-1]
    total = values[0][...].astype(jnp.float32)
    for ref in values[1:]:
        total += ref[...].astype(jnp.float32)
    out_ref[...] = total.astype(out_ref.dtype)


def pair_kernel(place_ref, own_ref, *refs):
    halves, active_ref, outs, sum_ref = refs[:4], refs[4], refs[5 : 5 + GROUP], refs[5 + GROUP]
    half = halves[0].shape[0]
    for k in range(2):
        rows = slice(k * half, (k + 1) * half)
        sum_ref[rows, :] = (
            own_ref[rows, :]
            + halves[k][...].astype(jnp.float32)
            + halves[2 + k][...].astype(jnp.float32)
        )
    for j, out_ref in enumerate(outs):
        block = block_rows(place_ref, "part", j, out_ref.shape[1])
        out_ref[0] = active_ref[block, :]
        out_ref[1] = sum_ref[block, :].astype(out_ref.dtype)


def close_kernel(place_ref, *refs):
    pairs, outs = refs[:GROUP], refs[GROUP:]
    for j, pair_ref in enumerate(pairs):
        for k, out_ref in enumerate(outs):
            channels, _, height, breadth = out_ref.shape
            value = pair_ref[k].astype(jnp.float32).reshape(channels, height, breadth)
            out_ref[:, partner_plane(place_ref, j)] = value.astype(out_ref.dtype)


def total_kernel(place_ref, parts_ref, out_ref, *, scale):
    del place_ref
    total = parts_ref[0].astype(jnp.float32)
    for s in range(1, parts_ref.shape[0]):
        total += parts_ref[s].astype(jnp.float32)
    out_ref[...] = jnp.transpose(total * scale)


DEPTH = ("space", "part")
CHANNELS = ("run", "part")


def shifted(value, by):
    count = lax.axis_size(DEPTH)
    at = {
        space * GROUP + plane_of(space, part): space * GROUP + part
        for space in range(count // GROUP)
        for part in range(GROUP)
    }
    return lax.ppermute(value, DEPTH, [(at[i], at[(i + by) % count]) for i in range(count)])


def swap(value, axis, j):
    return lax.ppermute(value, axis, [(i, i ^ j) for i in range(lax.axis_size(axis))])


def swapped(values, axis):
    return [values[0]] + [swap(values[j], axis, j) for j in range(1, GROUP)]


def body(volume, weight, cotangent):
    batch, in_local, planes, height, breadth = volume.shape
    out_local, in_total = weight.shape[3:]
    spaces = lax.axis_size("space")
    plane = height * breadth
    rows, depth, taps = GROUP * out_local, GROUP * in_local, 27 * out_local
    half = depth // 2
    grad_scale = 1.0 / math.sqrt(batch * planes * plane * spaces)
    bf16, f32 = jnp.bfloat16, jnp.float32
    place = lax.axis_index(("space", "run", "part")).reshape(1)
    ends = {"last": spaces - 1}

    (field,) = call(
        planes_kernel, [((planes, in_local, plane), bf16)], "volume_planes", place, volume[0]
    )
    field = lax.all_to_all(field, "part", split_axis=0, concat_axis=0, tiled=True)
    low, high = call(
        halves_kernel, [((half, plane), bf16)] * 2, "halves", place, field.reshape(depth, plane)
    )
    low_1, high_3 = swap(low, "run", 1), swap(high, "run", 3)
    high_1, low_3 = swap(high, "run", 1), swap(low, "run", 3)
    (matrix,) = call(
        same_kernel,
        [((taps, in_total), bf16)],
        "filters",
        place,
        weight.reshape(taps, in_total),
        unread=[low],
    )
    matrix_1, matrix_2 = swap(matrix, "part", 1), swap(matrix, "part", 2)
    low_2, high_2 = swap(low_1, "run", 3), swap(high_3, "run", 1)
    matrices = [matrix, matrix_1, matrix_2, swap(matrix_2, "part", 1)]
    cotangents = call(
        partner_planes_kernel,
        [((out_local, plane), bf16)] * GROUP,
        "cotangent_planes",
        place,
        cotangent[0],
        unread=[low_1, high_3],
    )
    cotangents = swapped(cotangents, "part")

    field, after = call(
        after_kernel,
        [((in_total, plane), bf16), ((rows, plane), bf16)],
        "after",
        place,
        *(low, high, low_1, high_1, low_2, high_2, low_3, high_3),
        *matrices,
    )
    after = shifted(after, 1)
    (before,) = call(
        before_kernel, [((rows, plane), bf16)], "before", place, field, *matrices
    )
    (same,) = call(
        centre_kernel,
        [((rows, plane), f32)],
        "centre",
        place,
        field,
        *matrices,
        unread=[before],
    )
    before = shifted(before, -1)
    active, grad = call(
        functools.partial(gate_kernel, **ends),
        [((rows, plane), bf16)] * 2,
        "gate",
        place,
        same,
        before,
        after,
        *cotangents,
    )

    around = (grad, shifted(grad, 1), shifted(grad, -1))
    moved = pltpu.VMEM((3, rows, 3 * (plane + 2 * BREADTH)), bf16)
    sums, sums_1, sums_2, sums_3 = call(
        functools.partial(filter_kernel, **ends),
        [((in_total, taps), bf16)] * GROUP,
        "filter_sums",
        place,
        field,
        *around,
        scratch=[moved],
    )
    sums_3, sums_1 = swap(sums_3, "part", 1), swap(sums_1, "part", 1)
    own, far_low, far_high, low_1, high_3, high_1, low_3 = call(
        functools.partial(input_kernel, **ends),
        [((depth, plane), f32)] + [((half, plane), bf16)] * 4 + [((half, plane), f32)] * 2,
        "input_sums",
        place,
        *around,
        *matrices,
        unread=[sums],
        scratch=[moved, pltpu.VMEM((in_total, plane), f32)],
    )
    far_low, far_high = swap(far_low, "run", 1), swap(far_high, "run", 3)
    low_1, high_3 = swap(low_1, "run", 1), swap(high_3, "run", 3)
    high_1, low_3 = call(
        join_kernel,
        [((half, plane), bf16)] * 2,
        "join",
        place,
        high_1,
        low_3,
        far_high,
        far_low,
    )
    high_1, low_3 = swap(high_1, "run", 1), swap(low_3, "run", 3)
    (sums_2,) = call(
        lift_kernel, [((in_total, taps), bf16)], "lift", place, sums_2, sums_3, unread=[far_low]
    )
    pairs = call(
        pair_kernel,
        [((2, in_local, plane), bf16)] * GROUP,
        "pairs",
        place,
        *(own, low_1, high_1, low_3, high_3),
        active,
        unread=[sums_2],
        scratch=[pltpu.VMEM((depth, plane), f32)],
    )
    sums_2 = swap(sums_2, "part", 2)
    pairs = swapped(pairs, "part")
    (sums,) = call(
        merge_kernel,
        [((in_total, taps), bf16)],
        "merge",
        place,
        *(sums, sums_1, sums_2),
        unread=[pairs[1]],
    )
    sums = lax.all_to_all(
        sums.reshape(spaces, in_total // spaces, taps),
        "space",
        split_axis=0,
        concat_axis=0,
        tiled=True,
    )
    (total,) = call(
        functools.partial(total_kernel, scale=grad_scale),
        [((taps, in_total // spaces), f32)],
        "total",
        place,
        sums,
    )
    active, back = call(
        close_kernel,
        [((in_local, planes, height, breadth), bf16)] * 2,
        "close",
        place,
        *pairs,
    )
    return (
        active[None],
        back[None],
        total.reshape(3, 3, 3, out_local, in_total // spaces),
    )


def solution(mesh):
    spaces, filts = mesh.devices.shape
    cut = Mesh(mesh.devices.reshape(spaces, filts // GROUP, GROUP), ("space", "run", "part"))
    in_specs = (
        P(None, CHANNELS, "space", None, None),
        P(None, None, None, CHANNELS, None),
        P(None, CHANNELS, "space", None, None),
    )
    out_specs = (
        P(None, CHANNELS, "space", None, None),
        P(None, CHANNELS, "space", None, None),
        P(None, None, None, CHANNELS, "space"),
    )
    return jax.shard_map(body, mesh=cut, in_specs=in_specs, out_specs=out_specs, check_vma=False)
```

time: 479 us -> 103 us (0.22)
  waiting for transfers between devices: 257 us -> 27.3 us
  local copies, waits for them, and re-layouts: 135 us -> 1.86 us
  starting transfers between devices: 10.3 us -> 49.9 us
  matrix products: 30.3 us -> 0 us
  other arithmetic: 17.3 us -> 0 us
  between operations: 13.9 us -> 0.79 us
  Pallas kernels: 0 us -> 12.4 us
    unnamed x4 -> x0, waiting for transfers between devices: 152 us -> none
    all_gather x2 -> x0, waiting for transfers between devices: 96.8 us -> none  [the longest x1 48.7 us: body(): grad_full = lax.all_gather(grad_halo, 'filt', axis=1, tiled=True)]
    ppermute x4 -> x28, starting transfers between devices: 10.1 us -> 46.4 us  [the longest x24 40 us: swap(): lax.ppermute(value, axis, [(i, i ^ j) for i in range(lax.axis_size(axis))])]
    dot_general x3 -> x0, matrix products: 30.3 us -> none  [the longest x1 12 us: filter_part(): jnp.einsum('bodhw,bcdhw->co', grad_cols, columns, preferred_element_type=...]
    unnamed x26 -> x6, local copies, waits for them, and re-layouts: 30.3 us -> 1.86 us
    dot_general x1 -> x0, local copies, waits for them, and re-layouts: 27.1 us -> none  [filter_part(): jnp.einsum('bodhw,bcdhw->co', grad_cols, columns, preferred_element_type=...]
    transpose x5 -> x0, local copies, waits for them, and re-layouts: 25.9 us -> none  [the longest x1 12.3 us: forward_part(): jnp.einsum('oc,bcdhw->bodhw', matrix, columns, preferred_element_type=jnp...]
    slice x4 -> x0, local copies, waits for them, and re-layouts: 25.6 us -> none  [the longest x2 24.7 us: stacked(): field[:, :, a:a + planes]]
  transfers between devices with their start and end apart: 7 -> 29, of which waited for: 5 -> 15; matrix products, arithmetic and copies ran while one was open for 4% -> 0% of each run, Pallas kernels for 0% -> 5%
where the time goes in v1:
time: 103 us
  starting transfers between devices  49.9 us (48%)
  waiting for transfers between devices  27.3 us (27%)
  Pallas kernels  12.4 us (12%)
  blocking collectives  10.6 us (10%)
  local copies, waits for them, and re-layouts  1.86 us (2%)
    ppermute x24, starting transfers between devices, swap(): lax.ppermute(value, axis, [(i, i ^ j) for i in range(lax.axis_size(axis))])  40 us
    ppermute x24, waiting for transfers between devices, swap(): lax.ppermute(value, axis, [(i, i ^ j) for i in range(lax.axis_size(axis))])  24 us
    pallas_call x16, Pallas kernels, call(): pl.pallas_call(run, in_specs=[pl.BlockSpec(memory_space=pltpu.SMEM)] + [p...  12.4 us
    all_to_all x1, blocking collectives, body(): lax.all_to_all(field, 'part', split_axis=0, concat_axis=0, tiled=True)  10.6 us
    ppermute x4, starting transfers between devices, shifted(): lax.ppermute(value, DEPTH, [(at[i], at[(i + by) % count]) for i in range(...  6.33 us
    all_to_all x1, starting transfers between devices, body(): lax.all_to_all(sums.reshape(spaces, in_total // spaces, taps), 'space', s...  3.53 us
    ppermute x4, waiting for transfers between devices, shifted(): lax.ppermute(value, DEPTH, [(at[i], at[(i + by) % count]) for i in range(...  3.32 us
  transfers between devices with their start and end apart: 29, of which 15 were waited for; matrix products, arithmetic and copies ran while one was open for 0% of the time, Pallas kernels for 5%

profile of v1, /device:TPU:1, one launch (start us, length us, event | category | flops | bytes accessed | tf_op | source)
XLA Modules:
  0.0 102.9 jit_solution(1524679493817615982)
XLA Ops:
  1.7 10.6 %all_to_all.10 = bf16[4,16,2048]{2,1,0:T(8,128)(2,1)S(1)} all-to-all(bf16[4,16,2048]{2,1,0:T(8,128)(2,1)S(1)} %volume_planes.1), channel_id=1, replica_groups=mesh['space'=16,'run'=4,'part'=4] {'part'}, dimensions={0} | all-to-all | bytes 524288 | tf_op jit(solution)/shard_map/all_to_all | solution.py:325
  13.9 1.2 %collective-permute-start.3 = (bf16[32,2048]{1,0:T(8,128)(2,1)S(1)}, bf16[32,2048]{1,0:T(8,128)(2,1)S(1)}, u32[]{:S(2)}, u32[]{:S(2)}) collective-permute-start(bf16[32,2048]{1,0:T(8,128)(2,1)S(1)} %get-tuple-element.33.refs_1_), channel_id=1, source_target_pairs={{0,12},{4,8},{8,4},{12,0},{1,13},{5,9},{9,5},{13,1},{2,14},{6,10},... | collective-permute-start | bytes 393224 | tf_op jit(solution)/shard_map/ppermute | solution.py:303
  15.1 1.5 %collective-permute-start = (bf16[32,2048]{1,0:T(8,128)(2,1)S(1)}, bf16[32,2048]{1,0:T(8,128)(2,1)S(1)}, u32[]{:S(2)}, u32[]{:S(2)}) collective-permute-start(bf16[32,2048]{1,0:T(8,128)(2,1)S(1)} %get-tuple-element.32.refs_1_.refs_0_), channel_id=1, source_target_pairs={{0,4},{4,0},{8,12},{12,8},{1,5},{5,1},{9,13},{13,9},{2,6},{6,2},{1... | collective-permute-start | bytes 393224 | tf_op jit(solution)/shard_map/ppermute | solution.py:303
  16.6 1.7 %collective-permute-start.6 = (bf16[432,256]{1,0:T(8,128)(2,1)S(1)}, bf16[432,256]{1,0:T(8,128)(2,1)S(1)}, u32[]{:S(2)}, u32[]{:S(2)}) collective-permute-start(bf16[432,256]{1,0:T(8,128)(2,1)S(1)} %filters.1.refs_8_.refs_1_.refs_3_), channel_id=1, source_target_pairs={{0,1},{1,0},{2,3},{3,2},{4,5},{5,4},{6,7},{7,6},{8,9},{9,8},{10,11... | collective-permute-start | bytes 663560 | tf_op jit(solution)/shard_map/ppermute | solution.py:303
  18.3 1.0 collective-permute-done.7.refs_10_.refs_3_.refs_5_
  19.3 2.0 %collective-permute-start.8 = (bf16[432,256]{1,0:T(8,128)(2,1)S(1)}, bf16[432,256]{1,0:T(8,128)(2,1)S(1)}, u32[]{:S(2)}, u32[]{:S(2)}) collective-permute-start(bf16[432,256]{1,0:T(8,128)(2,1)S(1)} %collective-permute-done.7.refs_10_.refs_3_.refs_5_), channel_id=1, source_target_pairs={{0,1},{1,0},{2,3},{3,2},{4,5},{5,4},{6,7},{7,6},{8,9},{9,8},{10,11... | collective-permute-start | bytes 663560 | tf_op jit(solution)/shard_map/ppermute | solution.py:303
  21.2 1.2 %collective-permute-start.5 = (bf16[32,2048]{1,0:T(8,128)(2,1)S(1)}, bf16[32,2048]{1,0:T(8,128)(2,1)S(1)}, u32[]{:S(2)}, u32[]{:S(2)}) collective-permute-start(bf16[32,2048]{1,0:T(8,128)(2,1)S(1)} %get-tuple-element.32.refs_1_.refs_0_), channel_id=1, source_target_pairs={{0,12},{4,8},{8,4},{12,0},{1,13},{5,9},{9,5},{13,1},{2,14},{6,10},... | collective-permute-start | bytes 393224 | tf_op jit(solution)/shard_map/ppermute | solution.py:303
  22.4 1.6 %collective-permute-start.2 = (bf16[32,2048]{1,0:T(8,128)(2,1)S(1)}, bf16[32,2048]{1,0:T(8,128)(2,1)S(1)}, u32[]{:S(2)}, u32[]{:S(2)}) collective-permute-start(bf16[32,2048]{1,0:T(8,128)(2,1)S(1)} %collective-permute-done.refs_2_.refs_1_), channel_id=1, source_target_pairs={{0,12},{4,8},{8,4},{12,0},{1,13},{5,9},{9,5},{13,1},{2,14},{6,10},... | collective-permute-start | bytes 393224 | tf_op jit(solution)/shard_map/ppermute | solution.py:303
  24.0 3.6 %collective-permute-done.5.refs_6_ = bf16[32,2048]{1,0:T(8,128)(2,1)S(1)} collective-permute-done((bf16[32,2048]{1,0:T(8,128)(2,1)S(1)}, bf16[32,2048]{1,0:T(8,128)(2,1)S(1)}, u32[]{:S(2)}, u32[]{:S(2)}) %collective-permute-start.5) | collective-permute-done | bytes 131104 | tf_op jit(solution)/shard_map/ppermute | solution.py:303
  27.6 2.8 %collective-permute-done.2.refs_4_ = bf16[32,2048]{1,0:T(8,128)(2,1)S(1)} collective-permute-done((bf16[32,2048]{1,0:T(8,128)(2,1)S(1)}, bf16[32,2048]{1,0:T(8,128)(2,1)S(1)}, u32[]{:S(2)}, u32[]{:S(2)}) %collective-permute-start.2) | collective-permute-done | bytes 131104 | tf_op jit(solution)/shard_map/ppermute | solution.py:303
  30.4 1.0 after.1
  34.0 6.4 %collective-permute-start.11 = (bf16[16,2048]{1,0:T(8,128)(2,1)S(1)}, bf16[16,2048]{1,0:T(8,128)(2,1)S(1)}, u32[]{:S(2)}, u32[]{:S(2)}) collective-permute-start(bf16[16,2048]{1,0:T(8,128)(2,1)S(1)} %get-tuple-element.37), channel_id=1, source_target_pairs={{0,1},{1,0},{2,3},{3,2},{4,5},{5,4},{6,7},{7,6},{8,9},{9,8},{10,11... | collective-permute-start | bytes 196616 | tf_op jit(solution)/shard_map/ppermute | solution.py:303
  40.4 1.7 %collective-permute-start.13 = (bf16[16,2048]{1,0:T(8,128)(2,1)S(1)}, bf16[16,2048]{1,0:T(8,128)(2,1)S(1)}, u32[]{:S(2)}, u32[]{:S(2)}) collective-permute-start(bf16[16,2048]{1,0:T(8,128)(2,1)S(1)} %get-tuple-element.39), channel_id=1, source_target_pairs={{0,3},{1,2},{2,1},{3,0},{4,7},{5,6},{6,5},{7,4},{8,11},{9,10},{10,... | collective-permute-start | bytes 196616 | tf_op jit(solution)/shard_map/ppermute | solution.py:303
  43.0 1.0 collective-permute-done.12.refs_5_
  44.0 1.6 %collective-permute-done.13.refs_6_ = bf16[16,2048]{1,0:T(8,128)(2,1)S(1)} collective-permute-done((bf16[16,2048]{1,0:T(8,128)(2,1)S(1)}, bf16[16,2048]{1,0:T(8,128)(2,1)S(1)}, u32[]{:S(2)}, u32[]{:S(2)}) %collective-permute-start.13) | collective-permute-done | bytes 65568 | tf_op jit(solution)/shard_map/ppermute | solution.py:303
  46.0 4.8 %collective-permute-start.15 = (bf16[64,2048]{1,0:T(8,128)(2,1)S(1)}, bf16[64,2048]{1,0:T(8,128)(2,1)S(1)}, u32[]{:S(2)}, u32[]{:S(2)}) collective-permute-start(bf16[64,2048]{1,0:T(8,128)(2,1)S(1)} %get-tuple-element.40.refs_1_.refs_0_), channel_id=1, source_target_pairs={{0,240},{1,0},{3,1},{2,3},{18,2},{19,18},{17,19},{16,17},{32,16},{... | collective-permute-start | bytes 786440 | tf_op jit(solution)/shard_map/ppermute | solution.py:299
  50.7 2.4 %collective-permute-done.15.refs_3_.refs_2_ = bf16[64,2048]{1,0:T(8,128)(2,1)S(1)} collective-permute-done((bf16[64,2048]{1,0:T(8,128)(2,1)S(1)}, bf16[64,2048]{1,0:T(8,128)(2,1)S(1)}, u32[]{:S(2)}, u32[]{:S(2)}) %collective-permute-start.15) | collective-permute-done | bytes 262176 | tf_op jit(solution)/shard_map/ppermute | solution.py:299
  54.1 3.0 %filter_sums.1 = (bf16[256,432]{1,0:T(8,128)(2,1)S(1)}, bf16[256,432]{1,0:T(8,128)(2,1)S(1)}, bf16[256,432]{1,0:T(8,128)(2,1)S(1)}, bf16[256,432]{1,0:T(8,128)(2,1)S(1)}) custom-call(s32[1]{0:T(128)} %bitcast.place_ref, bf16[256,2048]{1,0:T(8,128)(2,1)S(1)} %get-tuple-element.34.refs_0_, bf16[64,2048]{1,0:T(8,128)(2,1)S(1)} %get-tuple-element.40.refs_1_.refs_0_, ...), custom_call_target="tpu_custom_call" | custom-call | flops 1 | bytes 1 | tf_op jit(solution)/shard_map/filter_sums/pallas_call | solution.py:79
  57.0 8.1 %collective-permute-start.22 = (bf16[256,432]{1,0:T(8,128)(2,1)S(1)}, bf16[256,432]{1,0:T(8,128)(2,1)S(1)}, u32[]{:S(2)}, u32[]{:S(2)}) collective-permute-start(bf16[256,432]{1,0:T(8,128)(2,1)S(1)} %get-tuple-element.53), channel_id=1, source_target_pairs={{0,1},{1,0},{2,3},{3,2},{4,5},{5,4},{6,7},{7,6},{8,9},{9,8},{10,11... | collective-permute-start | bytes 663560 | tf_op jit(solution)/shard_map/ppermute | solution.py:303
  65.1 3.1 %input_sums.1 = (f32[64,2048]{1,0:T(8,128)S(1)}, bf16[32,2048]{1,0:T(8,128)(2,1)S(1)}, bf16[32,2048]{1,0:T(8,128)(2,1)S(1)}, bf16[32,2048]{1,0:T(8,128)(2,1)S(1)...) custom-call(s32[1]{0:T(128)} %bitcast.place_ref, ...), custom_call_target="tpu_custom_call" | custom-call | flops 1 | bytes 1 | tf_op jit(solution)/shard_map/input_sums/pallas_call | solution.py:79
  68.2 2.5 %collective-permute-start.17 = (bf16[32,2048]{1,0:T(8,128)(2,1)S(1)}, bf16[32,2048]{1,0:T(8,128)(2,1)S(1)}, u32[]{:S(2)}, u32[]{:S(2)}) collective-permute-start(bf16[32,2048]{1,0:T(8,128)(2,1)S(1)} %get-tuple-element.46), channel_id=1, source_target_pairs={{0,12},{4,8},{8,4},{12,0},{1,13},{5,9},{9,5},{13,1},{2,14},{6,10},... | collective-permute-start | bytes 393224 | tf_op jit(solution)/shard_map/ppermute | solution.py:303
  70.7 1.5 %collective-permute-start.16 = (bf16[32,2048]{1,0:T(8,128)(2,1)S(1)}, bf16[32,2048]{1,0:T(8,128)(2,1)S(1)}, u32[]{:S(2)}, u32[]{:S(2)}) collective-permute-start(bf16[32,2048]{1,0:T(8,128)(2,1)S(1)} %get-tuple-element.43), channel_id=1, source_target_pairs={{0,4},{4,0},{8,12},{12,8},{1,5},{5,1},{9,13},{13,9},{2,6},{6,2},{1... | collective-permute-start | bytes 393224 | tf_op jit(solution)/shard_map/ppermute | solution.py:303
  72.5 2.2 %collective-permute-done.17.refs_2_ = bf16[32,2048]{1,0:T(8,128)(2,1)S(1)} collective-permute-done((bf16[32,2048]{1,0:T(8,128)(2,1)S(1)}, bf16[32,2048]{1,0:T(8,128)(2,1)S(1)}, u32[]{:S(2)}, u32[]{:S(2)}) %collective-permute-start.17) | collective-permute-done | bytes 131104 | tf_op jit(solution)/shard_map/ppermute | solution.py:303
  75.9 1.3 %collective-permute-start.20 = (bf16[32,2048]{1,0:T(8,128)(2,1)S(1)}, bf16[32,2048]{1,0:T(8,128)(2,1)S(1)}, u32[]{:S(2)}, u32[]{:S(2)}) collective-permute-start(bf16[32,2048]{1,0:T(8,128)(2,1)S(1)} %get-tuple-element.49), channel_id=1, source_target_pairs={{0,12},{4,8},{8,4},{12,0},{1,13},{5,9},{9,5},{13,1},{2,14},{6,10},... | collective-permute-start | bytes 393224 | tf_op jit(solution)/shard_map/ppermute | solution.py:303
  77.3 1.5 %collective-permute-start.26 = (bf16[256,432]{1,0:T(8,128)(2,1)S(1)}, bf16[256,432]{1,0:T(8,128)(2,1)S(1)}, u32[]{:S(2)}, u32[]{:S(2)}) collective-permute-start(bf16[256,432]{1,0:T(8,128)(2,1)S(1)} %get-tuple-element.60), channel_id=1, source_target_pairs={{0,1},{1,0},{2,3},{3,2},{4,5},{5,4},{6,7},{7,6},{8,9},{9,8},{10,11... | collective-permute-start | bytes 663560 | tf_op jit(solution)/shard_map/ppermute | solution.py:303
  78.9 1.2 %collective-permute-done.19.refs_2_ = bf16[32,2048]{1,0:T(8,128)(2,1)S(1)} collective-permute-done((bf16[32,2048]{1,0:T(8,128)(2,1)S(1)}, bf16[32,2048]{1,0:T(8,128)(2,1)S(1)}, u32[]{:S(2)}, u32[]{:S(2)}) %collective-permute-start.19) | collective-permute-done | bytes 131104 | tf_op jit(solution)/shard_map/ppermute | solution.py:303
  81.1 2.9 %collective-permute-start.23 = (bf16[2,16,2048]{2,1,0:T(8,128)(2,1)S(1)}, bf16[2,16,2048]{2,1,0:T(8,128)(2,1)S(1)}, u32[]{:S(2)}, u32[]{:S(2)}) collective-permute-start(bf16[2,16,2048]{2,1,0:T(8,128)(2,1)S(1)} %get-tuple-element.55), channel_id=1, source_target_pairs={{0,1},{1,0},{2,3},{3,2},{4,5},{5,4},{6,7},{7,6},{8,9},{9,8},{10,11... | collective-permute-start | bytes 393224 | tf_op jit(solution)/shard_map/ppermute | solution.py:303
  84.0 1.0 collective-permute-done.23.refs_1_.refs_3_
  86.4 3.5 %all-to-all-start.1 = ((bf16[16,16,432]{2,1,0:T(8,128)(2,1)}), bf16[16,16,432]{2,1,0:T(8,128)(2,1)S(1)}, u32[]{:S(2)}, u32[]{:S(2)}) async-start(bf16[16,16,432]{2,1,0:T(8,128)(2,1)} %bitcast.7), calls=%async_computation.1 | async-start | bytes 524288 | tf_op jit(solution)/shard_map/all_to_all | solution.py:443
  90.3 3.4 %collective-permute-start.25 = (bf16[2,16,2048]{2,1,0:T(8,128)(2,1)S(1)}, bf16[2,16,2048]{2,1,0:T(8,128)(2,1)S(1)}, u32[]{:S(2)}, u32[]{:S(2)}) collective-permute-start(bf16[2,16,2048]{2,1,0:T(8,128)(2,1)S(1)} %get-tuple-element.57), channel_id=1, source_target_pairs={{0,3},{1,2},{2,1},{3,0},{4,7},{5,6},{6,5},{7,4},{8,11},{9,10},{10,... | collective-permute-start | bytes 393224 | tf_op jit(solution)/shard_map/ppermute | solution.py:303
  94.5 6.6 %collective-permute-done.25.refs_3_ = bf16[2,16,2048]{2,1,0:T(8,128)(2,1)S(1)} collective-permute-done((bf16[2,16,2048]{2,1,0:T(8,128)(2,1)S(1)}, bf16[2,16,2048]{2,1,0:T(8,128)(2,1)S(1)}, u32[]{:S(2)}, u32[]{:S(2)}) %collective-permute-start.25) | collective-permute-done | bytes 131104 | tf_op jit(solution)/shard_map/ppermute | solution.py:303
  101.1 1.0 close.1
  (49 shorter events, 13.7 us)
Async XLA Ops:
  0.6 1.0 copy-start
  12.3 0.9 copy-start.2
  13.3 6.0 %collective-permute-start.7 = (bf16[432,256]{1,0:T(8,128)(2,1)S(1)}, bf16[432,256]{1,0:T(8,128)(2,1)S(1)}, u32[]{:S(2)}, u32[]{:S(2)}) collective-permute-start(bf16[432,256]{1,0:T(8,128)(2,1)S(1)} %filters.1.refs_8_.refs_1_.refs_3_), channel_id=1, source_target_pairs={{0,2},{1,3},{2,0},{3,1},{4,6},{5,7},{6,4},{7,5},{8,10},{9,11},{10,... | collective-permute-start | bytes 663560 | tf_op jit(solution)/shard_map/ppermute | solution.py:303
  13.9 7.3 %collective-permute-start.3 = (bf16[32,2048]{1,0:T(8,128)(2,1)S(1)}, bf16[32,2048]{1,0:T(8,128)(2,1)S(1)}, u32[]{:S(2)}, u32[]{:S(2)}) collective-permute-start(bf16[32,2048]{1,0:T(8,128)(2,1)S(1)} %get-tuple-element.33.refs_1_), channel_id=1, source_target_pairs={{0,12},{4,8},{8,4},{12,0},{1,13},{5,9},{9,5},{13,1},{2,14},{6,10},... | collective-permute-start | bytes 393224 | tf_op jit(solution)/shard_map/ppermute | solution.py:303
  15.1 7.3 %collective-permute-start.1 = (bf16[32,2048]{1,0:T(8,128)(2,1)S(1)}, bf16[32,2048]{1,0:T(8,128)(2,1)S(1)}, u32[]{:S(2)}, u32[]{:S(2)}) collective-permute-start(bf16[32,2048]{1,0:T(8,128)(2,1)S(1)} %get-tuple-element.33.refs_1_), channel_id=1, source_target_pairs={{0,4},{4,0},{8,12},{12,8},{1,5},{5,1},{9,13},{13,9},{2,6},{6,2},{1... | collective-permute-start | bytes 393224 | tf_op jit(solution)/shard_map/ppermute | solution.py:303
  15.1 7.3 %collective-permute-start = (bf16[32,2048]{1,0:T(8,128)(2,1)S(1)}, bf16[32,2048]{1,0:T(8,128)(2,1)S(1)}, u32[]{:S(2)}, u32[]{:S(2)}) collective-permute-start(bf16[32,2048]{1,0:T(8,128)(2,1)S(1)} %get-tuple-element.32.refs_1_.refs_0_), channel_id=1, source_target_pairs={{0,4},{4,0},{8,12},{12,8},{1,5},{5,1},{9,13},{13,9},{2,6},{6,2},{1... | collective-permute-start | bytes 393224 | tf_op jit(solution)/shard_map/ppermute | solution.py:303
  16.6 11.0 %collective-permute-start.6 = (bf16[432,256]{1,0:T(8,128)(2,1)S(1)}, bf16[432,256]{1,0:T(8,128)(2,1)S(1)}, u32[]{:S(2)}, u32[]{:S(2)}) collective-permute-start(bf16[432,256]{1,0:T(8,128)(2,1)S(1)} %filters.1.refs_8_.refs_1_.refs_3_), channel_id=1, source_target_pairs={{0,1},{1,0},{2,3},{3,2},{4,5},{5,4},{6,7},{7,6},{8,9},{9,8},{10,11... | collective-permute-start | bytes 663560 | tf_op jit(solution)/shard_map/ppermute | solution.py:303
  19.3 11.1 %collective-permute-start.8 = (bf16[432,256]{1,0:T(8,128)(2,1)S(1)}, bf16[432,256]{1,0:T(8,128)(2,1)S(1)}, u32[]{:S(2)}, u32[]{:S(2)}) collective-permute-start(bf16[432,256]{1,0:T(8,128)(2,1)S(1)} %collective-permute-done.7.refs_10_.refs_3_.refs_5_), channel_id=1, source_target_pairs={{0,1},{1,0},{2,3},{3,2},{4,5},{5,4},{6,7},{7,6},{8,9},{9,8},{10,11... | collective-permute-start | bytes 663560 | tf_op jit(solution)/shard_map/ppermute | solution.py:303
  21.2 6.3 %collective-permute-start.5 = (bf16[32,2048]{1,0:T(8,128)(2,1)S(1)}, bf16[32,2048]{1,0:T(8,128)(2,1)S(1)}, u32[]{:S(2)}, u32[]{:S(2)}) collective-permute-start(bf16[32,2048]{1,0:T(8,128)(2,1)S(1)} %get-tuple-element.32.refs_1_.refs_0_), channel_id=1, source_target_pairs={{0,12},{4,8},{8,4},{12,0},{1,13},{5,9},{9,5},{13,1},{2,14},{6,10},... | collective-permute-start | bytes 393224 | tf_op jit(solution)/shard_map/ppermute | solution.py:303
  22.4 5.2 %collective-permute-start.4 = (bf16[32,2048]{1,0:T(8,128)(2,1)S(1)}, bf16[32,2048]{1,0:T(8,128)(2,1)S(1)}, u32[]{:S(2)}, u32[]{:S(2)}) collective-permute-start(bf16[32,2048]{1,0:T(8,128)(2,1)S(1)} %collective-permute-done.3.refs_7_.refs_2_), channel_id=1, source_target_pairs={{0,4},{4,0},{8,12},{12,8},{1,5},{5,1},{9,13},{13,9},{2,6},{6,2},{1... | collective-permute-start | bytes 393224 | tf_op jit(solution)/shard_map/ppermute | solution.py:303
  22.4 8.0 %collective-permute-start.2 = (bf16[32,2048]{1,0:T(8,128)(2,1)S(1)}, bf16[32,2048]{1,0:T(8,128)(2,1)S(1)}, u32[]{:S(2)}, u32[]{:S(2)}) collective-permute-start(bf16[32,2048]{1,0:T(8,128)(2,1)S(1)} %collective-permute-done.refs_2_.refs_1_), channel_id=1, source_target_pairs={{0,12},{4,8},{8,4},{12,0},{1,13},{5,9},{9,5},{13,1},{2,14},{6,10},... | collective-permute-start | bytes 393224 | tf_op jit(solution)/shard_map/ppermute | solution.py:303
  31.4 2.5 %copy-start.1 = (bf16[1,16,4,16,128]{4,3,2,1,0:T(8,128)(2,1)S(1)}, bf16[1,16,4,16,128]{4,3,2,1,0:T(8,128)(2,1)}, u32[]{:S(2)}) copy-start(bf16[1,16,4,16,128]{4,3,2,1,0:T(8,128)(2,1)} %param.5) | copy-start | bytes 786436
  32.3 13.3 %collective-permute-start.9 = (bf16[64,2048]{1,0:T(8,128)(2,1)S(1)}, bf16[64,2048]{1,0:T(8,128)(2,1)S(1)}, u32[]{:S(2)}, u32[]{:S(2)}) collective-permute-start(bf16[64,2048]{1,0:T(8,128)(2,1)S(1)} %before.1.refs_5_), channel_id=1, source_target_pairs={{0,240},{1,0},{3,1},{2,3},{18,2},{19,18},{17,19},{16,17},{32,16},{... | collective-permute-start | bytes 786440 | tf_op jit(solution)/shard_map/ppermute | solution.py:299
  33.2 12.4 %collective-permute-start.10 = (bf16[64,2048]{1,0:T(8,128)(2,1)S(1)}, bf16[64,2048]{1,0:T(8,128)(2,1)S(1)}, u32[]{:S(2)}, u32[]{:S(2)}) collective-permute-start(bf16[64,2048]{1,0:T(8,128)(2,1)S(1)} %get-tuple-element.35), channel_id=1, source_target_pairs={{0,1},{1,3},{3,2},{2,18},{18,19},{19,17},{17,16},{16,32},{32,33},{... | collective-permute-start | bytes 786440 | tf_op jit(solution)/shard_map/ppermute | solution.py:299
  34.0 9.0 %collective-permute-start.11 = (bf16[16,2048]{1,0:T(8,128)(2,1)S(1)}, bf16[16,2048]{1,0:T(8,128)(2,1)S(1)}, u32[]{:S(2)}, u32[]{:S(2)}) collective-permute-start(bf16[16,2048]{1,0:T(8,128)(2,1)S(1)} %get-tuple-element.37), channel_id=1, source_target_pairs={{0,1},{1,0},{2,3},{3,2},{4,5},{5,4},{6,7},{7,6},{8,9},{9,8},{10,11... | collective-permute-start | bytes 196616 | tf_op jit(solution)/shard_map/ppermute | solution.py:303
  40.4 3.7 %collective-permute-start.12 = (bf16[16,2048]{1,0:T(8,128)(2,1)S(1)}, bf16[16,2048]{1,0:T(8,128)(2,1)S(1)}, u32[]{:S(2)}, u32[]{:S(2)}) collective-permute-start(bf16[16,2048]{1,0:T(8,128)(2,1)S(1)} %get-tuple-element.38), channel_id=1, source_target_pairs={{0,2},{1,3},{2,0},{3,1},{4,6},{5,7},{6,4},{7,5},{8,10},{9,11},{10,... | collective-permute-start | bytes 196616 | tf_op jit(solution)/shard_map/ppermute | solution.py:303
  40.4 5.2 %collective-permute-start.13 = (bf16[16,2048]{1,0:T(8,128)(2,1)S(1)}, bf16[16,2048]{1,0:T(8,128)(2,1)S(1)}, u32[]{:S(2)}, u32[]{:S(2)}) collective-permute-start(bf16[16,2048]{1,0:T(8,128)(2,1)S(1)} %get-tuple-element.39), channel_id=1, source_target_pairs={{0,3},{1,2},{2,1},{3,0},{4,7},{5,6},{6,5},{7,4},{8,11},{9,10},{10,... | collective-permute-start | bytes 196616 | tf_op jit(solution)/shard_map/ppermute | solution.py:303
  46.0 7.1 %collective-permute-start.15 = (bf16[64,2048]{1,0:T(8,128)(2,1)S(1)}, bf16[64,2048]{1,0:T(8,128)(2,1)S(1)}, u32[]{:S(2)}, u32[]{:S(2)}) collective-permute-start(bf16[64,2048]{1,0:T(8,128)(2,1)S(1)} %get-tuple-element.40.refs_1_.refs_0_), channel_id=1, source_target_pairs={{0,240},{1,0},{3,1},{2,3},{18,2},{19,18},{17,19},{16,17},{32,16},{... | collective-permute-start | bytes 786440 | tf_op jit(solution)/shard_map/ppermute | solution.py:299
  50.7 3.3 %collective-permute-start.14 = (bf16[64,2048]{1,0:T(8,128)(2,1)S(1)}, bf16[64,2048]{1,0:T(8,128)(2,1)S(1)}, u32[]{:S(2)}, u32[]{:S(2)}) collective-permute-start(bf16[64,2048]{1,0:T(8,128)(2,1)S(1)} %get-tuple-element.40.refs_1_.refs_0_), channel_id=1, source_target_pairs={{0,1},{1,3},{3,2},{2,18},{18,19},{19,17},{17,16},{16,32},{32,33},{... | collective-permute-start | bytes 786440 | tf_op jit(solution)/shard_map/ppermute | solution.py:299
  57.0 20.2 %collective-permute-start.22 = (bf16[256,432]{1,0:T(8,128)(2,1)S(1)}, bf16[256,432]{1,0:T(8,128)(2,1)S(1)}, u32[]{:S(2)}, u32[]{:S(2)}) collective-permute-start(bf16[256,432]{1,0:T(8,128)(2,1)S(1)} %get-tuple-element.53), channel_id=1, source_target_pairs={{0,1},{1,0},{2,3},{3,2},{4,5},{5,4},{6,7},{7,6},{8,9},{9,8},{10,11... | collective-permute-start | bytes 663560 | tf_op jit(solution)/shard_map/ppermute | solution.py:303
  68.2 6.4 %collective-permute-start.17 = (bf16[32,2048]{1,0:T(8,128)(2,1)S(1)}, bf16[32,2048]{1,0:T(8,128)(2,1)S(1)}, u32[]{:S(2)}, u32[]{:S(2)}) collective-permute-start(bf16[32,2048]{1,0:T(8,128)(2,1)S(1)} %get-tuple-element.46), channel_id=1, source_target_pairs={{0,12},{4,8},{8,4},{12,0},{1,13},{5,9},{9,5},{13,1},{2,14},{6,10},... | collective-permute-start | bytes 393224 | tf_op jit(solution)/shard_map/ppermute | solution.py:303
  70.7 4.8 %collective-permute-start.18 = (bf16[32,2048]{1,0:T(8,128)(2,1)S(1)}, bf16[32,2048]{1,0:T(8,128)(2,1)S(1)}, u32[]{:S(2)}, u32[]{:S(2)}) collective-permute-start(bf16[32,2048]{1,0:T(8,128)(2,1)S(1)} %get-tuple-element.47), channel_id=1, source_target_pairs={{0,4},{4,0},{8,12},{12,8},{1,5},{5,1},{9,13},{13,9},{2,6},{6,2},{1... | collective-permute-start | bytes 393224 | tf_op jit(solution)/shard_map/ppermute | solution.py:303
  70.7 8.1 %collective-permute-start.16 = (bf16[32,2048]{1,0:T(8,128)(2,1)S(1)}, bf16[32,2048]{1,0:T(8,128)(2,1)S(1)}, u32[]{:S(2)}, u32[]{:S(2)}) collective-permute-start(bf16[32,2048]{1,0:T(8,128)(2,1)S(1)} %get-tuple-element.43), channel_id=1, source_target_pairs={{0,4},{4,0},{8,12},{12,8},{1,5},{5,1},{9,13},{13,9},{2,6},{6,2},{1... | collective-permute-start | bytes 393224 | tf_op jit(solution)/shard_map/ppermute | solution.py:303
  72.2 6.8 %collective-permute-start.21 = (bf16[32,2048]{1,0:T(8,128)(2,1)S(1)}, bf16[32,2048]{1,0:T(8,128)(2,1)S(1)}, u32[]{:S(2)}, u32[]{:S(2)}) collective-permute-start(bf16[32,2048]{1,0:T(8,128)(2,1)S(1)} %get-tuple-element.50), channel_id=1, source_target_pairs={{0,12},{4,8},{8,4},{12,0},{1,13},{5,9},{9,5},{13,1},{2,14},{6,10},... | collective-permute-start | bytes 393224 | tf_op jit(solution)/shard_map/ppermute | solution.py:303
  75.5 4.6 %collective-permute-start.19 = (bf16[32,2048]{1,0:T(8,128)(2,1)S(1)}, bf16[32,2048]{1,0:T(8,128)(2,1)S(1)}, u32[]{:S(2)}, u32[]{:S(2)}) collective-permute-start(bf16[32,2048]{1,0:T(8,128)(2,1)S(1)} %get-tuple-element.48), channel_id=1, source_target_pairs={{0,4},{4,0},{8,12},{12,8},{1,5},{5,1},{9,13},{13,9},{2,6},{6,2},{1... | collective-permute-start | bytes 393224 | tf_op jit(solution)/shard_map/ppermute | solution.py:303
  75.9 5.0 %collective-permute-start.20 = (bf16[32,2048]{1,0:T(8,128)(2,1)S(1)}, bf16[32,2048]{1,0:T(8,128)(2,1)S(1)}, u32[]{:S(2)}, u32[]{:S(2)}) collective-permute-start(bf16[32,2048]{1,0:T(8,128)(2,1)S(1)} %get-tuple-element.49), channel_id=1, source_target_pairs={{0,12},{4,8},{8,4},{12,0},{1,13},{5,9},{9,5},{13,1},{2,14},{6,10},... | collective-permute-start | bytes 393224 | tf_op jit(solution)/shard_map/ppermute | solution.py:303
  77.3 6.7 %collective-permute-start.26 = (bf16[256,432]{1,0:T(8,128)(2,1)S(1)}, bf16[256,432]{1,0:T(8,128)(2,1)S(1)}, u32[]{:S(2)}, u32[]{:S(2)}) collective-permute-start(bf16[256,432]{1,0:T(8,128)(2,1)S(1)} %get-tuple-element.60), channel_id=1, source_target_pairs={{0,1},{1,0},{2,3},{3,2},{4,5},{5,4},{6,7},{7,6},{8,9},{9,8},{10,11... | collective-permute-start | bytes 663560 | tf_op jit(solution)/shard_map/ppermute | solution.py:303
  78.8 6.7 %collective-permute-start.27 = (bf16[256,432]{1,0:T(8,128)(2,1)S(1)}, bf16[256,432]{1,0:T(8,128)(2,1)S(1)}, u32[]{:S(2)}, u32[]{:S(2)}) collective-permute-start(bf16[256,432]{1,0:T(8,128)(2,1)S(1)} %lift.1.refs_6_), channel_id=1, source_target_pairs={{0,2},{1,3},{2,0},{3,1},{4,6},{5,7},{6,4},{7,5},{8,10},{9,11},{10,... | collective-permute-start | bytes 663560 | tf_op jit(solution)/shard_map/ppermute | solution.py:303
  81.1 3.9 %collective-permute-start.23 = (bf16[2,16,2048]{2,1,0:T(8,128)(2,1)S(1)}, bf16[2,16,2048]{2,1,0:T(8,128)(2,1)S(1)}, u32[]{:S(2)}, u32[]{:S(2)}) collective-permute-start(bf16[2,16,2048]{2,1,0:T(8,128)(2,1)S(1)} %get-tuple-element.55), channel_id=1, source_target_pairs={{0,1},{1,0},{2,3},{3,2},{4,5},{5,4},{6,7},{7,6},{8,9},{9,8},{10,11... | collective-permute-start | bytes 393224 | tf_op jit(solution)/shard_map/ppermute | solution.py:303
  86.4 15.7 %all-to-all-start.1 = ((bf16[16,16,432]{2,1,0:T(8,128)(2,1)}), bf16[16,16,432]{2,1,0:T(8,128)(2,1)S(1)}, u32[]{:S(2)}, u32[]{:S(2)}) async-start(bf16[16,16,432]{2,1,0:T(8,128)(2,1)} %bitcast.7), calls=%async_computation.1 | async-start | bytes 524288 | tf_op jit(solution)/shard_map/all_to_all | solution.py:443
  89.9 4.6 %collective-permute-start.24 = (bf16[2,16,2048]{2,1,0:T(8,128)(2,1)S(1)}, bf16[2,16,2048]{2,1,0:T(8,128)(2,1)S(1)}, u32[]{:S(2)}, u32[]{:S(2)}) collective-permute-start(bf16[2,16,2048]{2,1,0:T(8,128)(2,1)S(1)} %get-tuple-element.56), channel_id=1, source_target_pairs={{0,2},{1,3},{2,0},{3,1},{4,6},{5,7},{6,4},{7,5},{8,10},{9,11},{10,... | collective-permute-start | bytes 393224 | tf_op jit(solution)/shard_map/ppermute | solution.py:303
  90.3 10.8 %collective-permute-start.25 = (bf16[2,16,2048]{2,1,0:T(8,128)(2,1)S(1)}, bf16[2,16,2048]{2,1,0:T(8,128)(2,1)S(1)}, u32[]{:S(2)}, u32[]{:S(2)}) collective-permute-start(bf16[2,16,2048]{2,1,0:T(8,128)(2,1)S(1)} %get-tuple-element.57), channel_id=1, source_target_pairs={{0,3},{1,2},{2,1},{3,0},{4,7},{5,6},{6,5},{7,4},{8,11},{9,10},{10,... | collective-permute-start | bytes 393224 | tf_op jit(solution)/shard_map/ppermute | solution.py:303

commit v2 on v1

--- a/solution.py
+++ b/solution.py
@@ -10,6 +10,7 @@
 
 BREADTH = 128
 GROUP = 4
+LAYERS = 8
 VMEM_LIMIT = 40 * 1024 * 1024
 
 
@@ -50,7 +51,8 @@
 
 
 def plane_of(space, part):
-    return part ^ (part // 2) ^ ((space % 2) * (GROUP - 1))
+    backwards = (1 + space + space // LAYERS) % 2
+    return part ^ (part // 2) ^ (backwards * (GROUP - 1))
 
 
 def partner_plane(place_ref, j):
@@ -90,30 +92,25 @@
     )(place, *operands, *unread)
 
 
-def planes_kernel(place_ref, value_ref, out_ref):
-    channels, planes, height, breadth = value_ref.shape
-    for p in range(planes):
-        value = value_ref[:, plane_of(place_ref[0] // GROUP**2, p)].astype(jnp.float32)
-        out_ref[p] = value.reshape(channels, height * breadth).astype(out_ref.dtype)
-
-
-def partner_planes_kernel(place_ref, value_ref, *outs):
+def planes_kernel(place_ref, value_ref, *outs):
     channels, _, height, breadth = value_ref.shape
     for j, out_ref in enumerate(outs):
         value = value_ref[:, partner_plane(place_ref, j)].astype(jnp.float32)
         out_ref[...] = value.reshape(channels, height * breadth).astype(out_ref.dtype)
 
 
-def same_kernel(place_ref, value_ref, out_ref):
-    del place_ref
-    out_ref[...] = value_ref[...]
-
-
-def halves_kernel(place_ref, value_ref, low_ref, high_ref):
-    del place_ref
+def rest_kernel(place_ref, cotangent_ref, filters_ref, matrix_ref, *outs):
+    planes_kernel(place_ref, cotangent_ref, *outs)
+    matrix_ref[...] = filters_ref[...]
+
+
+def halves_kernel(place_ref, *refs):
+    pieces, (low_ref, high_ref, order_ref) = refs[:GROUP], refs[GROUP:]
     half = low_ref.shape[0]
-    low_ref[...] = value_ref[:half]
-    high_ref[...] = value_ref[half:]
+    for j, piece_ref in enumerate(pieces):
+        order_ref[block_rows(place_ref, "part", j, half // 2), :] = piece_ref[...]
+    low_ref[...] = order_ref[:half]
+    high_ref[...] = order_ref[half:]
 
 
 def edge_sums(place_ref, field_ref, matrices, out_ref, a):
@@ -319,35 +316,32 @@
     place = lax.axis_index(("space", "run", "part")).reshape(1)
     ends = {"last": spaces - 1}
 
-    (field,) = call(
-        planes_kernel, [((planes, in_local, plane), bf16)], "volume_planes", place, volume[0]
-    )
-    field = lax.all_to_all(field, "part", split_axis=0, concat_axis=0, tiled=True)
+    volumes = call(
+        planes_kernel, [((in_local, plane), bf16)] * GROUP, "volume_planes", place, volume[0]
+    )
+    matrix, *cotangents = call(
+        rest_kernel,
+        [((taps, in_total), bf16)] + [((out_local, plane), bf16)] * GROUP,
+        "rest",
+        place,
+        cotangent[0],
+        weight.reshape(taps, in_total),
+        unread=[volumes[0]],
+    )
+    volumes, cotangents = swapped(volumes, "part"), swapped(cotangents, "part")
     low, high = call(
-        halves_kernel, [((half, plane), bf16)] * 2, "halves", place, field.reshape(depth, plane)
+        halves_kernel,
+        [((half, plane), bf16)] * 2,
+        "halves",
+        place,
+        *volumes,
+        unread=[matrix],
+        scratch=[pltpu.VMEM((depth, plane), bf16)],
     )
     low_1, high_3 = swap(low, "run", 1), swap(high, "run", 3)
     high_1, low_3 = swap(high, "run", 1), swap(low, "run", 3)
-    (matrix,) = call(
-        same_kernel,
-        [((taps, in_total), bf16)],
-        "filters",
-        place,
-        weight.reshape(taps, in_total),
-        unread=[low],
-    )
-    matrix_1, matrix_2 = swap(matrix, "part", 1), swap(matrix, "part", 2)
     low_2, high_2 = swap(low_1, "run", 3), swap(high_3, "run", 1)
-    matrices = [matrix, matrix_1, matrix_2, swap(matrix_2, "part", 1)]
-    cotangents = call(
-        partner_planes_kernel,
-        [((out_local, plane), bf16)] * GROUP,
-        "cotangent_planes",
-        place,
-        cotangent[0],
-        unread=[low_1, high_3],
-    )
-    cotangents = swapped(cotangents, "part")
+    matrices = swapped([matrix] * GROUP, "part")
 
     field, after = call(
         after_kernel,
@@ -359,7 +353,13 @@
     )
     after = shifted(after, 1)
     (before,) = call(
-        before_kernel, [((rows, plane), bf16)], "before", place, field, *matrices
+        before_kernel,
+        [((rows, plane), bf16)],
+        "before",
+        place,
+        field,
+        *matrices,
+        unread=cotangents[1:],
     )
     (same,) = call(
         centre_kernel,
@@ -406,6 +406,9 @@
     )
     far_low, far_high = swap(far_low, "run", 1), swap(far_high, "run", 3)
     low_1, high_3 = swap(low_1, "run", 1), swap(high_3, "run", 3)
+    (sums_2,) = call(
+        lift_kernel, [((in_total, taps), bf16)], "lift", place, sums_2, sums_3, unread=[own, sums_1]
+    )
     high_1, low_3 = call(
         join_kernel,
         [((half, plane), bf16)] * 2,
@@ -415,30 +418,17 @@
         low_3,
         far_high,
         far_low,
+        unread=[sums_2],
     )
     high_1, low_3 = swap(high_1, "run", 1), swap(low_3, "run", 3)
-    (sums_2,) = call(
-        lift_kernel, [((in_total, taps), bf16)], "lift", place, sums_2, sums_3, unread=[far_low]
-    )
-    pairs = call(
-        pair_kernel,
-        [((2, in_local, plane), bf16)] * GROUP,
-        "pairs",
-        place,
-        *(own, low_1, high_1, low_3, high_3),
-        active,
-        unread=[sums_2],
-        scratch=[pltpu.VMEM((depth, plane), f32)],
-    )
     sums_2 = swap(sums_2, "part", 2)
-    pairs = swapped(pairs, "part")
     (sums,) = call(
         merge_kernel,
         [((in_total, taps), bf16)],
         "merge",
         place,
         *(sums, sums_1, sums_2),
-        unread=[pairs[1]],
+        unread=[low_1, high_1, low_3, high_3],
     )
     sums = lax.all_to_all(
         sums.reshape(spaces, in_total // spaces, taps),
@@ -447,6 +437,16 @@
         concat_axis=0,
         tiled=True,
     )
+    pairs = call(
+        pair_kernel,
+        [((2, in_local, plane), bf16)] * GROUP,
+        "pairs",
+        place,
+        *(own, low_1, high_1, low_3, high_3),
+        active,
+        scratch=[pltpu.VMEM((depth, plane), f32)],
+    )
+    pairs = swapped(pairs, "part")
     (total,) = call(
         functools.partial(total_kernel, scale=grad_scale),
         [((taps, in_total // spaces), f32)],

time: 103 us -> 94.3 us (0.916)
  waiting for transfers between devices: 27.3 us -> 42 us
  starting transfers between devices: 49.9 us -> 36.9 us
  blocking collectives: 10.6 us -> 0 us
    ppermute x4, waiting for transfers between devices: 3.32 us -> 15.8 us  [shifted(): lax.ppermute(value, DEPTH, [(at[i], at[(i + by) % count]) for i in range(...]
    ppermute x24 -> x27, starting transfers between devices: 40 us -> 29 us  [swap(): lax.ppermute(value, axis, [(i, i ^ j) for i in range(lax.axis_size(axis))])]
    all_to_all x1 -> x0, blocking collectives: 10.6 us -> none  [body(): lax.all_to_all(field, 'part', split_axis=0, concat_axis=0, tiled=True)]
    ppermute x24 -> x27, waiting for transfers between devices: 24 us -> 26.2 us  [swap(): lax.ppermute(value, axis, [(i, i ^ j) for i in range(lax.axis_size(axis))])]
    ppermute x4, starting transfers between devices: 6.33 us -> 4.32 us  [shifted(): lax.ppermute(value, DEPTH, [(at[i], at[(i + by) % count]) for i in range(...]
    pallas_call x16 -> x15, Pallas kernels: 12.4 us -> 12.4 us  [call(): pl.pallas_call(run, in_specs=[pl.BlockSpec(memory_space=pltpu.SMEM)] + [p...]
  transfers between devices with their start and end apart: 29 -> 32, of which waited for: 15 -> 16; matrix products, arithmetic and copies ran while one was open for 0% -> 0% of each run, Pallas kernels for 5% -> 7%
where the time goes in v2:
time: 94.3 us; the launch traced here: 93.9 us
  waiting for transfers between devices  42 us (45%)
  starting transfers between devices  36.9 us (39%)
  Pallas kernels  12.4 us (13%)
  local copies, waits for them, and re-layouts  1.92 us (2%)
    ppermute x27, starting transfers between devices, swap(): lax.ppermute(value, axis, [(i, i ^ j) for i in range(lax.axis_size(axis))])  29 us
    ppermute x27, waiting for transfers between devices, swap(): lax.ppermute(value, axis, [(i, i ^ j) for i in range(lax.axis_size(axis))])  26.2 us
    ppermute x4, waiting for transfers between devices, shifted(): lax.ppermute(value, DEPTH, [(at[i], at[(i + by) % count]) for i in range(...  15.8 us
    pallas_call x15, Pallas kernels, call(): pl.pallas_call(run, in_specs=[pl.BlockSpec(memory_space=pltpu.SMEM)] + [p...  12.4 us
    ppermute x4, starting transfers between devices, shifted(): lax.ppermute(value, DEPTH, [(at[i], at[(i + by) % count]) for i in range(...  4.32 us
    all_to_all x1, starting transfers between devices, body(): lax.all_to_all(sums.reshape(spaces, in_total // spaces, taps), 'space', s...  3.53 us
    unnamed x6, local copies, waits for them, and re-layouts  1.92 us
  transfers between devices with their start and end apart: 32, of which 16 were waited for; matrix products, arithmetic and copies ran while one was open for 0% of the time, Pallas kernels for 7%

profile of v2, /device:TPU:1, one launch (start us, length us, event | category | flops | bytes accessed | tf_op | source)
XLA Modules:
  0.0 93.9 jit_solution(12171113014061109275)
XLA Ops:
  1.8 3.3 %collective-permute-start = (bf16[16,2048]{1,0:T(8,128)(2,1)S(1)}, bf16[16,2048]{1,0:T(8,128)(2,1)S(1)}, u32[]{:S(2)}, u32[]{:S(2)}) collective-permute-start(bf16[16,2048]{1,0:T(8,128)(2,1)S(1)} %get-tuple-element.38), channel_id=1, source_target_pairs={{0,1},{1,0},{2,3},{3,2},{4,5},{5,4},{6,7},{7,6},{8,9},{9,8},{10,11... | collective-permute-start | bytes 196616 | tf_op jit(solution)/shard_map/ppermute | solution.py:300
  5.1 1.7 %collective-permute-start.2 = (bf16[16,2048]{1,0:T(8,128)(2,1)S(1)}, bf16[16,2048]{1,0:T(8,128)(2,1)S(1)}, u32[]{:S(2)}, u32[]{:S(2)}) collective-permute-start(bf16[16,2048]{1,0:T(8,128)(2,1)S(1)} %get-tuple-element.40), channel_id=1, source_target_pairs={{0,3},{1,2},{2,1},{3,0},{4,7},{5,6},{6,5},{7,4},{8,11},{9,10},{10,... | collective-permute-start | bytes 196616 | tf_op jit(solution)/shard_map/ppermute | solution.py:300
  8.7 1.6 %collective-permute-done.2.refs_3_ = bf16[16,2048]{1,0:T(8,128)(2,1)S(1)} collective-permute-done((bf16[16,2048]{1,0:T(8,128)(2,1)S(1)}, bf16[16,2048]{1,0:T(8,128)(2,1)S(1)}, u32[]{:S(2)}, u32[]{:S(2)}) %collective-permute-start.2) | collective-permute-done | bytes 65568 | tf_op jit(solution)/shard_map/ppermute | solution.py:300
  10.4 1.1 %collective-permute-start.8 = (bf16[32,2048]{1,0:T(8,128)(2,1)S(1)}, bf16[32,2048]{1,0:T(8,128)(2,1)S(1)}, u32[]{:S(2)}, u32[]{:S(2)}) collective-permute-start(bf16[32,2048]{1,0:T(8,128)(2,1)S(1)} %get-tuple-element.42.refs_0_), channel_id=1, source_target_pairs={{0,12},{4,8},{8,4},{12,0},{1,13},{5,9},{9,5},{13,1},{2,14},{6,10},... | collective-permute-start | bytes 393224 | tf_op jit(solution)/shard_map/ppermute | solution.py:300
  11.5 1.7 %collective-permute-start.11 = (bf16[432,256]{1,0:T(8,128)(2,1)S(1)}, bf16[432,256]{1,0:T(8,128)(2,1)S(1)}, u32[]{:S(2)}, u32[]{:S(2)}) collective-permute-start(bf16[432,256]{1,0:T(8,128)(2,1)S(1)} %get-tuple-element.41.refs_4_.refs_8_.refs_1_.refs_3_), channel_id=1, source_target_pairs={{0,3},{1,2},{2,1},{3,0},{4,7},{5,6},{6,5},{7,4},{8,11},{9,10},{10,... | collective-permute-start | bytes 663560 | tf_op jit(solution)/shard_map/ppermute | solution.py:300
  13.7 2.9 %collective-permute-done.8.refs_6_ = bf16[32,2048]{1,0:T(8,128)(2,1)S(1)} collective-permute-done((bf16[32,2048]{1,0:T(8,128)(2,1)S(1)}, bf16[32,2048]{1,0:T(8,128)(2,1)S(1)}, u32[]{:S(2)}, u32[]{:S(2)}) %collective-permute-start.8) | collective-permute-done | bytes 131104 | tf_op jit(solution)/shard_map/ppermute | solution.py:300
  17.5 4.1 %collective-permute-done.6.refs_7_ = bf16[32,2048]{1,0:T(8,128)(2,1)S(1)} collective-permute-done((bf16[32,2048]{1,0:T(8,128)(2,1)S(1)}, bf16[32,2048]{1,0:T(8,128)(2,1)S(1)}, u32[]{:S(2)}, u32[]{:S(2)}) %collective-permute-start.6) | collective-permute-done | bytes 131104 | tf_op jit(solution)/shard_map/ppermute | solution.py:300
  22.5 2.7 %collective-permute-start.12 = (bf16[16,2048]{1,0:T(8,128)(2,1)S(1)}, bf16[16,2048]{1,0:T(8,128)(2,1)S(1)}, u32[]{:S(2)}, u32[]{:S(2)}) collective-permute-start(bf16[16,2048]{1,0:T(8,128)(2,1)S(1)} %get-tuple-element.45), channel_id=1, source_target_pairs={{0,1},{1,0},{2,3},{3,2},{4,5},{5,4},{6,7},{7,6},{8,9},{9,8},{10,11... | collective-permute-start | bytes 196616 | tf_op jit(solution)/shard_map/ppermute | solution.py:300
  25.2 1.2 %collective-permute-start.13 = (bf16[16,2048]{1,0:T(8,128)(2,1)S(1)}, bf16[16,2048]{1,0:T(8,128)(2,1)S(1)}, u32[]{:S(2)}, u32[]{:S(2)}) collective-permute-start(bf16[16,2048]{1,0:T(8,128)(2,1)S(1)} %get-tuple-element.46), channel_id=1, source_target_pairs={{0,2},{1,3},{2,0},{3,1},{4,6},{5,7},{6,4},{7,5},{8,10},{9,11},{10,... | collective-permute-start | bytes 196616 | tf_op jit(solution)/shard_map/ppermute | solution.py:300
  26.9 1.0 %after.1 = (bf16[256,2048]{1,0:T(8,128)(2,1)S(1)}, bf16[64,2048]{1,0:T(8,128)(2,1)S(1)}) custom-call(s32[1]{0:T(128)} %bitcast.place_ref, bf16[32,2048]{1,0:T(8,128)(2,1)S(1)} %get-tuple-element.42.refs_0_, bf16[32,2048]{1,0:T(8,128)(2,1)S(1)} %get-tuple-element.43.refs_1_, bf16[32,2048]{1,0:T(8,128)(2,1)S(1)} %collective-permute-done.3.refs_2_, ...), custom_call_target="tpu_custom_call" | custom-call | flops 1 | bytes 1 | tf_op jit(solution)/shard_map/after/pallas_call | solution.py:81
  28.9 1.6 %collective-permute-done.14.refs_7_.refs_6_ = bf16[16,2048]{1,0:T(8,128)(2,1)S(1)} collective-permute-done((bf16[16,2048]{1,0:T(8,128)(2,1)S(1)}, bf16[16,2048]{1,0:T(8,128)(2,1)S(1)}, u32[]{:S(2)}, u32[]{:S(2)}) %collective-permute-start.14) | collective-permute-done | bytes 65568 | tf_op jit(solution)/shard_map/ppermute | solution.py:300
  31.4 1.2 %collective-permute-start.15 = (bf16[64,2048]{1,0:T(8,128)(2,1)S(1)}, bf16[64,2048]{1,0:T(8,128)(2,1)S(1)}, u32[]{:S(2)}, u32[]{:S(2)}) collective-permute-start(bf16[64,2048]{1,0:T(8,128)(2,1)S(1)} %before.1.refs_5_), channel_id=1, source_target_pairs={{2,240},{3,2},{1,3},{0,1},{16,0},{17,16},{19,17},{18,19},{34,18},{... | collective-permute-start | bytes 786440 | tf_op jit(solution)/shard_map/ppermute | solution.py:296
  33.5 2.4 %collective-permute-done.15.refs_1_ = bf16[64,2048]{1,0:T(8,128)(2,1)S(1)} collective-permute-done((bf16[64,2048]{1,0:T(8,128)(2,1)S(1)}, bf16[64,2048]{1,0:T(8,128)(2,1)S(1)}, u32[]{:S(2)}, u32[]{:S(2)}) %collective-permute-start.15) | collective-permute-done | bytes 262176 | tf_op jit(solution)/shard_map/ppermute | solution.py:296
  35.9 2.2 %collective-permute-done.16.refs_2_ = bf16[64,2048]{1,0:T(8,128)(2,1)S(1)} collective-permute-done((bf16[64,2048]{1,0:T(8,128)(2,1)S(1)}, bf16[64,2048]{1,0:T(8,128)(2,1)S(1)}, u32[]{:S(2)}, u32[]{:S(2)}) %collective-permute-start.16) | collective-permute-done | bytes 262176 | tf_op jit(solution)/shard_map/ppermute | solution.py:296
  38.4 3.1 %collective-permute-start.18 = (bf16[64,2048]{1,0:T(8,128)(2,1)S(1)}, bf16[64,2048]{1,0:T(8,128)(2,1)S(1)}, u32[]{:S(2)}, u32[]{:S(2)}) collective-permute-start(bf16[64,2048]{1,0:T(8,128)(2,1)S(1)} %get-tuple-element.50.refs_1_.refs_0_), channel_id=1, source_target_pairs={{2,240},{3,2},{1,3},{0,1},{16,0},{17,16},{19,17},{18,19},{34,18},{... | collective-permute-start | bytes 786440 | tf_op jit(solution)/shard_map/ppermute | solution.py:296
  41.5 3.3 %collective-permute-done.18.refs_3_.refs_2_ = bf16[64,2048]{1,0:T(8,128)(2,1)S(1)} collective-permute-done((bf16[64,2048]{1,0:T(8,128)(2,1)S(1)}, bf16[64,2048]{1,0:T(8,128)(2,1)S(1)}, u32[]{:S(2)}, u32[]{:S(2)}) %collective-permute-start.18) | collective-permute-done | bytes 262176 | tf_op jit(solution)/shard_map/ppermute | solution.py:296
  44.8 7.9 %collective-permute-done.17.refs_2_.refs_1_ = bf16[64,2048]{1,0:T(8,128)(2,1)S(1)} collective-permute-done((bf16[64,2048]{1,0:T(8,128)(2,1)S(1)}, bf16[64,2048]{1,0:T(8,128)(2,1)S(1)}, u32[]{:S(2)}, u32[]{:S(2)}) %collective-permute-start.17) | collective-permute-done | bytes 262176 | tf_op jit(solution)/shard_map/ppermute | solution.py:296
  52.7 3.0 %filter_sums.1 = (bf16[256,432]{1,0:T(8,128)(2,1)S(1)}, bf16[256,432]{1,0:T(8,128)(2,1)S(1)}, bf16[256,432]{1,0:T(8,128)(2,1)S(1)}, bf16[256,432]{1,0:T(8,128)(2,1)S(1)}) custom-call(s32[1]{0:T(128)} %bitcast.place_ref, bf16[256,2048]{1,0:T(8,128)(2,1)S(1)} %get-tuple-element.44.refs_0_, bf16[64,2048]{1,0:T(8,128)(2,1)S(1)} %get-tuple-element.50.refs_1_.refs_0_, ...), custom_call_target="tpu_custom_call" | custom-call | flops 1 | bytes 1 | tf_op jit(solution)/shard_map/filter_sums/pallas_call | solution.py:81
  56.3 3.1 %input_sums.1 = (f32[64,2048]{1,0:T(8,128)S(1)}, bf16[32,2048]{1,0:T(8,128)(2,1)S(1)}, bf16[32,2048]{1,0:T(8,128)(2,1)S(1)}, bf16[32,2048]{1,0:T(8,128)(2,1)S(1)...) custom-call(s32[1]{0:T(128)} %bitcast.place_ref, ...), custom_call_target="tpu_custom_call" | custom-call | flops 1 | bytes 1 | tf_op jit(solution)/shard_map/input_sums/pallas_call | solution.py:81
  59.4 1.0 %collective-permute-start.20 = (bf16[32,2048]{1,0:T(8,128)(2,1)S(1)}, bf16[32,2048]{1,0:T(8,128)(2,1)S(1)}, u32[]{:S(2)}, u32[]{:S(2)}) collective-permute-start(bf16[32,2048]{1,0:T(8,128)(2,1)S(1)} %get-tuple-element.56), channel_id=1, source_target_pairs={{0,12},{4,8},{8,4},{12,0},{1,13},{5,9},{9,5},{13,1},{2,14},{6,10},... | collective-permute-start | bytes 393224 | tf_op jit(solution)/shard_map/ppermute | solution.py:300
  61.1 4.5 %collective-permute-start.30 = (bf16[256,432]{1,0:T(8,128)(2,1)S(1)}, bf16[256,432]{1,0:T(8,128)(2,1)S(1)}, u32[]{:S(2)}, u32[]{:S(2)}) collective-permute-start(bf16[256,432]{1,0:T(8,128)(2,1)S(1)} %lift.1.refs_4_), channel_id=1, source_target_pairs={{0,2},{1,3},{2,0},{3,1},{4,6},{5,7},{6,4},{7,5},{8,10},{9,11},{10,... | collective-permute-start | bytes 663560 | tf_op jit(solution)/shard_map/ppermute | solution.py:300
  66.5 1.7 %collective-permute-start.26 = (bf16[32,2048]{1,0:T(8,128)(2,1)S(1)}, bf16[32,2048]{1,0:T(8,128)(2,1)S(1)}, u32[]{:S(2)}, u32[]{:S(2)}) collective-permute-start(bf16[32,2048]{1,0:T(8,128)(2,1)S(1)} %get-tuple-element.63), channel_id=1, source_target_pairs={{0,12},{4,8},{8,4},{12,0},{1,13},{5,9},{9,5},{13,1},{2,14},{6,10},... | collective-permute-start | bytes 393224 | tf_op jit(solution)/shard_map/ppermute | solution.py:300
  68.5 1.1 %collective-permute-start.25 = (bf16[32,2048]{1,0:T(8,128)(2,1)S(1)}, bf16[32,2048]{1,0:T(8,128)(2,1)S(1)}, u32[]{:S(2)}, u32[]{:S(2)}) collective-permute-start(bf16[32,2048]{1,0:T(8,128)(2,1)S(1)} %get-tuple-element.62), channel_id=1, source_target_pairs={{0,12},{4,8},{8,4},{12,0},{1,13},{5,9},{9,5},{13,1},{2,14},{6,10},... | collective-permute-start | bytes 393224 | tf_op jit(solution)/shard_map/ppermute | solution.py:300
  69.7 1.8 %collective-permute-done.26.refs_4_.refs_6_ = bf16[32,2048]{1,0:T(8,128)(2,1)S(1)} collective-permute-done((bf16[32,2048]{1,0:T(8,128)(2,1)S(1)}, bf16[32,2048]{1,0:T(8,128)(2,1)S(1)}, u32[]{:S(2)}, u32[]{:S(2)}) %collective-permute-start.26) | collective-permute-done | bytes 131104 | tf_op jit(solution)/shard_map/ppermute | solution.py:300
  71.5 1.0 %collective-permute-done.24.refs_2_.refs_4_ = bf16[32,2048]{1,0:T(8,128)(2,1)S(1)} collective-permute-done((bf16[32,2048]{1,0:T(8,128)(2,1)S(1)}, bf16[32,2048]{1,0:T(8,128)(2,1)S(1)}, u32[]{:S(2)}, u32[]{:S(2)}) %collective-permute-start.24) | collective-permute-done | bytes 131104 | tf_op jit(solution)/shard_map/ppermute | solution.py:300
  72.5 2.8 %collective-permute-done.25.refs_3_.refs_5_ = bf16[32,2048]{1,0:T(8,128)(2,1)S(1)} collective-permute-done((bf16[32,2048]{1,0:T(8,128)(2,1)S(1)}, bf16[32,2048]{1,0:T(8,128)(2,1)S(1)}, u32[]{:S(2)}, u32[]{:S(2)}) %collective-permute-start.25) | collective-permute-done | bytes 131104 | tf_op jit(solution)/shard_map/ppermute | solution.py:300
  76.1 3.5 %all-to-all-start = ((bf16[16,16,432]{2,1,0:T(8,128)(2,1)}), bf16[16,16,432]{2,1,0:T(8,128)(2,1)S(1)}, u32[]{:S(2)}, u32[]{:S(2)}) async-start(bf16[16,16,432]{2,1,0:T(8,128)(2,1)} %bitcast.6), calls=%async_computation | async-start | bytes 524288 | tf_op jit(solution)/shard_map/all_to_all | solution.py:433
  79.8 2.1 %collective-permute-start.27 = (bf16[2,16,2048]{2,1,0:T(8,128)(2,1)S(1)}, bf16[2,16,2048]{2,1,0:T(8,128)(2,1)S(1)}, u32[]{:S(2)}, u32[]{:S(2)}) collective-permute-start(bf16[2,16,2048]{2,1,0:T(8,128)(2,1)S(1)} %get-tuple-element.66), channel_id=1, source_target_pairs={{0,1},{1,0},{2,3},{3,2},{4,5},{5,4},{6,7},{7,6},{8,9},{9,8},{10,11... | collective-permute-start | bytes 393224 | tf_op jit(solution)/shard_map/ppermute | solution.py:300
  81.9 1.5 %collective-permute-start.28 = (bf16[2,16,2048]{2,1,0:T(8,128)(2,1)S(1)}, bf16[2,16,2048]{2,1,0:T(8,128)(2,1)S(1)}, u32[]{:S(2)}, u32[]{:S(2)}) collective-permute-start(bf16[2,16,2048]{2,1,0:T(8,128)(2,1)S(1)} %get-tuple-element.67), channel_id=1, source_target_pairs={{0,2},{1,3},{2,0},{3,1},{4,6},{5,7},{6,4},{7,5},{8,10},{9,11},{10,... | collective-permute-start | bytes 393224 | tf_op jit(solution)/shard_map/ppermute | solution.py:300
  83.6 5.0 %collective-permute-done.28.refs_2_ = bf16[2,16,2048]{2,1,0:T(8,128)(2,1)S(1)} collective-permute-done((bf16[2,16,2048]{2,1,0:T(8,128)(2,1)S(1)}, bf16[2,16,2048]{2,1,0:T(8,128)(2,1)S(1)}, u32[]{:S(2)}, u32[]{:S(2)}) %collective-permute-start.28) | collective-permute-done | bytes 131104 | tf_op jit(solution)/shard_map/ppermute | solution.py:300
  88.6 3.5 %collective-permute-done.29.refs_3_ = bf16[2,16,2048]{2,1,0:T(8,128)(2,1)S(1)} collective-permute-done((bf16[2,16,2048]{2,1,0:T(8,128)(2,1)S(1)}, bf16[2,16,2048]{2,1,0:T(8,128)(2,1)S(1)}, u32[]{:S(2)}, u32[]{:S(2)}) %collective-permute-start.29) | collective-permute-done | bytes 131104 | tf_op jit(solution)/shard_map/ppermute | solution.py:300
  92.1 1.0 %close.1 = (bf16[16,4,16,128]{3,2,1,0:T(8,128)(2,1)}, bf16[16,4,16,128]{3,2,1,0:T(8,128)(2,1)}) custom-call(s32[1]{0:T(128)} %bitcast.place_ref, bf16[2,16,2048]{2,1,0:T(8,128)(2,1)S(1)} %get-tuple-element.65.refs_0_, bf16[2,16,2048]{2,1,0:T(8,128)(2,1)S(1)} %collective-permute-done.27.refs_1_, bf16[2,16,2048]{2,1,0:T(8,128)(2,1)S(1)} %collective-permute-done.28.refs_2_, ...), custom_call_target="tpu_custom_call" | custom-call | flops 1 | bytes 1 | tf_op jit(solution)/shard_map/close/pallas_call | solution.py:81
  (53 shorter events, 13.5 us)
Async XLA Ops:
  1.8 6.1 %collective-permute-start = (bf16[16,2048]{1,0:T(8,128)(2,1)S(1)}, bf16[16,2048]{1,0:T(8,128)(2,1)S(1)}, u32[]{:S(2)}, u32[]{:S(2)}) collective-permute-start(bf16[16,2048]{1,0:T(8,128)(2,1)S(1)} %get-tuple-element.38), channel_id=1, source_target_pairs={{0,1},{1,0},{2,3},{3,2},{4,5},{5,4},{6,7},{7,6},{8,9},{9,8},{10,11... | collective-permute-start | bytes 196616 | tf_op jit(solution)/shard_map/ppermute | solution.py:300
  5.1 3.7 %collective-permute-start.1 = (bf16[16,2048]{1,0:T(8,128)(2,1)S(1)}, bf16[16,2048]{1,0:T(8,128)(2,1)S(1)}, u32[]{:S(2)}, u32[]{:S(2)}) collective-permute-start(bf16[16,2048]{1,0:T(8,128)(2,1)S(1)} %get-tuple-element.39), channel_id=1, source_target_pairs={{0,2},{1,3},{2,0},{3,1},{4,6},{5,7},{6,4},{7,5},{8,10},{9,11},{10,... | collective-permute-start | bytes 196616 | tf_op jit(solution)/shard_map/ppermute | solution.py:300
  5.1 5.2 %collective-permute-start.2 = (bf16[16,2048]{1,0:T(8,128)(2,1)S(1)}, bf16[16,2048]{1,0:T(8,128)(2,1)S(1)}, u32[]{:S(2)}, u32[]{:S(2)}) collective-permute-start(bf16[16,2048]{1,0:T(8,128)(2,1)S(1)} %get-tuple-element.40), channel_id=1, source_target_pairs={{0,3},{1,2},{2,1},{3,0},{4,7},{5,6},{6,5},{7,4},{8,11},{9,10},{10,... | collective-permute-start | bytes 196616 | tf_op jit(solution)/shard_map/ppermute | solution.py:300
  10.4 6.2 %collective-permute-start.8 = (bf16[32,2048]{1,0:T(8,128)(2,1)S(1)}, bf16[32,2048]{1,0:T(8,128)(2,1)S(1)}, u32[]{:S(2)}, u32[]{:S(2)}) collective-permute-start(bf16[32,2048]{1,0:T(8,128)(2,1)S(1)} %get-tuple-element.42.refs_0_), channel_id=1, source_target_pairs={{0,12},{4,8},{8,4},{12,0},{1,13},{5,9},{9,5},{13,1},{2,14},{6,10},... | collective-permute-start | bytes 393224 | tf_op jit(solution)/shard_map/ppermute | solution.py:300
  11.5 5.9 %collective-permute-start.3 = (bf16[32,2048]{1,0:T(8,128)(2,1)S(1)}, bf16[32,2048]{1,0:T(8,128)(2,1)S(1)}, u32[]{:S(2)}, u32[]{:S(2)}) collective-permute-start(bf16[32,2048]{1,0:T(8,128)(2,1)S(1)} %get-tuple-element.42.refs_0_), channel_id=1, source_target_pairs={{0,4},{4,0},{8,12},{12,8},{1,5},{5,1},{9,13},{13,9},{2,6},{6,2},{1... | collective-permute-start | bytes 393224 | tf_op jit(solution)/shard_map/ppermute | solution.py:300
  11.5 11.0 %collective-permute-start.11 = (bf16[432,256]{1,0:T(8,128)(2,1)S(1)}, bf16[432,256]{1,0:T(8,128)(2,1)S(1)}, u32[]{:S(2)}, u32[]{:S(2)}) collective-permute-start(bf16[432,256]{1,0:T(8,128)(2,1)S(1)} %get-tuple-element.41.refs_4_.refs_8_.refs_1_.refs_3_), channel_id=1, source_target_pairs={{0,3},{1,2},{2,1},{3,0},{4,7},{5,6},{6,5},{7,4},{8,11},{9,10},{10,... | collective-permute-start | bytes 663560 | tf_op jit(solution)/shard_map/ppermute | solution.py:300
  13.2 12.0 %collective-permute-start.10 = (bf16[432,256]{1,0:T(8,128)(2,1)S(1)}, bf16[432,256]{1,0:T(8,128)(2,1)S(1)}, u32[]{:S(2)}, u32[]{:S(2)}) collective-permute-start(bf16[432,256]{1,0:T(8,128)(2,1)S(1)} %get-tuple-element.41.refs_4_.refs_8_.refs_1_.refs_3_), channel_id=1, source_target_pairs={{0,2},{1,3},{2,0},{3,1},{4,6},{5,7},{6,4},{7,5},{8,10},{9,11},{10,... | collective-permute-start | bytes 663560 | tf_op jit(solution)/shard_map/ppermute | solution.py:300
  13.6 12.7 %collective-permute-start.9 = (bf16[432,256]{1,0:T(8,128)(2,1)S(1)}, bf16[432,256]{1,0:T(8,128)(2,1)S(1)}, u32[]{:S(2)}, u32[]{:S(2)}) collective-permute-start(bf16[432,256]{1,0:T(8,128)(2,1)S(1)} %get-tuple-element.41.refs_4_.refs_8_.refs_1_.refs_3_), channel_id=1, source_target_pairs={{0,1},{1,0},{2,3},{3,2},{4,5},{5,4},{6,7},{7,6},{8,9},{9,8},{10,11... | collective-permute-start | bytes 663560 | tf_op jit(solution)/shard_map/ppermute | solution.py:300
  16.6 5.0 %collective-permute-start.6 = (bf16[32,2048]{1,0:T(8,128)(2,1)S(1)}, bf16[32,2048]{1,0:T(8,128)(2,1)S(1)}, u32[]{:S(2)}, u32[]{:S(2)}) collective-permute-start(bf16[32,2048]{1,0:T(8,128)(2,1)S(1)} %get-tuple-element.43.refs_1_), channel_id=1, source_target_pairs={{0,12},{4,8},{8,4},{12,0},{1,13},{5,9},{9,5},{13,1},{2,14},{6,10},... | collective-permute-start | bytes 393224 | tf_op jit(solution)/shard_map/ppermute | solution.py:300
  17.5 5.0 %collective-permute-start.4 = (bf16[32,2048]{1,0:T(8,128)(2,1)S(1)}, bf16[32,2048]{1,0:T(8,128)(2,1)S(1)}, u32[]{:S(2)}, u32[]{:S(2)}) collective-permute-start(bf16[32,2048]{1,0:T(8,128)(2,1)S(1)} %get-tuple-element.43.refs_1_), channel_id=1, source_target_pairs={{0,4},{4,0},{8,12},{12,8},{1,5},{5,1},{9,13},{13,9},{2,6},{6,2},{1... | collective-permute-start | bytes 393224 | tf_op jit(solution)/shard_map/ppermute | solution.py:300
  21.6 5.4 %collective-permute-start.5 = (bf16[32,2048]{1,0:T(8,128)(2,1)S(1)}, bf16[32,2048]{1,0:T(8,128)(2,1)S(1)}, u32[]{:S(2)}, u32[]{:S(2)}) collective-permute-start(bf16[32,2048]{1,0:T(8,128)(2,1)S(1)} %collective-permute-done.3.refs_2_), channel_id=1, source_target_pairs={{0,12},{4,8},{8,4},{12,0},{1,13},{5,9},{9,5},{13,1},{2,14},{6,10},... | collective-permute-start | bytes 393224 | tf_op jit(solution)/shard_map/ppermute | solution.py:300
  22.5 4.5 %collective-permute-start.7 = (bf16[32,2048]{1,0:T(8,128)(2,1)S(1)}, bf16[32,2048]{1,0:T(8,128)(2,1)S(1)}, u32[]{:S(2)}, u32[]{:S(2)}) collective-permute-start(bf16[32,2048]{1,0:T(8,128)(2,1)S(1)} %collective-permute-done.6.refs_7_), channel_id=1, source_target_pairs={{0,4},{4,0},{8,12},{12,8},{1,5},{5,1},{9,13},{13,9},{2,6},{6,2},{1... | collective-permute-start | bytes 393224 | tf_op jit(solution)/shard_map/ppermute | solution.py:300
  22.5 5.5 %collective-permute-start.12 = (bf16[16,2048]{1,0:T(8,128)(2,1)S(1)}, bf16[16,2048]{1,0:T(8,128)(2,1)S(1)}, u32[]{:S(2)}, u32[]{:S(2)}) collective-permute-start(bf16[16,2048]{1,0:T(8,128)(2,1)S(1)} %get-tuple-element.45), channel_id=1, source_target_pairs={{0,1},{1,0},{2,3},{3,2},{4,5},{5,4},{6,7},{7,6},{8,9},{9,8},{10,11... | collective-permute-start | bytes 196616 | tf_op jit(solution)/shard_map/ppermute | solution.py:300
  25.2 3.7 %collective-permute-start.13 = (bf16[16,2048]{1,0:T(8,128)(2,1)S(1)}, bf16[16,2048]{1,0:T(8,128)(2,1)S(1)}, u32[]{:S(2)}, u32[]{:S(2)}) collective-permute-start(bf16[16,2048]{1,0:T(8,128)(2,1)S(1)} %get-tuple-element.46), channel_id=1, source_target_pairs={{0,2},{1,3},{2,0},{3,1},{4,6},{5,7},{6,4},{7,5},{8,10},{9,11},{10,... | collective-permute-start | bytes 196616 | tf_op jit(solution)/shard_map/ppermute | solution.py:300
  26.4 4.1 %collective-permute-start.14 = (bf16[16,2048]{1,0:T(8,128)(2,1)S(1)}, bf16[16,2048]{1,0:T(8,128)(2,1)S(1)}, u32[]{:S(2)}, u32[]{:S(2)}) collective-permute-start(bf16[16,2048]{1,0:T(8,128)(2,1)S(1)} %get-tuple-element.47), channel_id=1, source_target_pairs={{0,3},{1,2},{2,1},{3,0},{4,7},{5,6},{6,5},{7,4},{8,11},{9,10},{10,... | collective-permute-start | bytes 196616 | tf_op jit(solution)/shard_map/ppermute | solution.py:300
  31.4 4.6 %collective-permute-start.15 = (bf16[64,2048]{1,0:T(8,128)(2,1)S(1)}, bf16[64,2048]{1,0:T(8,128)(2,1)S(1)}, u32[]{:S(2)}, u32[]{:S(2)}) collective-permute-start(bf16[64,2048]{1,0:T(8,128)(2,1)S(1)} %before.1.refs_5_), channel_id=1, source_target_pairs={{2,240},{3,2},{1,3},{0,1},{16,0},{17,16},{19,17},{18,19},{34,18},{... | collective-permute-start | bytes 786440 | tf_op jit(solution)/shard_map/ppermute | solution.py:296
  32.6 5.5 %collective-permute-start.16 = (bf16[64,2048]{1,0:T(8,128)(2,1)S(1)}, bf16[64,2048]{1,0:T(8,128)(2,1)S(1)}, u32[]{:S(2)}, u32[]{:S(2)}) collective-permute-start(bf16[64,2048]{1,0:T(8,128)(2,1)S(1)} %get-tuple-element.48), channel_id=1, source_target_pairs={{2,3},{3,1},{1,0},{0,16},{16,17},{17,19},{19,18},{18,34},{34,35},{... | collective-permute-start | bytes 786440 | tf_op jit(solution)/shard_map/ppermute | solution.py:296
  38.4 6.4 %collective-permute-start.18 = (bf16[64,2048]{1,0:T(8,128)(2,1)S(1)}, bf16[64,2048]{1,0:T(8,128)(2,1)S(1)}, u32[]{:S(2)}, u32[]{:S(2)}) collective-permute-start(bf16[64,2048]{1,0:T(8,128)(2,1)S(1)} %get-tuple-element.50.refs_1_.refs_0_), channel_id=1, source_target_pairs={{2,240},{3,2},{1,3},{0,1},{16,0},{17,16},{19,17},{18,19},{34,18},{... | collective-permute-start | bytes 786440 | tf_op jit(solution)/shard_map/ppermute | solution.py:296
  41.5 11.2 %collective-permute-start.17 = (bf16[64,2048]{1,0:T(8,128)(2,1)S(1)}, bf16[64,2048]{1,0:T(8,128)(2,1)S(1)}, u32[]{:S(2)}, u32[]{:S(2)}) collective-permute-start(bf16[64,2048]{1,0:T(8,128)(2,1)S(1)} %get-tuple-element.50.refs_1_.refs_0_), channel_id=1, source_target_pairs={{2,3},{3,1},{1,0},{0,16},{16,17},{17,19},{19,18},{18,34},{34,35},{... | collective-permute-start | bytes 786440 | tf_op jit(solution)/shard_map/ppermute | solution.py:296
  55.7 5.3 %collective-permute-start.22 = (bf16[256,432]{1,0:T(8,128)(2,1)S(1)}, bf16[256,432]{1,0:T(8,128)(2,1)S(1)}, u32[]{:S(2)}, u32[]{:S(2)}) collective-permute-start(bf16[256,432]{1,0:T(8,128)(2,1)S(1)} %get-tuple-element.59), channel_id=1, source_target_pairs={{0,1},{1,0},{2,3},{3,2},{4,5},{5,4},{6,7},{7,6},{8,9},{9,8},{10,11... | collective-permute-start | bytes 663560 | tf_op jit(solution)/shard_map/ppermute | solution.py:300
  55.8 5.2 %collective-permute-start.23 = (bf16[256,432]{1,0:T(8,128)(2,1)S(1)}, bf16[256,432]{1,0:T(8,128)(2,1)S(1)}, u32[]{:S(2)}, u32[]{:S(2)}) collective-permute-start(bf16[256,432]{1,0:T(8,128)(2,1)S(1)} %get-tuple-element.60), channel_id=1, source_target_pairs={{0,1},{1,0},{2,3},{3,2},{4,5},{5,4},{6,7},{7,6},{8,9},{9,8},{10,11... | collective-permute-start | bytes 663560 | tf_op jit(solution)/shard_map/ppermute | solution.py:300
  59.4 8.8 %collective-permute-start.20 = (bf16[32,2048]{1,0:T(8,128)(2,1)S(1)}, bf16[32,2048]{1,0:T(8,128)(2,1)S(1)}, u32[]{:S(2)}, u32[]{:S(2)}) collective-permute-start(bf16[32,2048]{1,0:T(8,128)(2,1)S(1)} %get-tuple-element.56), channel_id=1, source_target_pairs={{0,12},{4,8},{8,4},{12,0},{1,13},{5,9},{9,5},{13,1},{2,14},{6,10},... | collective-permute-start | bytes 393224 | tf_op jit(solution)/shard_map/ppermute | solution.py:300
  60.4 7.8 %collective-permute-start.21 = (bf16[32,2048]{1,0:T(8,128)(2,1)S(1)}, bf16[32,2048]{1,0:T(8,128)(2,1)S(1)}, u32[]{:S(2)}, u32[]{:S(2)}) collective-permute-start(bf16[32,2048]{1,0:T(8,128)(2,1)S(1)} %get-tuple-element.57), channel_id=1, source_target_pairs={{0,4},{4,0},{8,12},{12,8},{1,5},{5,1},{9,13},{13,9},{2,6},{6,2},{1... | collective-permute-start | bytes 393224 | tf_op jit(solution)/shard_map/ppermute | solution.py:300
  61.1 14.2 %collective-permute-start.30 = (bf16[256,432]{1,0:T(8,128)(2,1)S(1)}, bf16[256,432]{1,0:T(8,128)(2,1)S(1)}, u32[]{:S(2)}, u32[]{:S(2)}) collective-permute-start(bf16[256,432]{1,0:T(8,128)(2,1)S(1)} %lift.1.refs_4_), channel_id=1, source_target_pairs={{0,2},{1,3},{2,0},{3,1},{4,6},{5,7},{6,4},{7,5},{8,10},{9,11},{10,... | collective-permute-start | bytes 663560 | tf_op jit(solution)/shard_map/ppermute | solution.py:300
  65.6 4.1 %collective-permute-start.19 = (bf16[32,2048]{1,0:T(8,128)(2,1)S(1)}, bf16[32,2048]{1,0:T(8,128)(2,1)S(1)}, u32[]{:S(2)}, u32[]{:S(2)}) collective-permute-start(bf16[32,2048]{1,0:T(8,128)(2,1)S(1)} %get-tuple-element.53), channel_id=1, source_target_pairs={{0,4},{4,0},{8,12},{12,8},{1,5},{5,1},{9,13},{13,9},{2,6},{6,2},{1... | collective-permute-start | bytes 393224 | tf_op jit(solution)/shard_map/ppermute | solution.py:300
  66.5 5.0 %collective-permute-start.26 = (bf16[32,2048]{1,0:T(8,128)(2,1)S(1)}, bf16[32,2048]{1,0:T(8,128)(2,1)S(1)}, u32[]{:S(2)}, u32[]{:S(2)}) collective-permute-start(bf16[32,2048]{1,0:T(8,128)(2,1)S(1)} %get-tuple-element.63), channel_id=1, source_target_pairs={{0,12},{4,8},{8,4},{12,0},{1,13},{5,9},{9,5},{13,1},{2,14},{6,10},... | collective-permute-start | bytes 393224 | tf_op jit(solution)/shard_map/ppermute | solution.py:300
  68.3 4.2 %collective-permute-start.24 = (bf16[32,2048]{1,0:T(8,128)(2,1)S(1)}, bf16[32,2048]{1,0:T(8,128)(2,1)S(1)}, u32[]{:S(2)}, u32[]{:S(2)}) collective-permute-start(bf16[32,2048]{1,0:T(8,128)(2,1)S(1)} %get-tuple-element.61), channel_id=1, source_target_pairs={{0,4},{4,0},{8,12},{12,8},{1,5},{5,1},{9,13},{13,9},{2,6},{6,2},{1... | collective-permute-start | bytes 393224 | tf_op jit(solution)/shard_map/ppermute | solution.py:300
  68.5 6.8 %collective-permute-start.25 = (bf16[32,2048]{1,0:T(8,128)(2,1)S(1)}, bf16[32,2048]{1,0:T(8,128)(2,1)S(1)}, u32[]{:S(2)}, u32[]{:S(2)}) collective-permute-start(bf16[32,2048]{1,0:T(8,128)(2,1)S(1)} %get-tuple-element.62), channel_id=1, source_target_pairs={{0,12},{4,8},{8,4},{12,0},{1,13},{5,9},{9,5},{13,1},{2,14},{6,10},... | collective-permute-start | bytes 393224 | tf_op jit(solution)/shard_map/ppermute | solution.py:300
  76.1 17.0 %all-to-all-start = ((bf16[16,16,432]{2,1,0:T(8,128)(2,1)}), bf16[16,16,432]{2,1,0:T(8,128)(2,1)S(1)}, u32[]{:S(2)}, u32[]{:S(2)}) async-start(bf16[16,16,432]{2,1,0:T(8,128)(2,1)} %bitcast.6), calls=%async_computation | async-start | bytes 524288 | tf_op jit(solution)/shard_map/all_to_all | solution.py:433
  79.8 3.8 %collective-permute-start.27 = (bf16[2,16,2048]{2,1,0:T(8,128)(2,1)S(1)}, bf16[2,16,2048]{2,1,0:T(8,128)(2,1)S(1)}, u32[]{:S(2)}, u32[]{:S(2)}) collective-permute-start(bf16[2,16,2048]{2,1,0:T(8,128)(2,1)S(1)} %get-tuple-element.66), channel_id=1, source_target_pairs={{0,1},{1,0},{2,3},{3,2},{4,5},{5,4},{6,7},{7,6},{8,9},{9,8},{10,11... | collective-permute-start | bytes 393224 | tf_op jit(solution)/shard_map/ppermute | solution.py:300
  81.9 6.7 %collective-permute-start.28 = (bf16[2,16,2048]{2,1,0:T(8,128)(2,1)S(1)}, bf16[2,16,2048]{2,1,0:T(8,128)(2,1)S(1)}, u32[]{:S(2)}, u32[]{:S(2)}) collective-permute-start(bf16[2,16,2048]{2,1,0:T(8,128)(2,1)S(1)} %get-tuple-element.67), channel_id=1, source_target_pairs={{0,2},{1,3},{2,0},{3,1},{4,6},{5,7},{6,4},{7,5},{8,10},{9,11},{10,... | collective-permute-start | bytes 393224 | tf_op jit(solution)/shard_map/ppermute | solution.py:300
  83.3 8.8 %collective-permute-start.29 = (bf16[2,16,2048]{2,1,0:T(8,128)(2,1)S(1)}, bf16[2,16,2048]{2,1,0:T(8,128)(2,1)S(1)}, u32[]{:S(2)}, u32[]{:S(2)}) collective-permute-start(bf16[2,16,2048]{2,1,0:T(8,128)(2,1)S(1)} %get-tuple-element.68), channel_id=1, source_target_pairs={{0,3},{1,2},{2,1},{3,0},{4,7},{5,6},{6,5},{7,4},{8,11},{9,10},{10,... | collective-permute-start | bytes 393224 | tf_op jit(solution)/shard_map/ppermute | solution.py:300
  (3 other events, 8.1 us)

commit v3 on v2

--- a/solution.py
+++ b/solution.py
@@ -74,7 +74,7 @@
     return pl.ds(pl.multiple_of(partner(place_ref, axis, j) * rows, rows), rows)
 
 
-def call(kernel, outputs, name, place, *operands, unread=(), scratch=()):
+def call(kernel, outputs, name, place, *operands, unread=(), scratch=(), flops=1):
     def run(place_ref, *refs):
         kernel(place_ref, *refs[: len(operands)], *refs[len(operands) + len(unread) :])
 
@@ -87,7 +87,7 @@
         out_shape=[jax.ShapeDtypeStruct(shape, dtype) for shape, dtype in outputs],
         scratch_shapes=list(scratch),
         compiler_params=pltpu.CompilerParams(vmem_limit_bytes=VMEM_LIMIT),
-        cost_estimate=pl.CostEstimate(flops=1, bytes_accessed=1, transcendentals=0),
+        cost_estimate=pl.CostEstimate(flops=flops, bytes_accessed=1, transcendentals=0),
         name=name,
     )(place, *operands, *unread)
 
@@ -104,13 +104,17 @@
     matrix_ref[...] = filters_ref[...]
 
 
-def halves_kernel(place_ref, *refs):
-    pieces, (low_ref, high_ref, order_ref) = refs[:GROUP], refs[GROUP:]
+def order_kernel(place_ref, *refs):
+    pieces, (out_ref,) = refs[:GROUP], refs[GROUP:]
+    for j, piece_ref in enumerate(pieces):
+        out_ref[block_rows(place_ref, "part", j, piece_ref.shape[0]), :] = piece_ref[...]
+
+
+def cut_kernel(place_ref, near_ref, other_ref, low_ref, high_ref):
+    del place_ref
     half = low_ref.shape[0]
-    for j, piece_ref in enumerate(pieces):
-        order_ref[block_rows(place_ref, "part", j, half // 2), :] = piece_ref[...]
-    low_ref[...] = order_ref[:half]
-    high_ref[...] = order_ref[half:]
+    low_ref[...] = near_ref[:half]
+    high_ref[...] = other_ref[half:]
 
 
 def edge_sums(place_ref, field_ref, matrices, out_ref, a):
@@ -127,12 +131,14 @@
 
 
 def after_kernel(place_ref, *refs):
-    halves, matrices = refs[: 2 * GROUP], refs[2 * GROUP : 3 * GROUP]
-    field_ref, after_ref = refs[3 * GROUP :]
-    for k, part_ref in enumerate(halves):
-        half = part_ref.shape[0]
-        start = partner(place_ref, "run", k // 2) * 2 * half + (k % 2) * half
-        field_ref[pl.ds(pl.multiple_of(start, half), half), :] = part_ref[...]
+    blocks, halves, matrices = refs[:3], refs[3:5], refs[5 : 5 + GROUP]
+    field_ref, after_ref = refs[5 + GROUP :]
+    for j, ref in zip((0, 1, 3), blocks):
+        field_ref[block_rows(place_ref, "run", j, ref.shape[0]), :] = ref[...]
+    for k, ref in enumerate(halves):
+        half = ref.shape[0]
+        start = (partner(place_ref, "run", 2) * 2 + k) * half
+        field_ref[pl.ds(pl.multiple_of(start, half), half), :] = ref[...]
     edge_sums(place_ref, field_ref, matrices, after_ref, 0)
 
 
@@ -329,18 +335,14 @@
         unread=[volumes[0]],
     )
     volumes, cotangents = swapped(volumes, "part"), swapped(cotangents, "part")
-    low, high = call(
-        halves_kernel,
-        [((half, plane), bf16)] * 2,
-        "halves",
-        place,
-        *volumes,
-        unread=[matrix],
-        scratch=[pltpu.VMEM((depth, plane), bf16)],
-    )
-    low_1, high_3 = swap(low, "run", 1), swap(high, "run", 3)
-    high_1, low_3 = swap(high, "run", 1), swap(low, "run", 3)
-    low_2, high_2 = swap(low_1, "run", 3), swap(high_3, "run", 1)
+    (block,) = call(
+        order_kernel, [((depth, plane), bf16)], "order", place, *volumes, unread=[matrix]
+    )
+    block_1, block_3 = swap(block, "run", 1), swap(block, "run", 3)
+    low_2, high_2 = call(
+        cut_kernel, [((half, plane), bf16)] * 2, "cut", place, block_1, block_3
+    )
+    low_2, high_2 = swap(low_2, "run", 3), swap(high_2, "run", 1)
     matrices = swapped([matrix] * GROUP, "part")
 
     field, after = call(
@@ -348,7 +350,7 @@
         [((in_total, plane), bf16), ((rows, plane), bf16)],
         "after",
         place,
-        *(low, high, low_1, high_1, low_2, high_2, low_3, high_3),
+        *(block, block_1, block_3, low_2, high_2),
         *matrices,
     )
     after = shifted(after, 1)
@@ -428,7 +430,7 @@
         "merge",
         place,
         *(sums, sums_1, sums_2),
-        unread=[low_1, high_1, low_3, high_3],
+        unread=[low_1, high_3],
     )
     sums = lax.all_to_all(
         sums.reshape(spaces, in_total // spaces, taps),

time: 94.3 us -> 99.2 us (1.052)
  waiting for transfers between devices: 42 us -> 46.8 us
    ppermute x27 -> x25, waiting for transfers between devices: 26.2 us -> 31 us  [swap(): lax.ppermute(value, axis, [(i, i ^ j) for i in range(lax.axis_size(axis))])]
    ppermute x27 -> x25, starting transfers between devices: 29 us -> 29.7 us  [swap(): lax.ppermute(value, axis, [(i, i ^ j) for i in range(lax.axis_size(axis))])]
    pallas_call x15 -> x16, Pallas kernels: 12.4 us -> 12.4 us  [call(): pl.pallas_call(run, in_specs=[pl.BlockSpec(memory_space=pltpu.SMEM)] + [p...]
  transfers between devices with their start and end apart: 32 -> 30, of which waited for: 16 -> 17; matrix products, arithmetic and copies ran while one was open for 0% -> 0% of each run, Pallas kernels for 7% -> 6%
where the time goes in v3:
time: 99.2 us; the launch traced here: 99 us
  waiting for transfers between devices  46.8 us (47%)
  starting transfers between devices  37 us (37%)
  Pallas kernels  12.4 us (12%)
  local copies, waits for them, and re-layouts  1.92 us (2%)
    ppermute x25, waiting for transfers between devices, swap(): lax.ppermute(value, axis, [(i, i ^ j) for i in range(lax.axis_size(axis))])  31 us
    ppermute x25, starting transfers between devices, swap(): lax.ppermute(value, axis, [(i, i ^ j) for i in range(lax.axis_size(axis))])  29.7 us
    ppermute x4, waiting for transfers between devices, shifted(): lax.ppermute(value, DEPTH, [(at[i], at[(i + by) % count]) for i in range(...  15.8 us
    pallas_call x16, Pallas kernels, call(): pl.pallas_call(run, in_specs=[pl.BlockSpec(memory_space=pltpu.SMEM)] + [p...  12.4 us
    ppermute x4, starting transfers between devices, shifted(): lax.ppermute(value, DEPTH, [(at[i], at[(i + by) % count]) for i in range(...  3.85 us
    all_to_all x1, starting transfers between devices, body(): lax.all_to_all(sums.reshape(spaces, in_total // spaces, taps), 'space', s...  3.53 us
  transfers between devices with their start and end apart: 30, of which 17 were waited for; matrix products, arithmetic and copies ran while one was open for 0% of the time, Pallas kernels for 6%

profile of v3, /device:TPU:1, one launch (start us, length us, event | category | flops | bytes accessed | tf_op | source)
XLA Modules:
  0.0 99.0 jit_solution(641453734580569496)
XLA Ops:
  1.8 3.3 %collective-permute-start = (bf16[16,2048]{1,0:T(8,128)(2,1)S(1)}, bf16[16,2048]{1,0:T(8,128)(2,1)S(1)}, u32[]{:S(2)}, u32[]{:S(2)}) collective-permute-start(bf16[16,2048]{1,0:T(8,128)(2,1)S(1)} %get-tuple-element.38), channel_id=1, source_target_pairs={{0,1},{1,0},{2,3},{3,2},{4,5},{5,4},{6,7},{7,6},{8,9},{9,8},{10,11... | collective-permute-start | bytes 196616 | tf_op jit(solution)/shard_map/ppermute | solution.py:306
  5.1 1.7 %collective-permute-start.2 = (bf16[16,2048]{1,0:T(8,128)(2,1)S(1)}, bf16[16,2048]{1,0:T(8,128)(2,1)S(1)}, u32[]{:S(2)}, u32[]{:S(2)}) collective-permute-start(bf16[16,2048]{1,0:T(8,128)(2,1)S(1)} %get-tuple-element.40), channel_id=1, source_target_pairs={{0,3},{1,2},{2,1},{3,0},{4,7},{5,6},{6,5},{7,4},{8,11},{9,10},{10,... | collective-permute-start | bytes 196616 | tf_op jit(solution)/shard_map/ppermute | solution.py:306
  8.7 1.6 %collective-permute-done.2.refs_3_ = bf16[16,2048]{1,0:T(8,128)(2,1)S(1)} collective-permute-done((bf16[16,2048]{1,0:T(8,128)(2,1)S(1)}, bf16[16,2048]{1,0:T(8,128)(2,1)S(1)}, u32[]{:S(2)}, u32[]{:S(2)}) %collective-permute-start.2) | collective-permute-done | bytes 65568 | tf_op jit(solution)/shard_map/ppermute | solution.py:306
  10.4 1.1 %collective-permute-start.4 = (bf16[64,2048]{1,0:T(8,128)(2,1)S(1)}, bf16[64,2048]{1,0:T(8,128)(2,1)S(1)}, u32[]{:S(2)}, u32[]{:S(2)}) collective-permute-start(bf16[64,2048]{1,0:T(8,128)(2,1)S(1)} %order.1.refs_0_), channel_id=1, source_target_pairs={{0,12},{4,8},{8,4},{12,0},{1,13},{5,9},{9,5},{13,1},{2,14},{6,10},... | collective-permute-start | bytes 786440 | tf_op jit(solution)/shard_map/ppermute | solution.py:306
  11.5 1.7 %collective-permute-start.9 = (bf16[432,256]{1,0:T(8,128)(2,1)S(1)}, bf16[432,256]{1,0:T(8,128)(2,1)S(1)}, u32[]{:S(2)}, u32[]{:S(2)}) collective-permute-start(bf16[432,256]{1,0:T(8,128)(2,1)S(1)} %get-tuple-element.41.refs_4_.refs_5_.refs_1_.refs_3_), channel_id=1, source_target_pairs={{0,3},{1,2},{2,1},{3,0},{4,7},{5,6},{6,5},{7,4},{8,11},{9,10},{10,... | collective-permute-start | bytes 663560 | tf_op jit(solution)/shard_map/ppermute | solution.py:306
  13.6 5.7 %collective-permute-done.4.refs_1_.refs_2_ = bf16[64,2048]{1,0:T(8,128)(2,1)S(1)} collective-permute-done((bf16[64,2048]{1,0:T(8,128)(2,1)S(1)}, bf16[64,2048]{1,0:T(8,128)(2,1)S(1)}, u32[]{:S(2)}, u32[]{:S(2)}) %collective-permute-start.4) | collective-permute-done | bytes 262176 | tf_op jit(solution)/shard_map/ppermute | solution.py:306
  19.4 1.2 %collective-permute-start.5 = (bf16[32,2048]{1,0:T(8,128)(2,1)S(1)}, bf16[32,2048]{1,0:T(8,128)(2,1)S(1)}, u32[]{:S(2)}, u32[]{:S(2)}) collective-permute-start(bf16[32,2048]{1,0:T(8,128)(2,1)S(1)} %get-tuple-element.42), channel_id=1, source_target_pairs={{0,12},{4,8},{8,4},{12,0},{1,13},{5,9},{9,5},{13,1},{2,14},{6,10},... | collective-permute-start | bytes 393224 | tf_op jit(solution)/shard_map/ppermute | solution.py:306
  20.6 1.6 %collective-permute-start.10 = (bf16[16,2048]{1,0:T(8,128)(2,1)S(1)}, bf16[16,2048]{1,0:T(8,128)(2,1)S(1)}, u32[]{:S(2)}, u32[]{:S(2)}) collective-permute-start(bf16[16,2048]{1,0:T(8,128)(2,1)S(1)} %get-tuple-element.45), channel_id=1, source_target_pairs={{0,1},{1,0},{2,3},{3,2},{4,5},{5,4},{6,7},{7,6},{8,9},{9,8},{10,11... | collective-permute-start | bytes 196616 | tf_op jit(solution)/shard_map/ppermute | solution.py:306
  22.2 1.9 %collective-permute-done.8.refs_7_.refs_3_.refs_5_ = bf16[432,256]{1,0:T(8,128)(2,1)S(1)} collective-permute-done((bf16[432,256]{1,0:T(8,128)(2,1)S(1)}, bf16[432,256]{1,0:T(8,128)(2,1)S(1)}, u32[]{:S(2)}, u32[]{:S(2)}) %collective-permute-start.8) | collective-permute-done | bytes 221216 | tf_op jit(solution)/shard_map/ppermute | solution.py:306
  24.2 1.1 %collective-permute-start.11 = (bf16[16,2048]{1,0:T(8,128)(2,1)S(1)}, bf16[16,2048]{1,0:T(8,128)(2,1)S(1)}, u32[]{:S(2)}, u32[]{:S(2)}) collective-permute-start(bf16[16,2048]{1,0:T(8,128)(2,1)S(1)} %get-tuple-element.46), channel_id=1, source_target_pairs={{0,2},{1,3},{2,0},{3,1},{4,6},{5,7},{6,4},{7,5},{8,10},{9,11},{10,... | collective-permute-start | bytes 196616 | tf_op jit(solution)/shard_map/ppermute | solution.py:306
  26.2 1.0 %after.1 = (bf16[256,2048]{1,0:T(8,128)(2,1)S(1)}, bf16[64,2048]{1,0:T(8,128)(2,1)S(1)}) custom-call(s32[1]{0:T(128)} %bitcast.place_ref, bf16[64,2048]{1,0:T(8,128)(2,1)S(1)} %order.1.refs_0_, bf16[64,2048]{1,0:T(8,128)(2,1)S(1)} %collective-permute-done.3.refs_0_.refs_1_, bf16[64,2048]{1,0:T(8,128)(2,1)S(1)} %collective-permute-done.4.refs_1_.refs_2_, ...), custom_call_target="tpu_custom_call" | custom-call | flops 1 | bytes 1 | tf_op jit(solution)/shard_map/after/pallas_call | solution.py:81
  27.3 2.6 %collective-permute-done.12.refs_7_.refs_6_ = bf16[16,2048]{1,0:T(8,128)(2,1)S(1)} collective-permute-done((bf16[16,2048]{1,0:T(8,128)(2,1)S(1)}, bf16[16,2048]{1,0:T(8,128)(2,1)S(1)}, u32[]{:S(2)}, u32[]{:S(2)}) %collective-permute-start.12) | collective-permute-done | bytes 65568 | tf_op jit(solution)/shard_map/ppermute | solution.py:306
  32.7 2.4 %collective-permute-done.13.refs_1_ = bf16[64,2048]{1,0:T(8,128)(2,1)S(1)} collective-permute-done((bf16[64,2048]{1,0:T(8,128)(2,1)S(1)}, bf16[64,2048]{1,0:T(8,128)(2,1)S(1)}, u32[]{:S(2)}, u32[]{:S(2)}) %collective-permute-start.13) | collective-permute-done | bytes 262176 | tf_op jit(solution)/shard_map/ppermute | solution.py:302
  35.0 2.2 %collective-permute-done.14.refs_2_ = bf16[64,2048]{1,0:T(8,128)(2,1)S(1)} collective-permute-done((bf16[64,2048]{1,0:T(8,128)(2,1)S(1)}, bf16[64,2048]{1,0:T(8,128)(2,1)S(1)}, u32[]{:S(2)}, u32[]{:S(2)}) %collective-permute-start.14) | collective-permute-done | bytes 262176 | tf_op jit(solution)/shard_map/ppermute | solution.py:302
  37.6 3.0 %collective-permute-start.16 = (bf16[64,2048]{1,0:T(8,128)(2,1)S(1)}, bf16[64,2048]{1,0:T(8,128)(2,1)S(1)}, u32[]{:S(2)}, u32[]{:S(2)}) collective-permute-start(bf16[64,2048]{1,0:T(8,128)(2,1)S(1)} %get-tuple-element.50.refs_1_.refs_0_), channel_id=1, source_target_pairs={{2,240},{3,2},{1,3},{0,1},{16,0},{17,16},{19,17},{18,19},{34,18},{... | collective-permute-start | bytes 786440 | tf_op jit(solution)/shard_map/ppermute | solution.py:302
  40.6 3.3 %collective-permute-done.16.refs_3_.refs_2_ = bf16[64,2048]{1,0:T(8,128)(2,1)S(1)} collective-permute-done((bf16[64,2048]{1,0:T(8,128)(2,1)S(1)}, bf16[64,2048]{1,0:T(8,128)(2,1)S(1)}, u32[]{:S(2)}, u32[]{:S(2)}) %collective-permute-start.16) | collective-permute-done | bytes 262176 | tf_op jit(solution)/shard_map/ppermute | solution.py:302
  43.9 7.9 %collective-permute-done.15.refs_2_.refs_1_ = bf16[64,2048]{1,0:T(8,128)(2,1)S(1)} collective-permute-done((bf16[64,2048]{1,0:T(8,128)(2,1)S(1)}, bf16[64,2048]{1,0:T(8,128)(2,1)S(1)}, u32[]{:S(2)}, u32[]{:S(2)}) %collective-permute-start.15) | collective-permute-done | bytes 262176 | tf_op jit(solution)/shard_map/ppermute | solution.py:302
  51.8 3.0 %filter_sums.1 = (bf16[256,432]{1,0:T(8,128)(2,1)S(1)}, bf16[256,432]{1,0:T(8,128)(2,1)S(1)}, bf16[256,432]{1,0:T(8,128)(2,1)S(1)}, bf16[256,432]{1,0:T(8,128)(2,1)S(1)}) custom-call(s32[1]{0:T(128)} %bitcast.place_ref, bf16[256,2048]{1,0:T(8,128)(2,1)S(1)} %get-tuple-element.44.refs_0_, bf16[64,2048]{1,0:T(8,128)(2,1)S(1)} %get-tuple-element.50.refs_1_.refs_0_, ...), custom_call_target="tpu_custom_call" | custom-call | flops 1 | bytes 1 | tf_op jit(solution)/shard_map/filter_sums/pallas_call | solution.py:81
  55.3 3.1 %input_sums.1 = (f32[64,2048]{1,0:T(8,128)S(1)}, bf16[32,2048]{1,0:T(8,128)(2,1)S(1)}, bf16[32,2048]{1,0:T(8,128)(2,1)S(1)}, bf16[32,2048]{1,0:T(8,128)(2,1)S(1)...) custom-call(s32[1]{0:T(128)} %bitcast.place_ref, ...), custom_call_target="tpu_custom_call" | custom-call | flops 1 | bytes 1 | tf_op jit(solution)/shard_map/input_sums/pallas_call | solution.py:81
  58.5 4.5 %collective-permute-start.28 = (bf16[256,432]{1,0:T(8,128)(2,1)S(1)}, bf16[256,432]{1,0:T(8,128)(2,1)S(1)}, u32[]{:S(2)}, u32[]{:S(2)}) collective-permute-start(bf16[256,432]{1,0:T(8,128)(2,1)S(1)} %lift.1.refs_4_), channel_id=1, source_target_pairs={{0,2},{1,3},{2,0},{3,1},{4,6},{5,7},{6,4},{7,5},{8,10},{9,11},{10,... | collective-permute-start | bytes 663560 | tf_op jit(solution)/shard_map/ppermute | solution.py:306
  63.1 1.4 %collective-permute-start.17 = (bf16[32,2048]{1,0:T(8,128)(2,1)S(1)}, bf16[32,2048]{1,0:T(8,128)(2,1)S(1)}, u32[]{:S(2)}, u32[]{:S(2)}) collective-permute-start(bf16[32,2048]{1,0:T(8,128)(2,1)S(1)} %get-tuple-element.53), channel_id=1, source_target_pairs={{0,4},{4,0},{8,12},{12,8},{1,5},{5,1},{9,13},{13,9},{2,6},{6,2},{1... | collective-permute-start | bytes 393224 | tf_op jit(solution)/shard_map/ppermute | solution.py:306
  64.6 2.8 %collective-permute-done.17.refs_1_.refs_3_ = bf16[32,2048]{1,0:T(8,128)(2,1)S(1)} collective-permute-done((bf16[32,2048]{1,0:T(8,128)(2,1)S(1)}, bf16[32,2048]{1,0:T(8,128)(2,1)S(1)}, u32[]{:S(2)}, u32[]{:S(2)}) %collective-permute-start.17) | collective-permute-done | bytes 131104 | tf_op jit(solution)/shard_map/ppermute | solution.py:306
  67.4 2.1 %collective-permute-done.24.refs_4_ = bf16[32,2048]{1,0:T(8,128)(2,1)S(1)} collective-permute-done((bf16[32,2048]{1,0:T(8,128)(2,1)S(1)}, bf16[32,2048]{1,0:T(8,128)(2,1)S(1)}, u32[]{:S(2)}, u32[]{:S(2)}) %collective-permute-start.24) | collective-permute-done | bytes 131104 | tf_op jit(solution)/shard_map/ppermute | solution.py:306
  70.3 3.5 %all-to-all-start = ((bf16[16,16,432]{2,1,0:T(8,128)(2,1)}), bf16[16,16,432]{2,1,0:T(8,128)(2,1)S(1)}, u32[]{:S(2)}, u32[]{:S(2)}) async-start(bf16[16,16,432]{2,1,0:T(8,128)(2,1)} %bitcast.6), calls=%async_computation | async-start | bytes 524288 | tf_op jit(solution)/shard_map/all_to_all | solution.py:435
  75.3 3.6 %collective-permute-done.18.refs_2_ = bf16[32,2048]{1,0:T(8,128)(2,1)S(1)} collective-permute-done((bf16[32,2048]{1,0:T(8,128)(2,1)S(1)}, bf16[32,2048]{1,0:T(8,128)(2,1)S(1)}, u32[]{:S(2)}, u32[]{:S(2)}) %collective-permute-start.18) | collective-permute-done | bytes 131104 | tf_op jit(solution)/shard_map/ppermute | solution.py:306
  79.8 2.0 %collective-permute-start.23 = (bf16[32,2048]{1,0:T(8,128)(2,1)S(1)}, bf16[32,2048]{1,0:T(8,128)(2,1)S(1)}, u32[]{:S(2)}, u32[]{:S(2)}) collective-permute-start(bf16[32,2048]{1,0:T(8,128)(2,1)S(1)} %get-tuple-element.62), channel_id=1, source_target_pairs={{0,12},{4,8},{8,4},{12,0},{1,13},{5,9},{9,5},{13,1},{2,14},{6,10},... | collective-permute-start | bytes 393224 | tf_op jit(solution)/shard_map/ppermute | solution.py:306
  81.8 1.7 %collective-permute-done.22.refs_2_ = bf16[32,2048]{1,0:T(8,128)(2,1)S(1)} collective-permute-done((bf16[32,2048]{1,0:T(8,128)(2,1)S(1)}, bf16[32,2048]{1,0:T(8,128)(2,1)S(1)}, u32[]{:S(2)}, u32[]{:S(2)}) %collective-permute-start.22) | collective-permute-done | bytes 131104 | tf_op jit(solution)/shard_map/ppermute | solution.py:306
  83.4 1.7 %collective-permute-done.23.refs_3_ = bf16[32,2048]{1,0:T(8,128)(2,1)S(1)} collective-permute-done((bf16[32,2048]{1,0:T(8,128)(2,1)S(1)}, bf16[32,2048]{1,0:T(8,128)(2,1)S(1)}, u32[]{:S(2)}, u32[]{:S(2)}) %collective-permute-start.23) | collective-permute-done | bytes 131104 | tf_op jit(solution)/shard_map/ppermute | solution.py:306
  85.3 3.8 %collective-permute-start.25 = (bf16[2,16,2048]{2,1,0:T(8,128)(2,1)S(1)}, bf16[2,16,2048]{2,1,0:T(8,128)(2,1)S(1)}, u32[]{:S(2)}, u32[]{:S(2)}) collective-permute-start(bf16[2,16,2048]{2,1,0:T(8,128)(2,1)S(1)} %get-tuple-element.66), channel_id=1, source_target_pairs={{0,1},{1,0},{2,3},{3,2},{4,5},{5,4},{6,7},{7,6},{8,9},{9,8},{10,11... | collective-permute-start | bytes 393224 | tf_op jit(solution)/shard_map/ppermute | solution.py:306
  89.7 1.1 %collective-permute-start.27 = (bf16[2,16,2048]{2,1,0:T(8,128)(2,1)S(1)}, bf16[2,16,2048]{2,1,0:T(8,128)(2,1)S(1)}, u32[]{:S(2)}, u32[]{:S(2)}) collective-permute-start(bf16[2,16,2048]{2,1,0:T(8,128)(2,1)S(1)} %get-tuple-element.68), channel_id=1, source_target_pairs={{0,3},{1,2},{2,1},{3,0},{4,7},{5,6},{6,5},{7,4},{8,11},{9,10},{10,... | collective-permute-start | bytes 393224 | tf_op jit(solution)/shard_map/ppermute | solution.py:306
  90.8 3.3 %collective-permute-done.26.refs_2_ = bf16[2,16,2048]{2,1,0:T(8,128)(2,1)S(1)} collective-permute-done((bf16[2,16,2048]{2,1,0:T(8,128)(2,1)S(1)}, bf16[2,16,2048]{2,1,0:T(8,128)(2,1)S(1)}, u32[]{:S(2)}, u32[]{:S(2)}) %collective-permute-start.26) | collective-permute-done | bytes 131104 | tf_op jit(solution)/shard_map/ppermute | solution.py:306
  94.2 3.0 %collective-permute-done.27.refs_3_ = bf16[2,16,2048]{2,1,0:T(8,128)(2,1)S(1)} collective-permute-done((bf16[2,16,2048]{2,1,0:T(8,128)(2,1)S(1)}, bf16[2,16,2048]{2,1,0:T(8,128)(2,1)S(1)}, u32[]{:S(2)}, u32[]{:S(2)}) %collective-permute-start.27) | collective-permute-done | bytes 131104 | tf_op jit(solution)/shard_map/ppermute | solution.py:306
  (50 shorter events, 14.1 us)
Async XLA Ops:
  0.6 6.2 %copy-start = (bf16[1,16,4,16,128]{4,3,2,1,0:T(8,128)(2,1)S(1)}, bf16[1,16,4,16,128]{4,3,2,1,0:T(8,128)(2,1)}, u32[]{:S(2)}) copy-start(bf16[1,16,4,16,128]{4,3,2,1,0:T(8,128)(2,1)} %param.5) | copy-start | bytes 786436
  0.6 1.0 %copy-start.1 = (bf16[1,16,4,16,128]{4,3,2,1,0:T(8,128)(2,1)S(1)}, bf16[1,16,4,16,128]{4,3,2,1,0:T(8,128)(2,1)}, u32[]{:S(2)}) copy-start(bf16[1,16,4,16,128]{4,3,2,1,0:T(8,128)(2,1)} %param.3) | copy-start | bytes 786436
  1.8 6.1 %collective-permute-start = (bf16[16,2048]{1,0:T(8,128)(2,1)S(1)}, bf16[16,2048]{1,0:T(8,128)(2,1)S(1)}, u32[]{:S(2)}, u32[]{:S(2)}) collective-permute-start(bf16[16,2048]{1,0:T(8,128)(2,1)S(1)} %get-tuple-element.38), channel_id=1, source_target_pairs={{0,1},{1,0},{2,3},{3,2},{4,5},{5,4},{6,7},{7,6},{8,9},{9,8},{10,11... | collective-permute-start | bytes 196616 | tf_op jit(solution)/shard_map/ppermute | solution.py:306
  5.1 3.7 %collective-permute-start.1 = (bf16[16,2048]{1,0:T(8,128)(2,1)S(1)}, bf16[16,2048]{1,0:T(8,128)(2,1)S(1)}, u32[]{:S(2)}, u32[]{:S(2)}) collective-permute-start(bf16[16,2048]{1,0:T(8,128)(2,1)S(1)} %get-tuple-element.39), channel_id=1, source_target_pairs={{0,2},{1,3},{2,0},{3,1},{4,6},{5,7},{6,4},{7,5},{8,10},{9,11},{10,... | collective-permute-start | bytes 196616 | tf_op jit(solution)/shard_map/ppermute | solution.py:306
  5.1 5.2 %collective-permute-start.2 = (bf16[16,2048]{1,0:T(8,128)(2,1)S(1)}, bf16[16,2048]{1,0:T(8,128)(2,1)S(1)}, u32[]{:S(2)}, u32[]{:S(2)}) collective-permute-start(bf16[16,2048]{1,0:T(8,128)(2,1)S(1)} %get-tuple-element.40), channel_id=1, source_target_pairs={{0,3},{1,2},{2,1},{3,0},{4,7},{5,6},{6,5},{7,4},{8,11},{9,10},{10,... | collective-permute-start | bytes 196616 | tf_op jit(solution)/shard_map/ppermute | solution.py:306
  10.4 9.0 %collective-permute-start.4 = (bf16[64,2048]{1,0:T(8,128)(2,1)S(1)}, bf16[64,2048]{1,0:T(8,128)(2,1)S(1)}, u32[]{:S(2)}, u32[]{:S(2)}) collective-permute-start(bf16[64,2048]{1,0:T(8,128)(2,1)S(1)} %order.1.refs_0_), channel_id=1, source_target_pairs={{0,12},{4,8},{8,4},{12,0},{1,13},{5,9},{9,5},{13,1},{2,14},{6,10},... | collective-permute-start | bytes 786440 | tf_op jit(solution)/shard_map/ppermute | solution.py:306
  11.5 7.9 %collective-permute-start.3 = (bf16[64,2048]{1,0:T(8,128)(2,1)S(1)}, bf16[64,2048]{1,0:T(8,128)(2,1)S(1)}, u32[]{:S(2)}, u32[]{:S(2)}) collective-permute-start(bf16[64,2048]{1,0:T(8,128)(2,1)S(1)} %order.1.refs_0_), channel_id=1, source_target_pairs={{0,4},{4,0},{8,12},{12,8},{1,5},{5,1},{9,13},{13,9},{2,6},{6,2},{1... | collective-permute-start | bytes 786440 | tf_op jit(solution)/shard_map/ppermute | solution.py:306
  11.5 9.1 %collective-permute-start.9 = (bf16[432,256]{1,0:T(8,128)(2,1)S(1)}, bf16[432,256]{1,0:T(8,128)(2,1)S(1)}, u32[]{:S(2)}, u32[]{:S(2)}) collective-permute-start(bf16[432,256]{1,0:T(8,128)(2,1)S(1)} %get-tuple-element.41.refs_4_.refs_5_.refs_1_.refs_3_), channel_id=1, source_target_pairs={{0,3},{1,2},{2,1},{3,0},{4,7},{5,6},{6,5},{7,4},{8,11},{9,10},{10,... | collective-permute-start | bytes 663560 | tf_op jit(solution)/shard_map/ppermute | solution.py:306
  13.2 11.0 %collective-permute-start.8 = (bf16[432,256]{1,0:T(8,128)(2,1)S(1)}, bf16[432,256]{1,0:T(8,128)(2,1)S(1)}, u32[]{:S(2)}, u32[]{:S(2)}) collective-permute-start(bf16[432,256]{1,0:T(8,128)(2,1)S(1)} %get-tuple-element.41.refs_4_.refs_5_.refs_1_.refs_3_), channel_id=1, source_target_pairs={{0,2},{1,3},{2,0},{3,1},{4,6},{5,7},{6,4},{7,5},{8,10},{9,11},{10,... | collective-permute-start | bytes 663560 | tf_op jit(solution)/shard_map/ppermute | solution.py:306
  13.6 11.7 %collective-permute-start.7 = (bf16[432,256]{1,0:T(8,128)(2,1)S(1)}, bf16[432,256]{1,0:T(8,128)(2,1)S(1)}, u32[]{:S(2)}, u32[]{:S(2)}) collective-permute-start(bf16[432,256]{1,0:T(8,128)(2,1)S(1)} %get-tuple-element.41.refs_4_.refs_5_.refs_1_.refs_3_), channel_id=1, source_target_pairs={{0,1},{1,0},{2,3},{3,2},{4,5},{5,4},{6,7},{7,6},{8,9},{9,8},{10,11... | collective-permute-start | bytes 663560 | tf_op jit(solution)/shard_map/ppermute | solution.py:306
  19.4 6.8 %collective-permute-start.5 = (bf16[32,2048]{1,0:T(8,128)(2,1)S(1)}, bf16[32,2048]{1,0:T(8,128)(2,1)S(1)}, u32[]{:S(2)}, u32[]{:S(2)}) collective-permute-start(bf16[32,2048]{1,0:T(8,128)(2,1)S(1)} %get-tuple-element.42), channel_id=1, source_target_pairs={{0,12},{4,8},{8,4},{12,0},{1,13},{5,9},{9,5},{13,1},{2,14},{6,10},... | collective-permute-start | bytes 393224 | tf_op jit(solution)/shard_map/ppermute | solution.py:306
  20.6 5.6 %collective-permute-start.6 = (bf16[32,2048]{1,0:T(8,128)(2,1)S(1)}, bf16[32,2048]{1,0:T(8,128)(2,1)S(1)}, u32[]{:S(2)}, u32[]{:S(2)}) collective-permute-start(bf16[32,2048]{1,0:T(8,128)(2,1)S(1)} %get-tuple-element.43), channel_id=1, source_target_pairs={{0,4},{4,0},{8,12},{12,8},{1,5},{5,1},{9,13},{13,9},{2,6},{6,2},{1... | collective-permute-start | bytes 393224 | tf_op jit(solution)/shard_map/ppermute | solution.py:306
  20.6 6.6 %collective-permute-start.10 = (bf16[16,2048]{1,0:T(8,128)(2,1)S(1)}, bf16[16,2048]{1,0:T(8,128)(2,1)S(1)}, u32[]{:S(2)}, u32[]{:S(2)}) collective-permute-start(bf16[16,2048]{1,0:T(8,128)(2,1)S(1)} %get-tuple-element.45), channel_id=1, source_target_pairs={{0,1},{1,0},{2,3},{3,2},{4,5},{5,4},{6,7},{7,6},{8,9},{9,8},{10,11... | collective-permute-start | bytes 196616 | tf_op jit(solution)/shard_map/ppermute | solution.py:306
  24.2 3.1 %collective-permute-start.11 = (bf16[16,2048]{1,0:T(8,128)(2,1)S(1)}, bf16[16,2048]{1,0:T(8,128)(2,1)S(1)}, u32[]{:S(2)}, u32[]{:S(2)}) collective-permute-start(bf16[16,2048]{1,0:T(8,128)(2,1)S(1)} %get-tuple-element.46), channel_id=1, source_target_pairs={{0,2},{1,3},{2,0},{3,1},{4,6},{5,7},{6,4},{7,5},{8,10},{9,11},{10,... | collective-permute-start | bytes 196616 | tf_op jit(solution)/shard_map/ppermute | solution.py:306
  25.3 4.6 %collective-permute-start.12 = (bf16[16,2048]{1,0:T(8,128)(2,1)S(1)}, bf16[16,2048]{1,0:T(8,128)(2,1)S(1)}, u32[]{:S(2)}, u32[]{:S(2)}) collective-permute-start(bf16[16,2048]{1,0:T(8,128)(2,1)S(1)} %get-tuple-element.47), channel_id=1, source_target_pairs={{0,3},{1,2},{2,1},{3,0},{4,7},{5,6},{6,5},{7,4},{8,11},{9,10},{10,... | collective-permute-start | bytes 196616 | tf_op jit(solution)/shard_map/ppermute | solution.py:306
  30.9 4.2 %collective-permute-start.13 = (bf16[64,2048]{1,0:T(8,128)(2,1)S(1)}, bf16[64,2048]{1,0:T(8,128)(2,1)S(1)}, u32[]{:S(2)}, u32[]{:S(2)}) collective-permute-start(bf16[64,2048]{1,0:T(8,128)(2,1)S(1)} %before.1.refs_5_), channel_id=1, source_target_pairs={{2,240},{3,2},{1,3},{0,1},{16,0},{17,16},{19,17},{18,19},{34,18},{... | collective-permute-start | bytes 786440 | tf_op jit(solution)/shard_map/ppermute | solution.py:302
  31.7 5.5 %collective-permute-start.14 = (bf16[64,2048]{1,0:T(8,128)(2,1)S(1)}, bf16[64,2048]{1,0:T(8,128)(2,1)S(1)}, u32[]{:S(2)}, u32[]{:S(2)}) collective-permute-start(bf16[64,2048]{1,0:T(8,128)(2,1)S(1)} %get-tuple-element.48), channel_id=1, source_target_pairs={{2,3},{3,1},{1,0},{0,16},{16,17},{17,19},{19,18},{18,34},{34,35},{... | collective-permute-start | bytes 786440 | tf_op jit(solution)/shard_map/ppermute | solution.py:302
  37.6 6.3 %collective-permute-start.16 = (bf16[64,2048]{1,0:T(8,128)(2,1)S(1)}, bf16[64,2048]{1,0:T(8,128)(2,1)S(1)}, u32[]{:S(2)}, u32[]{:S(2)}) collective-permute-start(bf16[64,2048]{1,0:T(8,128)(2,1)S(1)} %get-tuple-element.50.refs_1_.refs_0_), channel_id=1, source_target_pairs={{2,240},{3,2},{1,3},{0,1},{16,0},{17,16},{19,17},{18,19},{34,18},{... | collective-permute-start | bytes 786440 | tf_op jit(solution)/shard_map/ppermute | solution.py:302
  40.6 11.2 %collective-permute-start.15 = (bf16[64,2048]{1,0:T(8,128)(2,1)S(1)}, bf16[64,2048]{1,0:T(8,128)(2,1)S(1)}, u32[]{:S(2)}, u32[]{:S(2)}) collective-permute-start(bf16[64,2048]{1,0:T(8,128)(2,1)S(1)} %get-tuple-element.50.refs_1_.refs_0_), channel_id=1, source_target_pairs={{2,3},{3,1},{1,0},{0,16},{16,17},{17,19},{19,18},{18,34},{34,35},{... | collective-permute-start | bytes 786440 | tf_op jit(solution)/shard_map/ppermute | solution.py:302
  54.8 3.7 %collective-permute-start.20 = (bf16[256,432]{1,0:T(8,128)(2,1)S(1)}, bf16[256,432]{1,0:T(8,128)(2,1)S(1)}, u32[]{:S(2)}, u32[]{:S(2)}) collective-permute-start(bf16[256,432]{1,0:T(8,128)(2,1)S(1)} %get-tuple-element.59), channel_id=1, source_target_pairs={{0,1},{1,0},{2,3},{3,2},{4,5},{5,4},{6,7},{7,6},{8,9},{9,8},{10,11... | collective-permute-start | bytes 663560 | tf_op jit(solution)/shard_map/ppermute | solution.py:306
  54.9 3.6 %collective-permute-start.21 = (bf16[256,432]{1,0:T(8,128)(2,1)S(1)}, bf16[256,432]{1,0:T(8,128)(2,1)S(1)}, u32[]{:S(2)}, u32[]{:S(2)}) collective-permute-start(bf16[256,432]{1,0:T(8,128)(2,1)S(1)} %get-tuple-element.60), channel_id=1, source_target_pairs={{0,1},{1,0},{2,3},{3,2},{4,5},{5,4},{6,7},{7,6},{8,9},{9,8},{10,11... | collective-permute-start | bytes 663560 | tf_op jit(solution)/shard_map/ppermute | solution.py:306
  58.5 10.9 %collective-permute-start.28 = (bf16[256,432]{1,0:T(8,128)(2,1)S(1)}, bf16[256,432]{1,0:T(8,128)(2,1)S(1)}, u32[]{:S(2)}, u32[]{:S(2)}) collective-permute-start(bf16[256,432]{1,0:T(8,128)(2,1)S(1)} %lift.1.refs_4_), channel_id=1, source_target_pairs={{0,2},{1,3},{2,0},{3,1},{4,6},{5,7},{6,4},{7,5},{8,10},{9,11},{10,... | collective-permute-start | bytes 663560 | tf_op jit(solution)/shard_map/ppermute | solution.py:306
  63.1 4.3 %collective-permute-start.17 = (bf16[32,2048]{1,0:T(8,128)(2,1)S(1)}, bf16[32,2048]{1,0:T(8,128)(2,1)S(1)}, u32[]{:S(2)}, u32[]{:S(2)}) collective-permute-start(bf16[32,2048]{1,0:T(8,128)(2,1)S(1)} %get-tuple-element.53), channel_id=1, source_target_pairs={{0,4},{4,0},{8,12},{12,8},{1,5},{5,1},{9,13},{13,9},{2,6},{6,2},{1... | collective-permute-start | bytes 393224 | tf_op jit(solution)/shard_map/ppermute | solution.py:306
  64.5 5.0 %collective-permute-start.24 = (bf16[32,2048]{1,0:T(8,128)(2,1)S(1)}, bf16[32,2048]{1,0:T(8,128)(2,1)S(1)}, u32[]{:S(2)}, u32[]{:S(2)}) collective-permute-start(bf16[32,2048]{1,0:T(8,128)(2,1)S(1)} %get-tuple-element.63), channel_id=1, source_target_pairs={{0,12},{4,8},{8,4},{12,0},{1,13},{5,9},{9,5},{13,1},{2,14},{6,10},... | collective-permute-start | bytes 393224 | tf_op jit(solution)/shard_map/ppermute | solution.py:306
  70.3 27.9 %all-to-all-start = ((bf16[16,16,432]{2,1,0:T(8,128)(2,1)}), bf16[16,16,432]{2,1,0:T(8,128)(2,1)S(1)}, u32[]{:S(2)}, u32[]{:S(2)}) async-start(bf16[16,16,432]{2,1,0:T(8,128)(2,1)} %bitcast.6), calls=%async_computation | async-start | bytes 524288 | tf_op jit(solution)/shard_map/all_to_all | solution.py:435
  73.8 5.1 %collective-permute-start.18 = (bf16[32,2048]{1,0:T(8,128)(2,1)S(1)}, bf16[32,2048]{1,0:T(8,128)(2,1)S(1)}, u32[]{:S(2)}, u32[]{:S(2)}) collective-permute-start(bf16[32,2048]{1,0:T(8,128)(2,1)S(1)} %get-tuple-element.56), channel_id=1, source_target_pairs={{0,12},{4,8},{8,4},{12,0},{1,13},{5,9},{9,5},{13,1},{2,14},{6,10},... | collective-permute-start | bytes 393224 | tf_op jit(solution)/shard_map/ppermute | solution.py:306
  74.4 4.5 %collective-permute-start.19 = (bf16[32,2048]{1,0:T(8,128)(2,1)S(1)}, bf16[32,2048]{1,0:T(8,128)(2,1)S(1)}, u32[]{:S(2)}, u32[]{:S(2)}) collective-permute-start(bf16[32,2048]{1,0:T(8,128)(2,1)S(1)} %get-tuple-element.57), channel_id=1, source_target_pairs={{0,4},{4,0},{8,12},{12,8},{1,5},{5,1},{9,13},{13,9},{2,6},{6,2},{1... | collective-permute-start | bytes 393224 | tf_op jit(solution)/shard_map/ppermute | solution.py:306
  79.0 4.4 %collective-permute-start.22 = (bf16[32,2048]{1,0:T(8,128)(2,1)S(1)}, bf16[32,2048]{1,0:T(8,128)(2,1)S(1)}, u32[]{:S(2)}, u32[]{:S(2)}) collective-permute-start(bf16[32,2048]{1,0:T(8,128)(2,1)S(1)} %get-tuple-element.61), channel_id=1, source_target_pairs={{0,4},{4,0},{8,12},{12,8},{1,5},{5,1},{9,13},{13,9},{2,6},{6,2},{1... | collective-permute-start | bytes 393224 | tf_op jit(solution)/shard_map/ppermute | solution.py:306
  79.8 5.3 %collective-permute-start.23 = (bf16[32,2048]{1,0:T(8,128)(2,1)S(1)}, bf16[32,2048]{1,0:T(8,128)(2,1)S(1)}, u32[]{:S(2)}, u32[]{:S(2)}) collective-permute-start(bf16[32,2048]{1,0:T(8,128)(2,1)S(1)} %get-tuple-element.62), channel_id=1, source_target_pairs={{0,12},{4,8},{8,4},{12,0},{1,13},{5,9},{9,5},{13,1},{2,14},{6,10},... | collective-permute-start | bytes 393224 | tf_op jit(solution)/shard_map/ppermute | solution.py:306
  85.3 5.6 %collective-permute-start.25 = (bf16[2,16,2048]{2,1,0:T(8,128)(2,1)S(1)}, bf16[2,16,2048]{2,1,0:T(8,128)(2,1)S(1)}, u32[]{:S(2)}, u32[]{:S(2)}) collective-permute-start(bf16[2,16,2048]{2,1,0:T(8,128)(2,1)S(1)} %get-tuple-element.66), channel_id=1, source_target_pairs={{0,1},{1,0},{2,3},{3,2},{4,5},{5,4},{6,7},{7,6},{8,9},{9,8},{10,11... | collective-permute-start | bytes 393224 | tf_op jit(solution)/shard_map/ppermute | solution.py:306
  89.1 5.1 %collective-permute-start.26 = (bf16[2,16,2048]{2,1,0:T(8,128)(2,1)S(1)}, bf16[2,16,2048]{2,1,0:T(8,128)(2,1)S(1)}, u32[]{:S(2)}, u32[]{:S(2)}) collective-permute-start(bf16[2,16,2048]{2,1,0:T(8,128)(2,1)S(1)} %get-tuple-element.67), channel_id=1, source_target_pairs={{0,2},{1,3},{2,0},{3,1},{4,6},{5,7},{6,4},{7,5},{8,10},{9,11},{10,... | collective-permute-start | bytes 393224 | tf_op jit(solution)/shard_map/ppermute | solution.py:306
  89.7 7.4 %collective-permute-start.27 = (bf16[2,16,2048]{2,1,0:T(8,128)(2,1)S(1)}, bf16[2,16,2048]{2,1,0:T(8,128)(2,1)S(1)}, u32[]{:S(2)}, u32[]{:S(2)}) collective-permute-start(bf16[2,16,2048]{2,1,0:T(8,128)(2,1)S(1)} %get-tuple-element.68), channel_id=1, source_target_pairs={{0,3},{1,2},{2,1},{3,0},{4,7},{5,6},{6,5},{7,4},{8,11},{9,10},{10,... | collective-permute-start | bytes 393224 | tf_op jit(solution)/shard_map/ppermute | solution.py:306
  (1 other events, 0.9 us)

commit v4 on v3

--- a/solution.py
+++ b/solution.py
@@ -430,7 +430,7 @@
         "merge",
         place,
         *(sums, sums_1, sums_2),
-        unread=[low_1, high_3],
+        unread=[low_1, high_1, low_3, high_3],
     )
     sums = lax.all_to_all(
         sums.reshape(spaces, in_total // spaces, taps),

time: 99.2 us -> 93.2 us (0.940)
  waiting for transfers between devices: 46.8 us -> 42.6 us
  starting transfers between devices: 37 us -> 35.3 us
    ppermute x25, waiting for transfers between devices: 31 us -> 26.8 us  [swap(): lax.ppermute(value, axis, [(i, i ^ j) for i in range(lax.axis_size(axis))])]
    ppermute x25, starting transfers between devices: 29.7 us -> 27.9 us  [swap(): lax.ppermute(value, axis, [(i, i ^ j) for i in range(lax.axis_size(axis))])]
  transfers between devices with their start and end apart: 30 -> 30, of which waited for: 17 -> 16; matrix products, arithmetic and copies ran while one was open for 0% -> 0% of each run, Pallas kernels for 6% -> 7%
where the time goes in v4:
time: 93.2 us; the launch traced here: 93 us
  waiting for transfers between devices  42.6 us (46%)
  starting transfers between devices  35.3 us (38%)
  Pallas kernels  12.4 us (13%)
  local copies, waits for them, and re-layouts  1.92 us (2%)
    ppermute x25, starting transfers between devices, swap(): lax.ppermute(value, axis, [(i, i ^ j) for i in range(lax.axis_size(axis))])  27.9 us
    ppermute x25, waiting for transfers between devices, swap(): lax.ppermute(value, axis, [(i, i ^ j) for i in range(lax.axis_size(axis))])  26.8 us
    ppermute x4, waiting for transfers between devices, shifted(): lax.ppermute(value, DEPTH, [(at[i], at[(i + by) % count]) for i in range(...  15.8 us
    pallas_call x16, Pallas kernels, call(): pl.pallas_call(run, in_specs=[pl.BlockSpec(memory_space=pltpu.SMEM)] + [p...  12.4 us
    ppermute x4, starting transfers between devices, shifted(): lax.ppermute(value, DEPTH, [(at[i], at[(i + by) % count]) for i in range(...  3.85 us
    all_to_all x1, starting transfers between devices, body(): lax.all_to_all(sums.reshape(spaces, in_total // spaces, taps), 'space', s...  3.53 us
    unnamed x6, local copies, waits for them, and re-layouts  1.92 us
  transfers between devices with their start and end apart: 30, of which 16 were waited for; matrix products, arithmetic and copies ran while one was open for 0% of the time, Pallas kernels for 7%

profile of v4, /device:TPU:1, one launch (start us, length us, event | category | flops | bytes accessed | tf_op | source)
XLA Modules:
  0.0 93.0 jit_solution(9698932924491254034)
XLA Ops:
  0.7 1.0 %copy-done.1 = bf16[1,16,4,16,128]{4,3,2,1,0:T(8,128)(2,1)S(1)} copy-done((bf16[1,16,4,16,128]{4,3,2,1,0:T(8,128)(2,1)S(1)}, bf16[1,16,4,16,128]{4,3,2,1,0:T(8,128)(2,1)}, u32[]{:S(2)}) %copy-start.1) | copy-done | bytes 262168
  1.8 3.3 %collective-permute-start = (bf16[16,2048]{1,0:T(8,128)(2,1)S(1)}, bf16[16,2048]{1,0:T(8,128)(2,1)S(1)}, u32[]{:S(2)}, u32[]{:S(2)}) collective-permute-start(bf16[16,2048]{1,0:T(8,128)(2,1)S(1)} %get-tuple-element.38), channel_id=1, source_target_pairs={{0,1},{1,0},{2,3},{3,2},{4,5},{5,4},{6,7},{7,6},{8,9},{9,8},{10,11... | collective-permute-start | bytes 196616 | tf_op jit(solution)/shard_map/ppermute | solution.py:306
  5.1 1.7 %collective-permute-start.2 = (bf16[16,2048]{1,0:T(8,128)(2,1)S(1)}, bf16[16,2048]{1,0:T(8,128)(2,1)S(1)}, u32[]{:S(2)}, u32[]{:S(2)}) collective-permute-start(bf16[16,2048]{1,0:T(8,128)(2,1)S(1)} %get-tuple-element.40), channel_id=1, source_target_pairs={{0,3},{1,2},{2,1},{3,0},{4,7},{5,6},{6,5},{7,4},{8,11},{9,10},{10,... | collective-permute-start | bytes 196616 | tf_op jit(solution)/shard_map/ppermute | solution.py:306
  6.8 0.9 %copy-done.2 = bf16[3,3,3,16,256]{4,3,2,1,0:T(8,128)(2,1)S(1)} copy-done((bf16[3,3,3,16,256]{4,3,2,1,0:T(8,128)(2,1)S(1)}, bf16[3,3,3,16,256]{4,3,2,1,0:T(8,128)(2,1)}, u32[]{:S(2)}) %copy-start.2) | copy-done | bytes 221208
  8.7 1.6 %collective-permute-done.2.refs_3_ = bf16[16,2048]{1,0:T(8,128)(2,1)S(1)} collective-permute-done((bf16[16,2048]{1,0:T(8,128)(2,1)S(1)}, bf16[16,2048]{1,0:T(8,128)(2,1)S(1)}, u32[]{:S(2)}, u32[]{:S(2)}) %collective-permute-start.2) | collective-permute-done | bytes 65568 | tf_op jit(solution)/shard_map/ppermute | solution.py:306
  10.4 1.1 %collective-permute-start.4 = (bf16[64,2048]{1,0:T(8,128)(2,1)S(1)}, bf16[64,2048]{1,0:T(8,128)(2,1)S(1)}, u32[]{:S(2)}, u32[]{:S(2)}) collective-permute-start(bf16[64,2048]{1,0:T(8,128)(2,1)S(1)} %order.1.refs_0_), channel_id=1, source_target_pairs={{0,12},{4,8},{8,4},{12,0},{1,13},{5,9},{9,5},{13,1},{2,14},{6,10},... | collective-permute-start | bytes 786440 | tf_op jit(solution)/shard_map/ppermute | solution.py:306
  11.5 1.7 %collective-permute-start.9 = (bf16[432,256]{1,0:T(8,128)(2,1)S(1)}, bf16[432,256]{1,0:T(8,128)(2,1)S(1)}, u32[]{:S(2)}, u32[]{:S(2)}) collective-permute-start(bf16[432,256]{1,0:T(8,128)(2,1)S(1)} %get-tuple-element.41.refs_4_.refs_5_.refs_1_.refs_3_), channel_id=1, source_target_pairs={{0,3},{1,2},{2,1},{3,0},{4,7},{5,6},{6,5},{7,4},{8,11},{9,10},{10,... | collective-permute-start | bytes 663560 | tf_op jit(solution)/shard_map/ppermute | solution.py:306
  13.6 5.7 %collective-permute-done.4.refs_1_.refs_2_ = bf16[64,2048]{1,0:T(8,128)(2,1)S(1)} collective-permute-done((bf16[64,2048]{1,0:T(8,128)(2,1)S(1)}, bf16[64,2048]{1,0:T(8,128)(2,1)S(1)}, u32[]{:S(2)}, u32[]{:S(2)}) %collective-permute-start.4) | collective-permute-done | bytes 262176 | tf_op jit(solution)/shard_map/ppermute | solution.py:306
  19.4 1.2 %collective-permute-start.5 = (bf16[32,2048]{1,0:T(8,128)(2,1)S(1)}, bf16[32,2048]{1,0:T(8,128)(2,1)S(1)}, u32[]{:S(2)}, u32[]{:S(2)}) collective-permute-start(bf16[32,2048]{1,0:T(8,128)(2,1)S(1)} %get-tuple-element.42), channel_id=1, source_target_pairs={{0,12},{4,8},{8,4},{12,0},{1,13},{5,9},{9,5},{13,1},{2,14},{6,10},... | collective-permute-start | bytes 393224 | tf_op jit(solution)/shard_map/ppermute | solution.py:306
  20.6 1.6 %collective-permute-start.10 = (bf16[16,2048]{1,0:T(8,128)(2,1)S(1)}, bf16[16,2048]{1,0:T(8,128)(2,1)S(1)}, u32[]{:S(2)}, u32[]{:S(2)}) collective-permute-start(bf16[16,2048]{1,0:T(8,128)(2,1)S(1)} %get-tuple-element.45), channel_id=1, source_target_pairs={{0,1},{1,0},{2,3},{3,2},{4,5},{5,4},{6,7},{7,6},{8,9},{9,8},{10,11... | collective-permute-start | bytes 196616 | tf_op jit(solution)/shard_map/ppermute | solution.py:306
  22.2 1.9 %collective-permute-done.8.refs_7_.refs_3_.refs_5_ = bf16[432,256]{1,0:T(8,128)(2,1)S(1)} collective-permute-done((bf16[432,256]{1,0:T(8,128)(2,1)S(1)}, bf16[432,256]{1,0:T(8,128)(2,1)S(1)}, u32[]{:S(2)}, u32[]{:S(2)}) %collective-permute-start.8) | collective-permute-done | bytes 221216 | tf_op jit(solution)/shard_map/ppermute | solution.py:306
  24.2 1.1 %collective-permute-start.11 = (bf16[16,2048]{1,0:T(8,128)(2,1)S(1)}, bf16[16,2048]{1,0:T(8,128)(2,1)S(1)}, u32[]{:S(2)}, u32[]{:S(2)}) collective-permute-start(bf16[16,2048]{1,0:T(8,128)(2,1)S(1)} %get-tuple-element.46), channel_id=1, source_target_pairs={{0,2},{1,3},{2,0},{3,1},{4,6},{5,7},{6,4},{7,5},{8,10},{9,11},{10,... | collective-permute-start | bytes 196616 | tf_op jit(solution)/shard_map/ppermute | solution.py:306
  26.2 1.0 %after.1 = (bf16[256,2048]{1,0:T(8,128)(2,1)S(1)}, bf16[64,2048]{1,0:T(8,128)(2,1)S(1)}) custom-call(s32[1]{0:T(128)} %bitcast.place_ref, bf16[64,2048]{1,0:T(8,128)(2,1)S(1)} %order.1.refs_0_, bf16[64,2048]{1,0:T(8,128)(2,1)S(1)} %collective-permute-done.3.refs_0_.refs_1_, bf16[64,2048]{1,0:T(8,128)(2,1)S(1)} %collective-permute-done.4.refs_1_.refs_2_, ...), custom_call_target="tpu_custom_call" | custom-call | flops 1 | bytes 1 | tf_op jit(solution)/shard_map/after/pallas_call | solution.py:81
  27.3 2.6 %collective-permute-done.12.refs_7_.refs_6_ = bf16[16,2048]{1,0:T(8,128)(2,1)S(1)} collective-permute-done((bf16[16,2048]{1,0:T(8,128)(2,1)S(1)}, bf16[16,2048]{1,0:T(8,128)(2,1)S(1)}, u32[]{:S(2)}, u32[]{:S(2)}) %collective-permute-start.12) | collective-permute-done | bytes 65568 | tf_op jit(solution)/shard_map/ppermute | solution.py:306
  32.7 2.4 %collective-permute-done.13.refs_1_ = bf16[64,2048]{1,0:T(8,128)(2,1)S(1)} collective-permute-done((bf16[64,2048]{1,0:T(8,128)(2,1)S(1)}, bf16[64,2048]{1,0:T(8,128)(2,1)S(1)}, u32[]{:S(2)}, u32[]{:S(2)}) %collective-permute-start.13) | collective-permute-done | bytes 262176 | tf_op jit(solution)/shard_map/ppermute | solution.py:302
  35.0 2.2 %collective-permute-done.14.refs_2_ = bf16[64,2048]{1,0:T(8,128)(2,1)S(1)} collective-permute-done((bf16[64,2048]{1,0:T(8,128)(2,1)S(1)}, bf16[64,2048]{1,0:T(8,128)(2,1)S(1)}, u32[]{:S(2)}, u32[]{:S(2)}) %collective-permute-start.14) | collective-permute-done | bytes 262176 | tf_op jit(solution)/shard_map/ppermute | solution.py:302
  37.6 3.0 %collective-permute-start.16 = (bf16[64,2048]{1,0:T(8,128)(2,1)S(1)}, bf16[64,2048]{1,0:T(8,128)(2,1)S(1)}, u32[]{:S(2)}, u32[]{:S(2)}) collective-permute-start(bf16[64,2048]{1,0:T(8,128)(2,1)S(1)} %get-tuple-element.50.refs_1_.refs_0_), channel_id=1, source_target_pairs={{2,240},{3,2},{1,3},{0,1},{16,0},{17,16},{19,17},{18,19},{34,18},{... | collective-permute-start | bytes 786440 | tf_op jit(solution)/shard_map/ppermute | solution.py:302
  40.6 3.3 %collective-permute-done.16.refs_3_.refs_2_ = bf16[64,2048]{1,0:T(8,128)(2,1)S(1)} collective-permute-done((bf16[64,2048]{1,0:T(8,128)(2,1)S(1)}, bf16[64,2048]{1,0:T(8,128)(2,1)S(1)}, u32[]{:S(2)}, u32[]{:S(2)}) %collective-permute-start.16) | collective-permute-done | bytes 262176 | tf_op jit(solution)/shard_map/ppermute | solution.py:302
  43.9 7.9 %collective-permute-done.15.refs_2_.refs_1_ = bf16[64,2048]{1,0:T(8,128)(2,1)S(1)} collective-permute-done((bf16[64,2048]{1,0:T(8,128)(2,1)S(1)}, bf16[64,2048]{1,0:T(8,128)(2,1)S(1)}, u32[]{:S(2)}, u32[]{:S(2)}) %collective-permute-start.15) | collective-permute-done | bytes 262176 | tf_op jit(solution)/shard_map/ppermute | solution.py:302
  51.8 3.0 %filter_sums.1 = (bf16[256,432]{1,0:T(8,128)(2,1)S(1)}, bf16[256,432]{1,0:T(8,128)(2,1)S(1)}, bf16[256,432]{1,0:T(8,128)(2,1)S(1)}, bf16[256,432]{1,0:T(8,128)(2,1)S(1)}) custom-call(s32[1]{0:T(128)} %bitcast.place_ref, bf16[256,2048]{1,0:T(8,128)(2,1)S(1)} %get-tuple-element.44.refs_0_, bf16[64,2048]{1,0:T(8,128)(2,1)S(1)} %get-tuple-element.50.refs_1_.refs_0_, ...), custom_call_target="tpu_custom_call" | custom-call | flops 1 | bytes 1 | tf_op jit(solution)/shard_map/filter_sums/pallas_call | solution.py:81
  55.3 3.1 %input_sums.1 = (f32[64,2048]{1,0:T(8,128)S(1)}, bf16[32,2048]{1,0:T(8,128)(2,1)S(1)}, bf16[32,2048]{1,0:T(8,128)(2,1)S(1)}, bf16[32,2048]{1,0:T(8,128)(2,1)S(1)...) custom-call(s32[1]{0:T(128)} %bitcast.place_ref, ...), custom_call_target="tpu_custom_call" | custom-call | flops 1 | bytes 1 | tf_op jit(solution)/shard_map/input_sums/pallas_call | solution.py:81
  60.1 4.5 %collective-permute-start.28 = (bf16[256,432]{1,0:T(8,128)(2,1)S(1)}, bf16[256,432]{1,0:T(8,128)(2,1)S(1)}, u32[]{:S(2)}, u32[]{:S(2)}) collective-permute-start(bf16[256,432]{1,0:T(8,128)(2,1)S(1)} %lift.1.refs_4_), channel_id=1, source_target_pairs={{0,2},{1,3},{2,0},{3,1},{4,6},{5,7},{6,4},{7,5},{8,10},{9,11},{10,... | collective-permute-start | bytes 663560 | tf_op jit(solution)/shard_map/ppermute | solution.py:306
  65.2 2.0 %collective-permute-start.24 = (bf16[32,2048]{1,0:T(8,128)(2,1)S(1)}, bf16[32,2048]{1,0:T(8,128)(2,1)S(1)}, u32[]{:S(2)}, u32[]{:S(2)}) collective-permute-start(bf16[32,2048]{1,0:T(8,128)(2,1)S(1)} %get-tuple-element.63), channel_id=1, source_target_pairs={{0,12},{4,8},{8,4},{12,0},{1,13},{5,9},{9,5},{13,1},{2,14},{6,10},... | collective-permute-start | bytes 393224 | tf_op jit(solution)/shard_map/ppermute | solution.py:306
  68.7 1.5 %collective-permute-done.24.refs_4_.refs_6_ = bf16[32,2048]{1,0:T(8,128)(2,1)S(1)} collective-permute-done((bf16[32,2048]{1,0:T(8,128)(2,1)S(1)}, bf16[32,2048]{1,0:T(8,128)(2,1)S(1)}, u32[]{:S(2)}, u32[]{:S(2)}) %collective-permute-start.24) | collective-permute-done | bytes 131104 | tf_op jit(solution)/shard_map/ppermute | solution.py:306
  70.2 1.3 %collective-permute-done.22.refs_2_.refs_4_ = bf16[32,2048]{1,0:T(8,128)(2,1)S(1)} collective-permute-done((bf16[32,2048]{1,0:T(8,128)(2,1)S(1)}, bf16[32,2048]{1,0:T(8,128)(2,1)S(1)}, u32[]{:S(2)}, u32[]{:S(2)}) %collective-permute-start.22) | collective-permute-done | bytes 131104 | tf_op jit(solution)/shard_map/ppermute | solution.py:306
  71.6 2.1 %collective-permute-done.23.refs_3_.refs_5_ = bf16[32,2048]{1,0:T(8,128)(2,1)S(1)} collective-permute-done((bf16[32,2048]{1,0:T(8,128)(2,1)S(1)}, bf16[32,2048]{1,0:T(8,128)(2,1)S(1)}, u32[]{:S(2)}, u32[]{:S(2)}) %collective-permute-start.23) | collective-permute-done | bytes 131104 | tf_op jit(solution)/shard_map/ppermute | solution.py:306
  74.4 3.5 %all-to-all-start = ((bf16[16,16,432]{2,1,0:T(8,128)(2,1)}), bf16[16,16,432]{2,1,0:T(8,128)(2,1)S(1)}, u32[]{:S(2)}, u32[]{:S(2)}) async-start(bf16[16,16,432]{2,1,0:T(8,128)(2,1)} %bitcast.6), calls=%async_computation | async-start | bytes 524288 | tf_op jit(solution)/shard_map/all_to_all | solution.py:435
  78.1 2.4 %collective-permute-start.25 = (bf16[2,16,2048]{2,1,0:T(8,128)(2,1)S(1)}, bf16[2,16,2048]{2,1,0:T(8,128)(2,1)S(1)}, u32[]{:S(2)}, u32[]{:S(2)}) collective-permute-start(bf16[2,16,2048]{2,1,0:T(8,128)(2,1)S(1)} %get-tuple-element.66), channel_id=1, source_target_pairs={{0,1},{1,0},{2,3},{3,2},{4,5},{5,4},{6,7},{7,6},{8,9},{9,8},{10,11... | collective-permute-start | bytes 393224 | tf_op jit(solution)/shard_map/ppermute | solution.py:306
  80.6 1.8 %collective-permute-start.26 = (bf16[2,16,2048]{2,1,0:T(8,128)(2,1)S(1)}, bf16[2,16,2048]{2,1,0:T(8,128)(2,1)S(1)}, u32[]{:S(2)}, u32[]{:S(2)}) collective-permute-start(bf16[2,16,2048]{2,1,0:T(8,128)(2,1)S(1)} %get-tuple-element.67), channel_id=1, source_target_pairs={{0,2},{1,3},{2,0},{3,1},{4,6},{5,7},{6,4},{7,5},{8,10},{9,11},{10,... | collective-permute-start | bytes 393224 | tf_op jit(solution)/shard_map/ppermute | solution.py:306
  82.5 5.1 %collective-permute-done.26.refs_2_ = bf16[2,16,2048]{2,1,0:T(8,128)(2,1)S(1)} collective-permute-done((bf16[2,16,2048]{2,1,0:T(8,128)(2,1)S(1)}, bf16[2,16,2048]{2,1,0:T(8,128)(2,1)S(1)}, u32[]{:S(2)}, u32[]{:S(2)}) %collective-permute-start.26) | collective-permute-done | bytes 131104 | tf_op jit(solution)/shard_map/ppermute | solution.py:306
  87.6 3.5 %collective-permute-done.27.refs_3_ = bf16[2,16,2048]{2,1,0:T(8,128)(2,1)S(1)} collective-permute-done((bf16[2,16,2048]{2,1,0:T(8,128)(2,1)S(1)}, bf16[2,16,2048]{2,1,0:T(8,128)(2,1)S(1)}, u32[]{:S(2)}, u32[]{:S(2)}) %collective-permute-start.27) | collective-permute-done | bytes 131104 | tf_op jit(solution)/shard_map/ppermute | solution.py:306
  91.1 1.0 %close.1 = (bf16[16,4,16,128]{3,2,1,0:T(8,128)(2,1)}, bf16[16,4,16,128]{3,2,1,0:T(8,128)(2,1)}) custom-call(s32[1]{0:T(128)} %bitcast.place_ref, bf16[2,16,2048]{2,1,0:T(8,128)(2,1)S(1)} %get-tuple-element.65.refs_0_, bf16[2,16,2048]{2,1,0:T(8,128)(2,1)S(1)} %collective-permute-done.25.refs_1_, bf16[2,16,2048]{2,1,0:T(8,128)(2,1)S(1)} %collective-permute-done.26.refs_2_, ...), custom_call_target="tpu_custom_call" | custom-call | flops 1 | bytes 1 | tf_op jit(solution)/shard_map/close/pallas_call | solution.py:81
  (50 shorter events, 11.8 us)
Async XLA Ops:
  0.6 6.2 %copy-start = (bf16[1,16,4,16,128]{4,3,2,1,0:T(8,128)(2,1)S(1)}, bf16[1,16,4,16,128]{4,3,2,1,0:T(8,128)(2,1)}, u32[]{:S(2)}) copy-start(bf16[1,16,4,16,128]{4,3,2,1,0:T(8,128)(2,1)} %param.5) | copy-start | bytes 786436
  0.6 1.0 %copy-start.1 = (bf16[1,16,4,16,128]{4,3,2,1,0:T(8,128)(2,1)S(1)}, bf16[1,16,4,16,128]{4,3,2,1,0:T(8,128)(2,1)}, u32[]{:S(2)}) copy-start(bf16[1,16,4,16,128]{4,3,2,1,0:T(8,128)(2,1)} %param.3) | copy-start | bytes 786436
  1.8 6.1 %collective-permute-start = (bf16[16,2048]{1,0:T(8,128)(2,1)S(1)}, bf16[16,2048]{1,0:T(8,128)(2,1)S(1)}, u32[]{:S(2)}, u32[]{:S(2)}) collective-permute-start(bf16[16,2048]{1,0:T(8,128)(2,1)S(1)} %get-tuple-element.38), channel_id=1, source_target_pairs={{0,1},{1,0},{2,3},{3,2},{4,5},{5,4},{6,7},{7,6},{8,9},{9,8},{10,11... | collective-permute-start | bytes 196616 | tf_op jit(solution)/shard_map/ppermute | solution.py:306
  5.1 3.7 %collective-permute-start.1 = (bf16[16,2048]{1,0:T(8,128)(2,1)S(1)}, bf16[16,2048]{1,0:T(8,128)(2,1)S(1)}, u32[]{:S(2)}, u32[]{:S(2)}) collective-permute-start(bf16[16,2048]{1,0:T(8,128)(2,1)S(1)} %get-tuple-element.39), channel_id=1, source_target_pairs={{0,2},{1,3},{2,0},{3,1},{4,6},{5,7},{6,4},{7,5},{8,10},{9,11},{10,... | collective-permute-start | bytes 196616 | tf_op jit(solution)/shard_map/ppermute | solution.py:306
  5.1 5.2 %collective-permute-start.2 = (bf16[16,2048]{1,0:T(8,128)(2,1)S(1)}, bf16[16,2048]{1,0:T(8,128)(2,1)S(1)}, u32[]{:S(2)}, u32[]{:S(2)}) collective-permute-start(bf16[16,2048]{1,0:T(8,128)(2,1)S(1)} %get-tuple-element.40), channel_id=1, source_target_pairs={{0,3},{1,2},{2,1},{3,0},{4,7},{5,6},{6,5},{7,4},{8,11},{9,10},{10,... | collective-permute-start | bytes 196616 | tf_op jit(solution)/shard_map/ppermute | solution.py:306
  10.4 9.0 %collective-permute-start.4 = (bf16[64,2048]{1,0:T(8,128)(2,1)S(1)}, bf16[64,2048]{1,0:T(8,128)(2,1)S(1)}, u32[]{:S(2)}, u32[]{:S(2)}) collective-permute-start(bf16[64,2048]{1,0:T(8,128)(2,1)S(1)} %order.1.refs_0_), channel_id=1, source_target_pairs={{0,12},{4,8},{8,4},{12,0},{1,13},{5,9},{9,5},{13,1},{2,14},{6,10},... | collective-permute-start | bytes 786440 | tf_op jit(solution)/shard_map/ppermute | solution.py:306
  11.5 7.9 %collective-permute-start.3 = (bf16[64,2048]{1,0:T(8,128)(2,1)S(1)}, bf16[64,2048]{1,0:T(8,128)(2,1)S(1)}, u32[]{:S(2)}, u32[]{:S(2)}) collective-permute-start(bf16[64,2048]{1,0:T(8,128)(2,1)S(1)} %order.1.refs_0_), channel_id=1, source_target_pairs={{0,4},{4,0},{8,12},{12,8},{1,5},{5,1},{9,13},{13,9},{2,6},{6,2},{1... | collective-permute-start | bytes 786440 | tf_op jit(solution)/shard_map/ppermute | solution.py:306
  11.5 9.1 %collective-permute-start.9 = (bf16[432,256]{1,0:T(8,128)(2,1)S(1)}, bf16[432,256]{1,0:T(8,128)(2,1)S(1)}, u32[]{:S(2)}, u32[]{:S(2)}) collective-permute-start(bf16[432,256]{1,0:T(8,128)(2,1)S(1)} %get-tuple-element.41.refs_4_.refs_5_.refs_1_.refs_3_), channel_id=1, source_target_pairs={{0,3},{1,2},{2,1},{3,0},{4,7},{5,6},{6,5},{7,4},{8,11},{9,10},{10,... | collective-permute-start | bytes 663560 | tf_op jit(solution)/shard_map/ppermute | solution.py:306
  13.2 11.0 %collective-permute-start.8 = (bf16[432,256]{1,0:T(8,128)(2,1)S(1)}, bf16[432,256]{1,0:T(8,128)(2,1)S(1)}, u32[]{:S(2)}, u32[]{:S(2)}) collective-permute-start(bf16[432,256]{1,0:T(8,128)(2,1)S(1)} %get-tuple-element.41.refs_4_.refs_5_.refs_1_.refs_3_), channel_id=1, source_target_pairs={{0,2},{1,3},{2,0},{3,1},{4,6},{5,7},{6,4},{7,5},{8,10},{9,11},{10,... | collective-permute-start | bytes 663560 | tf_op jit(solution)/shard_map/ppermute | solution.py:306
  13.6 11.7 %collective-permute-start.7 = (bf16[432,256]{1,0:T(8,128)(2,1)S(1)}, bf16[432,256]{1,0:T(8,128)(2,1)S(1)}, u32[]{:S(2)}, u32[]{:S(2)}) collective-permute-start(bf16[432,256]{1,0:T(8,128)(2,1)S(1)} %get-tuple-element.41.refs_4_.refs_5_.refs_1_.refs_3_), channel_id=1, source_target_pairs={{0,1},{1,0},{2,3},{3,2},{4,5},{5,4},{6,7},{7,6},{8,9},{9,8},{10,11... | collective-permute-start | bytes 663560 | tf_op jit(solution)/shard_map/ppermute | solution.py:306
  19.4 6.8 %collective-permute-start.5 = (bf16[32,2048]{1,0:T(8,128)(2,1)S(1)}, bf16[32,2048]{1,0:T(8,128)(2,1)S(1)}, u32[]{:S(2)}, u32[]{:S(2)}) collective-permute-start(bf16[32,2048]{1,0:T(8,128)(2,1)S(1)} %get-tuple-element.42), channel_id=1, source_target_pairs={{0,12},{4,8},{8,4},{12,0},{1,13},{5,9},{9,5},{13,1},{2,14},{6,10},... | collective-permute-start | bytes 393224 | tf_op jit(solution)/shard_map/ppermute | solution.py:306
  20.6 5.6 %collective-permute-start.6 = (bf16[32,2048]{1,0:T(8,128)(2,1)S(1)}, bf16[32,2048]{1,0:T(8,128)(2,1)S(1)}, u32[]{:S(2)}, u32[]{:S(2)}) collective-permute-start(bf16[32,2048]{1,0:T(8,128)(2,1)S(1)} %get-tuple-element.43), channel_id=1, source_target_pairs={{0,4},{4,0},{8,12},{12,8},{1,5},{5,1},{9,13},{13,9},{2,6},{6,2},{1... | collective-permute-start | bytes 393224 | tf_op jit(solution)/shard_map/ppermute | solution.py:306
  20.6 6.6 %collective-permute-start.10 = (bf16[16,2048]{1,0:T(8,128)(2,1)S(1)}, bf16[16,2048]{1,0:T(8,128)(2,1)S(1)}, u32[]{:S(2)}, u32[]{:S(2)}) collective-permute-start(bf16[16,2048]{1,0:T(8,128)(2,1)S(1)} %get-tuple-element.45), channel_id=1, source_target_pairs={{0,1},{1,0},{2,3},{3,2},{4,5},{5,4},{6,7},{7,6},{8,9},{9,8},{10,11... | collective-permute-start | bytes 196616 | tf_op jit(solution)/shard_map/ppermute | solution.py:306
  24.2 3.1 %collective-permute-start.11 = (bf16[16,2048]{1,0:T(8,128)(2,1)S(1)}, bf16[16,2048]{1,0:T(8,128)(2,1)S(1)}, u32[]{:S(2)}, u32[]{:S(2)}) collective-permute-start(bf16[16,2048]{1,0:T(8,128)(2,1)S(1)} %get-tuple-element.46), channel_id=1, source_target_pairs={{0,2},{1,3},{2,0},{3,1},{4,6},{5,7},{6,4},{7,5},{8,10},{9,11},{10,... | collective-permute-start | bytes 196616 | tf_op jit(solution)/shard_map/ppermute | solution.py:306
  25.3 4.6 %collective-permute-start.12 = (bf16[16,2048]{1,0:T(8,128)(2,1)S(1)}, bf16[16,2048]{1,0:T(8,128)(2,1)S(1)}, u32[]{:S(2)}, u32[]{:S(2)}) collective-permute-start(bf16[16,2048]{1,0:T(8,128)(2,1)S(1)} %get-tuple-element.47), channel_id=1, source_target_pairs={{0,3},{1,2},{2,1},{3,0},{4,7},{5,6},{6,5},{7,4},{8,11},{9,10},{10,... | collective-permute-start | bytes 196616 | tf_op jit(solution)/shard_map/ppermute | solution.py:306
  30.9 4.2 %collective-permute-start.13 = (bf16[64,2048]{1,0:T(8,128)(2,1)S(1)}, bf16[64,2048]{1,0:T(8,128)(2,1)S(1)}, u32[]{:S(2)}, u32[]{:S(2)}) collective-permute-start(bf16[64,2048]{1,0:T(8,128)(2,1)S(1)} %before.1.refs_5_), channel_id=1, source_target_pairs={{2,240},{3,2},{1,3},{0,1},{16,0},{17,16},{19,17},{18,19},{34,18},{... | collective-permute-start | bytes 786440 | tf_op jit(solution)/shard_map/ppermute | solution.py:302
  31.7 5.5 %collective-permute-start.14 = (bf16[64,2048]{1,0:T(8,128)(2,1)S(1)}, bf16[64,2048]{1,0:T(8,128)(2,1)S(1)}, u32[]{:S(2)}, u32[]{:S(2)}) collective-permute-start(bf16[64,2048]{1,0:T(8,128)(2,1)S(1)} %get-tuple-element.48), channel_id=1, source_target_pairs={{2,3},{3,1},{1,0},{0,16},{16,17},{17,19},{19,18},{18,34},{34,35},{... | collective-permute-start | bytes 786440 | tf_op jit(solution)/shard_map/ppermute | solution.py:302
  37.6 6.3 %collective-permute-start.16 = (bf16[64,2048]{1,0:T(8,128)(2,1)S(1)}, bf16[64,2048]{1,0:T(8,128)(2,1)S(1)}, u32[]{:S(2)}, u32[]{:S(2)}) collective-permute-start(bf16[64,2048]{1,0:T(8,128)(2,1)S(1)} %get-tuple-element.50.refs_1_.refs_0_), channel_id=1, source_target_pairs={{2,240},{3,2},{1,3},{0,1},{16,0},{17,16},{19,17},{18,19},{34,18},{... | collective-permute-start | bytes 786440 | tf_op jit(solution)/shard_map/ppermute | solution.py:302
  40.6 11.2 %collective-permute-start.15 = (bf16[64,2048]{1,0:T(8,128)(2,1)S(1)}, bf16[64,2048]{1,0:T(8,128)(2,1)S(1)}, u32[]{:S(2)}, u32[]{:S(2)}) collective-permute-start(bf16[64,2048]{1,0:T(8,128)(2,1)S(1)} %get-tuple-element.50.refs_1_.refs_0_), channel_id=1, source_target_pairs={{2,3},{3,1},{1,0},{0,16},{16,17},{17,19},{19,18},{18,34},{34,35},{... | collective-permute-start | bytes 786440 | tf_op jit(solution)/shard_map/ppermute | solution.py:302
  54.8 5.3 %collective-permute-start.20 = (bf16[256,432]{1,0:T(8,128)(2,1)S(1)}, bf16[256,432]{1,0:T(8,128)(2,1)S(1)}, u32[]{:S(2)}, u32[]{:S(2)}) collective-permute-start(bf16[256,432]{1,0:T(8,128)(2,1)S(1)} %get-tuple-element.59), channel_id=1, source_target_pairs={{0,1},{1,0},{2,3},{3,2},{4,5},{5,4},{6,7},{7,6},{8,9},{9,8},{10,11... | collective-permute-start | bytes 663560 | tf_op jit(solution)/shard_map/ppermute | solution.py:306
  54.9 5.2 %collective-permute-start.21 = (bf16[256,432]{1,0:T(8,128)(2,1)S(1)}, bf16[256,432]{1,0:T(8,128)(2,1)S(1)}, u32[]{:S(2)}, u32[]{:S(2)}) collective-permute-start(bf16[256,432]{1,0:T(8,128)(2,1)S(1)} %get-tuple-element.60), channel_id=1, source_target_pairs={{0,1},{1,0},{2,3},{3,2},{4,5},{5,4},{6,7},{7,6},{8,9},{9,8},{10,11... | collective-permute-start | bytes 663560 | tf_op jit(solution)/shard_map/ppermute | solution.py:306
  58.5 8.8 %collective-permute-start.18 = (bf16[32,2048]{1,0:T(8,128)(2,1)S(1)}, bf16[32,2048]{1,0:T(8,128)(2,1)S(1)}, u32[]{:S(2)}, u32[]{:S(2)}) collective-permute-start(bf16[32,2048]{1,0:T(8,128)(2,1)S(1)} %get-tuple-element.56), channel_id=1, source_target_pairs={{0,12},{4,8},{8,4},{12,0},{1,13},{5,9},{9,5},{13,1},{2,14},{6,10},... | collective-permute-start | bytes 393224 | tf_op jit(solution)/shard_map/ppermute | solution.py:306
  59.2 8.1 %collective-permute-start.19 = (bf16[32,2048]{1,0:T(8,128)(2,1)S(1)}, bf16[32,2048]{1,0:T(8,128)(2,1)S(1)}, u32[]{:S(2)}, u32[]{:S(2)}) collective-permute-start(bf16[32,2048]{1,0:T(8,128)(2,1)S(1)} %get-tuple-element.57), channel_id=1, source_target_pairs={{0,4},{4,0},{8,12},{12,8},{1,5},{5,1},{9,13},{13,9},{2,6},{6,2},{1... | collective-permute-start | bytes 393224 | tf_op jit(solution)/shard_map/ppermute | solution.py:306
  60.1 13.5 %collective-permute-start.28 = (bf16[256,432]{1,0:T(8,128)(2,1)S(1)}, bf16[256,432]{1,0:T(8,128)(2,1)S(1)}, u32[]{:S(2)}, u32[]{:S(2)}) collective-permute-start(bf16[256,432]{1,0:T(8,128)(2,1)S(1)} %lift.1.refs_4_), channel_id=1, source_target_pairs={{0,2},{1,3},{2,0},{3,1},{4,6},{5,7},{6,4},{7,5},{8,10},{9,11},{10,... | collective-permute-start | bytes 663560 | tf_op jit(solution)/shard_map/ppermute | solution.py:306
  64.6 4.1 %collective-permute-start.17 = (bf16[32,2048]{1,0:T(8,128)(2,1)S(1)}, bf16[32,2048]{1,0:T(8,128)(2,1)S(1)}, u32[]{:S(2)}, u32[]{:S(2)}) collective-permute-start(bf16[32,2048]{1,0:T(8,128)(2,1)S(1)} %get-tuple-element.53), channel_id=1, source_target_pairs={{0,4},{4,0},{8,12},{12,8},{1,5},{5,1},{9,13},{13,9},{2,6},{6,2},{1... | collective-permute-start | bytes 393224 | tf_op jit(solution)/shard_map/ppermute | solution.py:306
  65.2 5.0 %collective-permute-start.24 = (bf16[32,2048]{1,0:T(8,128)(2,1)S(1)}, bf16[32,2048]{1,0:T(8,128)(2,1)S(1)}, u32[]{:S(2)}, u32[]{:S(2)}) collective-permute-start(bf16[32,2048]{1,0:T(8,128)(2,1)S(1)} %get-tuple-element.63), channel_id=1, source_target_pairs={{0,12},{4,8},{8,4},{12,0},{1,13},{5,9},{9,5},{13,1},{2,14},{6,10},... | collective-permute-start | bytes 393224 | tf_op jit(solution)/shard_map/ppermute | solution.py:306
  67.3 4.2 %collective-permute-start.22 = (bf16[32,2048]{1,0:T(8,128)(2,1)S(1)}, bf16[32,2048]{1,0:T(8,128)(2,1)S(1)}, u32[]{:S(2)}, u32[]{:S(2)}) collective-permute-start(bf16[32,2048]{1,0:T(8,128)(2,1)S(1)} %get-tuple-element.61), channel_id=1, source_target_pairs={{0,4},{4,0},{8,12},{12,8},{1,5},{5,1},{9,13},{13,9},{2,6},{6,2},{1... | collective-permute-start | bytes 393224 | tf_op jit(solution)/shard_map/ppermute | solution.py:306
  67.6 6.0 %collective-permute-start.23 = (bf16[32,2048]{1,0:T(8,128)(2,1)S(1)}, bf16[32,2048]{1,0:T(8,128)(2,1)S(1)}, u32[]{:S(2)}, u32[]{:S(2)}) collective-permute-start(bf16[32,2048]{1,0:T(8,128)(2,1)S(1)} %get-tuple-element.62), channel_id=1, source_target_pairs={{0,12},{4,8},{8,4},{12,0},{1,13},{5,9},{9,5},{13,1},{2,14},{6,10},... | collective-permute-start | bytes 393224 | tf_op jit(solution)/shard_map/ppermute | solution.py:306
  74.4 17.7 %all-to-all-start = ((bf16[16,16,432]{2,1,0:T(8,128)(2,1)}), bf16[16,16,432]{2,1,0:T(8,128)(2,1)S(1)}, u32[]{:S(2)}, u32[]{:S(2)}) async-start(bf16[16,16,432]{2,1,0:T(8,128)(2,1)} %bitcast.6), calls=%async_computation | async-start | bytes 524288 | tf_op jit(solution)/shard_map/all_to_all | solution.py:435
  78.1 4.3 %collective-permute-start.25 = (bf16[2,16,2048]{2,1,0:T(8,128)(2,1)S(1)}, bf16[2,16,2048]{2,1,0:T(8,128)(2,1)S(1)}, u32[]{:S(2)}, u32[]{:S(2)}) collective-permute-start(bf16[2,16,2048]{2,1,0:T(8,128)(2,1)S(1)} %get-tuple-element.66), channel_id=1, source_target_pairs={{0,1},{1,0},{2,3},{3,2},{4,5},{5,4},{6,7},{7,6},{8,9},{9,8},{10,11... | collective-permute-start | bytes 393224 | tf_op jit(solution)/shard_map/ppermute | solution.py:306
  80.6 7.1 %collective-permute-start.26 = (bf16[2,16,2048]{2,1,0:T(8,128)(2,1)S(1)}, bf16[2,16,2048]{2,1,0:T(8,128)(2,1)S(1)}, u32[]{:S(2)}, u32[]{:S(2)}) collective-permute-start(bf16[2,16,2048]{2,1,0:T(8,128)(2,1)S(1)} %get-tuple-element.67), channel_id=1, source_target_pairs={{0,2},{1,3},{2,0},{3,1},{4,6},{5,7},{6,4},{7,5},{8,10},{9,11},{10,... | collective-permute-start | bytes 393224 | tf_op jit(solution)/shard_map/ppermute | solution.py:306
  82.4 8.7 %collective-permute-start.27 = (bf16[2,16,2048]{2,1,0:T(8,128)(2,1)S(1)}, bf16[2,16,2048]{2,1,0:T(8,128)(2,1)S(1)}, u32[]{:S(2)}, u32[]{:S(2)}) collective-permute-start(bf16[2,16,2048]{2,1,0:T(8,128)(2,1)S(1)} %get-tuple-element.68), channel_id=1, source_target_pairs={{0,3},{1,2},{2,1},{3,0},{4,7},{5,6},{6,5},{7,4},{8,11},{9,10},{10,... | collective-permute-start | bytes 393224 | tf_op jit(solution)/shard_map/ppermute | solution.py:306
  (1 other events, 0.9 us)

commit v5 on v4

--- a/solution.py
+++ b/solution.py
@@ -167,29 +167,30 @@
         ).astype(grad_ref.dtype)
 
 
-def fill_moved(place_ref, moved_ref, grad_ref, low_ref, high_ref, last):
-    plane = grad_ref.shape[1]
-    stride = plane + 2 * BREADTH
-    gap = jnp.zeros((grad_ref.shape[0], BREADTH), moved_ref.dtype)
-    for p, ref in enumerate((low_ref, grad_ref, high_ref)):
-        source = ref[...].astype(jnp.float32)
-        if p != 1:
-            source = unless(at_end(place_ref, last if p else None), source)
-        for c in range(3):
-            moved_ref[c, :, p * stride : p * stride + BREADTH] = gap
-            moved_ref[c, :, p * stride + BREADTH : p * stride + BREADTH + plane] = lane_shifted(
-                source, 1 - c
-            ).astype(moved_ref.dtype)
-            moved_ref[c, :, (p + 1) * stride - BREADTH : (p + 1) * stride] = gap
-
-
-def tap_rows(moved_ref, block, plane):
-    stride = plane + 2 * BREADTH
+def fill_plane(moved_ref, p, source):
+    rows, plane = source.shape
+    start = p * (plane + 2 * BREADTH)
+    gap = jnp.zeros((rows, BREADTH), moved_ref.dtype)
+    source = source.astype(jnp.float32)
+    for c in range(3):
+        moved_ref[c, :, start : start + BREADTH] = gap
+        moved_ref[c, :, start + BREADTH : start + BREADTH + plane] = lane_shifted(
+            source, 1 - c
+        ).astype(moved_ref.dtype)
+        moved_ref[c, :, start + BREADTH + plane : start + 2 * BREADTH + plane] = gap
+
+
+def fill_sides(place_ref, moved_ref, slots, low_ref, high_ref, last):
+    fill_plane(moved_ref, slots[0], unless(at_end(place_ref, None), low_ref[...]))
+    fill_plane(moved_ref, slots[1], unless(at_end(place_ref, last), high_ref[...]))
+
+
+def tap_rows(moved_ref, block, plane, slots):
     parts = []
-    for a in range(3):
+    for p in slots:
         for b in range(3):
             for c in range(3):
-                at = (2 - a) * stride + (2 - b) * BREADTH
+                at = p * (plane + 2 * BREADTH) + (2 - b) * BREADTH
                 parts.append(moved_ref[c, block, at : at + plane])
     return jnp.concatenate(parts, axis=0)
 
@@ -197,33 +198,56 @@
 def filter_kernel(place_ref, field_ref, grad_ref, low_ref, high_ref, *refs, last):
     outs, moved_ref = refs[:GROUP], refs[GROUP]
     rows, plane = grad_ref.shape
-    fill_moved(place_ref, moved_ref, grad_ref, low_ref, high_ref, last)
+    fill_plane(moved_ref, 1, grad_ref[...])
+    fill_sides(place_ref, moved_ref, (0, 2), low_ref, high_ref, last)
     for j, out_ref in enumerate(outs):
+        block = block_rows(place_ref, "part", j, rows // GROUP)
         sums = lax.dot_general(
             field_ref[...],
-            tap_rows(moved_ref, block_rows(place_ref, "part", j, rows // GROUP), plane),
+            tap_rows(moved_ref, block, plane, (2, 1, 0)),
             (((1,), (1,)), ((), ())),
             preferred_element_type=jnp.float32,
         )
         out_ref[...] = sums.astype(out_ref.dtype)
 
 
-def input_kernel(place_ref, grad_ref, low_ref, high_ref, *refs, last):
-    matrices, outs = refs[:GROUP], refs[GROUP : GROUP + 7]
-    moved_ref, sum_ref = refs[GROUP + 7 :]
-    rows, plane = grad_ref.shape
-    fill_moved(place_ref, moved_ref, grad_ref, low_ref, high_ref, last)
+def add_taps(place_ref, sum_ref, moved_ref, matrices, slots, pick, start=None):
+    plane = sum_ref.shape[1]
     for j, matrix_ref in enumerate(matrices):
+        taps = pick(matrix_ref)
+        block = block_rows(place_ref, "part", j, matrix_ref.shape[0] // 27)
         part = lax.dot_general(
-            matrix_ref[...],
-            tap_rows(moved_ref, block_rows(place_ref, "part", j, rows // GROUP), plane),
+            taps,
+            tap_rows(moved_ref, block, plane, slots),
             (((0,), (0,)), ((), ())),
             preferred_element_type=jnp.float32,
         )
         if j == 0:
-            sum_ref[...] = part
+            sum_ref[...] = part if start is None else start + part
         else:
             sum_ref[...] += part
+
+
+def third(matrix_ref, a):
+    rows = matrix_ref.shape[0] // 3
+    return matrix_ref[a * rows : (a + 1) * rows]
+
+
+def middle_kernel(place_ref, grad_ref, *refs):
+    matrices, (sum_ref, moved_ref) = refs[:GROUP], refs[GROUP:]
+    fill_plane(moved_ref, 0, grad_ref[...])
+    add_taps(place_ref, sum_ref, moved_ref, matrices, (0,), lambda ref: third(ref, 1))
+
+
+def input_kernel(place_ref, middle_ref, low_ref, high_ref, *refs, last):
+    matrices, outs = refs[:GROUP], refs[GROUP : GROUP + 7]
+    moved_ref, sum_ref = refs[GROUP + 7 :]
+    fill_sides(place_ref, moved_ref, (0, 1), low_ref, high_ref, last)
+
+    def sides(ref):
+        return jnp.concatenate([third(ref, 0), third(ref, 2)], axis=0)
+
+    add_taps(place_ref, sum_ref, moved_ref, matrices, (1, 0), sides, middle_ref[...])
     half = outs[1].shape[0]
     for out_ref, (j, start) in zip(outs, INPUT_CUTS):
         start = partner(place_ref, "run", j) * 2 * half + start * half
@@ -384,16 +408,31 @@
         *cotangents,
     )
 
-    around = (grad, shifted(grad, 1), shifted(grad, -1))
-    moved = pltpu.VMEM((3, rows, 3 * (plane + 2 * BREADTH)), bf16)
+    sides = (shifted(grad, 1), shifted(grad, -1))
+
+    def moved(planes):
+        return pltpu.VMEM((3, rows, planes * (plane + 2 * BREADTH)), bf16)
+
+    (middle,) = call(
+        middle_kernel,
+        [((in_total, plane), f32)],
+        "middle",
+        place,
+        grad,
+        *matrices,
+        scratch=[moved(1)],
+        flops=2 * 9 * rows * in_total * plane,
+    )
     sums, sums_1, sums_2, sums_3 = call(
         functools.partial(filter_kernel, **ends),
         [((in_total, taps), bf16)] * GROUP,
         "filter_sums",
         place,
         field,
-        *around,
-        scratch=[moved],
+        grad,
+        *sides,
+        unread=[middle],
+        scratch=[moved(3)],
     )
     sums_3, sums_1 = swap(sums_3, "part", 1), swap(sums_1, "part", 1)
     own, far_low, far_high, low_1, high_3, high_1, low_3 = call(
@@ -401,10 +440,11 @@
         [((depth, plane), f32)] + [((half, plane), bf16)] * 4 + [((half, plane), f32)] * 2,
         "input_sums",
         place,
-        *around,
+        middle,
+        *sides,
         *matrices,
         unread=[sums],
-        scratch=[moved, pltpu.VMEM((in_total, plane), f32)],
+        scratch=[moved(2), pltpu.VMEM((in_total, plane), f32)],
     )
     far_low, far_high = swap(far_low, "run", 1), swap(far_high, "run", 3)
     low_1, high_3 = swap(low_1, "run", 1), swap(high_3, "run", 3)

time: 93.2 us -> 93.1 us (level)
  waiting for transfers between devices: 42.6 us -> 40 us
  Pallas kernels: 12.4 us -> 13.5 us
    ppermute x4, waiting for transfers between devices: 15.8 us -> 14.3 us  [shifted(): lax.ppermute(value, DEPTH, [(at[i], at[(i + by) % count]) for i in range(...]
    pallas_call x16 -> x17, Pallas kernels: 12.4 us -> 13.5 us  [call(): pl.pallas_call(run, in_specs=[pl.BlockSpec(memory_space=pltpu.SMEM)] + [p...]
    ppermute x25, waiting for transfers between devices: 26.8 us -> 25.7 us  [swap(): lax.ppermute(value, axis, [(i, i ^ j) for i in range(lax.axis_size(axis))])]
  transfers between devices with their start and end apart: 30 -> 30, of which waited for: 16 -> 15; matrix products, arithmetic and copies ran while one was open for 0% -> 0% of each run, Pallas kernels for 7% -> 8%
where the time goes in v5:
time: 93.1 us; the launch traced here: 92.9 us
  waiting for transfers between devices  40 us (43%)
  starting transfers between devices  35.7 us (38%)
  Pallas kernels  13.5 us (15%)
  local copies, waits for them, and re-layouts  2.83 us (3%)
    ppermute x25, starting transfers between devices, swap(): lax.ppermute(value, axis, [(i, i ^ j) for i in range(lax.axis_size(axis))])  28.3 us
    ppermute x25, waiting for transfers between devices, swap(): lax.ppermute(value, axis, [(i, i ^ j) for i in range(lax.axis_size(axis))])  25.7 us
    ppermute x4, waiting for transfers between devices, shifted(): lax.ppermute(value, DEPTH, [(at[i], at[(i + by) % count]) for i in range(...  14.3 us
    pallas_call x17, Pallas kernels, call(): pl.pallas_call(run, in_specs=[pl.BlockSpec(memory_space=pltpu.SMEM)] + [p...  13.5 us
    ppermute x4, starting transfers between devices, shifted(): lax.ppermute(value, DEPTH, [(at[i], at[(i + by) % count]) for i in range(...  3.85 us
    all_to_all x1, starting transfers between devices, body(): lax.all_to_all(sums.reshape(spaces, in_total // spaces, taps), 'space', s...  3.53 us
    unnamed x6, local copies, waits for them, and re-layouts  2.83 us
  transfers between devices with their start and end apart: 30, of which 15 were waited for; matrix products, arithmetic and copies ran while one was open for 0% of the time, Pallas kernels for 8%

profile of v5, /device:TPU:1, one launch (start us, length us, event | category | flops | bytes accessed | tf_op | source)
XLA Modules:
  0.0 92.9 jit_solution(424383229289117704)
XLA Ops:
  1.7 3.3 %collective-permute-start = (bf16[16,2048]{1,0:T(8,128)(2,1)S(1)}, bf16[16,2048]{1,0:T(8,128)(2,1)S(1)}, u32[]{:S(2)}, u32[]{:S(2)}) collective-permute-start(bf16[16,2048]{1,0:T(8,128)(2,1)S(1)} %get-tuple-element.38), channel_id=1, source_target_pairs={{0,1},{1,0},{2,3},{3,2},{4,5},{5,4},{6,7},{7,6},{8,9},{9,8},{10,11... | collective-permute-start | bytes 196616 | tf_op jit(solution)/shard_map/ppermute | solution.py:330
  5.0 1.7 %collective-permute-start.2 = (bf16[16,2048]{1,0:T(8,128)(2,1)S(1)}, bf16[16,2048]{1,0:T(8,128)(2,1)S(1)}, u32[]{:S(2)}, u32[]{:S(2)}) collective-permute-start(bf16[16,2048]{1,0:T(8,128)(2,1)S(1)} %get-tuple-element.40), channel_id=1, source_target_pairs={{0,3},{1,2},{2,1},{3,0},{4,7},{5,6},{6,5},{7,4},{8,11},{9,10},{10,... | collective-permute-start | bytes 196616 | tf_op jit(solution)/shard_map/ppermute | solution.py:330
  6.8 0.9 %copy-done = bf16[1,16,4,16,128]{4,3,2,1,0:T(8,128)(2,1)S(1)} copy-done((bf16[1,16,4,16,128]{4,3,2,1,0:T(8,128)(2,1)S(1)}, bf16[1,16,4,16,128]{4,3,2,1,0:T(8,128)(2,1)}, u32[]{:S(2)}) %copy-start) | copy-done | bytes 262168
  8.8 1.5 %collective-permute-done.2.refs_3_ = bf16[16,2048]{1,0:T(8,128)(2,1)S(1)} collective-permute-done((bf16[16,2048]{1,0:T(8,128)(2,1)S(1)}, bf16[16,2048]{1,0:T(8,128)(2,1)S(1)}, u32[]{:S(2)}, u32[]{:S(2)}) %collective-permute-start.2) | collective-permute-done | bytes 65568 | tf_op jit(solution)/shard_map/ppermute | solution.py:330
  10.3 1.1 %collective-permute-start.4 = (bf16[64,2048]{1,0:T(8,128)(2,1)S(1)}, bf16[64,2048]{1,0:T(8,128)(2,1)S(1)}, u32[]{:S(2)}, u32[]{:S(2)}) collective-permute-start(bf16[64,2048]{1,0:T(8,128)(2,1)S(1)} %order.1.refs_0_), channel_id=1, source_target_pairs={{0,12},{4,8},{8,4},{12,0},{1,13},{5,9},{9,5},{13,1},{2,14},{6,10},... | collective-permute-start | bytes 786440 | tf_op jit(solution)/shard_map/ppermute | solution.py:330
  11.4 1.7 %collective-permute-start.9 = (bf16[432,256]{1,0:T(8,128)(2,1)S(1)}, bf16[432,256]{1,0:T(8,128)(2,1)S(1)}, u32[]{:S(2)}, u32[]{:S(2)}) collective-permute-start(bf16[432,256]{1,0:T(8,128)(2,1)S(1)} %get-tuple-element.41.refs_4_.refs_5_.refs_1_.refs_3_), channel_id=1, source_target_pairs={{0,3},{1,2},{2,1},{3,0},{4,7},{5,6},{6,5},{7,4},{8,11},{9,10},{10,... | collective-permute-start | bytes 663560 | tf_op jit(solution)/shard_map/ppermute | solution.py:330
  13.6 5.7 %collective-permute-done.4.refs_1_.refs_2_ = bf16[64,2048]{1,0:T(8,128)(2,1)S(1)} collective-permute-done((bf16[64,2048]{1,0:T(8,128)(2,1)S(1)}, bf16[64,2048]{1,0:T(8,128)(2,1)S(1)}, u32[]{:S(2)}, u32[]{:S(2)}) %collective-permute-start.4) | collective-permute-done | bytes 262176 | tf_op jit(solution)/shard_map/ppermute | solution.py:330
  19.3 1.2 %collective-permute-start.5 = (bf16[32,2048]{1,0:T(8,128)(2,1)S(1)}, bf16[32,2048]{1,0:T(8,128)(2,1)S(1)}, u32[]{:S(2)}, u32[]{:S(2)}) collective-permute-start(bf16[32,2048]{1,0:T(8,128)(2,1)S(1)} %get-tuple-element.42), channel_id=1, source_target_pairs={{0,12},{4,8},{8,4},{12,0},{1,13},{5,9},{9,5},{13,1},{2,14},{6,10},... | collective-permute-start | bytes 393224 | tf_op jit(solution)/shard_map/ppermute | solution.py:330
  20.6 1.6 %collective-permute-start.10 = (bf16[16,2048]{1,0:T(8,128)(2,1)S(1)}, bf16[16,2048]{1,0:T(8,128)(2,1)S(1)}, u32[]{:S(2)}, u32[]{:S(2)}) collective-permute-start(bf16[16,2048]{1,0:T(8,128)(2,1)S(1)} %get-tuple-element.45), channel_id=1, source_target_pairs={{0,1},{1,0},{2,3},{3,2},{4,5},{5,4},{6,7},{7,6},{8,9},{9,8},{10,11... | collective-permute-start | bytes 196616 | tf_op jit(solution)/shard_map/ppermute | solution.py:330
  22.2 1.9 %collective-permute-done.8.refs_7_.refs_3_.refs_5_ = bf16[432,256]{1,0:T(8,128)(2,1)S(1)} collective-permute-done((bf16[432,256]{1,0:T(8,128)(2,1)S(1)}, bf16[432,256]{1,0:T(8,128)(2,1)S(1)}, u32[]{:S(2)}, u32[]{:S(2)}) %collective-permute-start.8) | collective-permute-done | bytes 221216 | tf_op jit(solution)/shard_map/ppermute | solution.py:330
  24.1 1.1 %collective-permute-start.11 = (bf16[16,2048]{1,0:T(8,128)(2,1)S(1)}, bf16[16,2048]{1,0:T(8,128)(2,1)S(1)}, u32[]{:S(2)}, u32[]{:S(2)}) collective-permute-start(bf16[16,2048]{1,0:T(8,128)(2,1)S(1)} %get-tuple-element.46), channel_id=1, source_target_pairs={{0,2},{1,3},{2,0},{3,1},{4,6},{5,7},{6,4},{7,5},{8,10},{9,11},{10,... | collective-permute-start | bytes 196616 | tf_op jit(solution)/shard_map/ppermute | solution.py:330
  26.2 1.0 %after.1 = (bf16[256,2048]{1,0:T(8,128)(2,1)S(1)}, bf16[64,2048]{1,0:T(8,128)(2,1)S(1)}) custom-call(s32[1]{0:T(128)} %bitcast.place_ref, bf16[64,2048]{1,0:T(8,128)(2,1)S(1)} %order.1.refs_0_, bf16[64,2048]{1,0:T(8,128)(2,1)S(1)} %collective-permute-done.3.refs_0_.refs_1_, bf16[64,2048]{1,0:T(8,128)(2,1)S(1)} %collective-permute-done.4.refs_1_.refs_2_, ...), custom_call_target="tpu_custom_call" | custom-call | flops 1 | bytes 1 | tf_op jit(solution)/shard_map/after/pallas_call | solution.py:81
  27.2 2.6 %collective-permute-done.12.refs_7_.refs_6_ = bf16[16,2048]{1,0:T(8,128)(2,1)S(1)} collective-permute-done((bf16[16,2048]{1,0:T(8,128)(2,1)S(1)}, bf16[16,2048]{1,0:T(8,128)(2,1)S(1)}, u32[]{:S(2)}, u32[]{:S(2)}) %collective-permute-start.12) | collective-permute-done | bytes 65568 | tf_op jit(solution)/shard_map/ppermute | solution.py:330
  32.6 2.4 %collective-permute-done.13.refs_1_ = bf16[64,2048]{1,0:T(8,128)(2,1)S(1)} collective-permute-done((bf16[64,2048]{1,0:T(8,128)(2,1)S(1)}, bf16[64,2048]{1,0:T(8,128)(2,1)S(1)}, u32[]{:S(2)}, u32[]{:S(2)}) %collective-permute-start.13) | collective-permute-done | bytes 262176 | tf_op jit(solution)/shard_map/ppermute | solution.py:326
  35.0 2.2 %collective-permute-done.14.refs_2_ = bf16[64,2048]{1,0:T(8,128)(2,1)S(1)} collective-permute-done((bf16[64,2048]{1,0:T(8,128)(2,1)S(1)}, bf16[64,2048]{1,0:T(8,128)(2,1)S(1)}, u32[]{:S(2)}, u32[]{:S(2)}) %collective-permute-start.14) | collective-permute-done | bytes 262176 | tf_op jit(solution)/shard_map/ppermute | solution.py:326
  37.5 3.0 %collective-permute-start.16 = (bf16[64,2048]{1,0:T(8,128)(2,1)S(1)}, bf16[64,2048]{1,0:T(8,128)(2,1)S(1)}, u32[]{:S(2)}, u32[]{:S(2)}) collective-permute-start(bf16[64,2048]{1,0:T(8,128)(2,1)S(1)} %get-tuple-element.50.refs_0_.refs_1_), channel_id=1, source_target_pairs={{2,240},{3,2},{1,3},{0,1},{16,0},{17,16},{19,17},{18,19},{34,18},{... | collective-permute-start | bytes 786440 | tf_op jit(solution)/shard_map/ppermute | solution.py:326
  40.5 1.5 %middle.1.refs_4_.refs_0_ = f32[256,2048]{1,0:T(8,128)S(1)} custom-call(s32[1]{0:T(128)} %bitcast.place_ref, bf16[64,2048]{1,0:T(8,128)(2,1)S(1)} %get-tuple-element.50.refs_0_.refs_1_, bf16[432,256]{1,0:T(8,128)(2,1)S(1)} %get-tuple-element.41.refs_4_.refs_5_.refs_1_.refs_3_, bf16[432,256]{1,0:T(8,128)(2,1)S(1)} %collective-permute-done.7.refs_6_.refs_2_.refs_4_, ...), custom_call_target="tpu_custom_call" | custom-call | flops 603979776 | bytes 1 | tf_op jit(solution)/shard_map/middle/pallas_call | solution.py:81
  42.0 1.8 %collective-permute-done.16.refs_3_.refs_2_ = bf16[64,2048]{1,0:T(8,128)(2,1)S(1)} collective-permute-done((bf16[64,2048]{1,0:T(8,128)(2,1)S(1)}, bf16[64,2048]{1,0:T(8,128)(2,1)S(1)}, u32[]{:S(2)}, u32[]{:S(2)}) %collective-permute-start.16) | collective-permute-done | bytes 262176 | tf_op jit(solution)/shard_map/ppermute | solution.py:326
  43.8 7.9 %collective-permute-done.15.refs_2_.refs_1_ = bf16[64,2048]{1,0:T(8,128)(2,1)S(1)} collective-permute-done((bf16[64,2048]{1,0:T(8,128)(2,1)S(1)}, bf16[64,2048]{1,0:T(8,128)(2,1)S(1)}, u32[]{:S(2)}, u32[]{:S(2)}) %collective-permute-start.15) | collective-permute-done | bytes 262176 | tf_op jit(solution)/shard_map/ppermute | solution.py:326
  51.7 2.9 %filter_sums.1 = (bf16[256,432]{1,0:T(8,128)(2,1)S(1)}, bf16[256,432]{1,0:T(8,128)(2,1)S(1)}, bf16[256,432]{1,0:T(8,128)(2,1)S(1)}, bf16[256,432]{1,0:T(8,128)(2,1)S(1)}) custom-call(s32[1]{0:T(128)} %bitcast.place_ref, bf16[256,2048]{1,0:T(8,128)(2,1)S(1)} %get-tuple-element.44.refs_0_, bf16[64,2048]{1,0:T(8,128)(2,1)S(1)} %get-tuple-element.50.refs_0_.refs_1_, ...), custom_call_target="tpu_custom_call" | custom-call | flops 1 | bytes 1 | tf_op jit(solution)/shard_map/filter_sums/pallas_call | solution.py:81
  55.2 2.9 %input_sums.1 = (f32[64,2048]{1,0:T(8,128)S(1)}, bf16[32,2048]{1,0:T(8,128)(2,1)S(1)}, bf16[32,2048]{1,0:T(8,128)(2,1)S(1)}, bf16[32,2048]{1,0:T(8,128)(2,1)S(1)...) custom-call(s32[1]{0:T(128)} %bitcast.place_ref, ...), custom_call_target="tpu_custom_call" | custom-call | flops 1 | bytes 1 | tf_op jit(solution)/shard_map/input_sums/pallas_call | solution.py:81
  59.8 4.5 %collective-permute-start.28 = (bf16[256,432]{1,0:T(8,128)(2,1)S(1)}, bf16[256,432]{1,0:T(8,128)(2,1)S(1)}, u32[]{:S(2)}, u32[]{:S(2)}) collective-permute-start(bf16[256,432]{1,0:T(8,128)(2,1)S(1)} %lift.1.refs_4_), channel_id=1, source_target_pairs={{0,2},{1,3},{2,0},{3,1},{4,6},{5,7},{6,4},{7,5},{8,10},{9,11},{10,... | collective-permute-start | bytes 663560 | tf_op jit(solution)/shard_map/ppermute | solution.py:330
  64.9 2.0 %collective-permute-start.24 = (bf16[32,2048]{1,0:T(8,128)(2,1)S(1)}, bf16[32,2048]{1,0:T(8,128)(2,1)S(1)}, u32[]{:S(2)}, u32[]{:S(2)}) collective-permute-start(bf16[32,2048]{1,0:T(8,128)(2,1)S(1)} %get-tuple-element.63), channel_id=1, source_target_pairs={{0,12},{4,8},{8,4},{12,0},{1,13},{5,9},{9,5},{13,1},{2,14},{6,10},... | collective-permute-start | bytes 393224 | tf_op jit(solution)/shard_map/ppermute | solution.py:330
  68.4 1.5 %collective-permute-done.24.refs_4_.refs_6_ = bf16[32,2048]{1,0:T(8,128)(2,1)S(1)} collective-permute-done((bf16[32,2048]{1,0:T(8,128)(2,1)S(1)}, bf16[32,2048]{1,0:T(8,128)(2,1)S(1)}, u32[]{:S(2)}, u32[]{:S(2)}) %collective-permute-start.24) | collective-permute-done | bytes 131104 | tf_op jit(solution)/shard_map/ppermute | solution.py:330
  69.9 1.5 %collective-permute-done.22.refs_2_.refs_4_ = bf16[32,2048]{1,0:T(8,128)(2,1)S(1)} collective-permute-done((bf16[32,2048]{1,0:T(8,128)(2,1)S(1)}, bf16[32,2048]{1,0:T(8,128)(2,1)S(1)}, u32[]{:S(2)}, u32[]{:S(2)}) %collective-permute-start.22) | collective-permute-done | bytes 131104 | tf_op jit(solution)/shard_map/ppermute | solution.py:330
  71.4 1.9 %collective-permute-done.23.refs_3_.refs_5_ = bf16[32,2048]{1,0:T(8,128)(2,1)S(1)} collective-permute-done((bf16[32,2048]{1,0:T(8,128)(2,1)S(1)}, bf16[32,2048]{1,0:T(8,128)(2,1)S(1)}, u32[]{:S(2)}, u32[]{:S(2)}) %collective-permute-start.23) | collective-permute-done | bytes 131104 | tf_op jit(solution)/shard_map/ppermute | solution.py:330
  74.1 3.5 %all-to-all-start = ((bf16[16,16,432]{2,1,0:T(8,128)(2,1)}), bf16[16,16,432]{2,1,0:T(8,128)(2,1)S(1)}, u32[]{:S(2)}, u32[]{:S(2)}) async-start(bf16[16,16,432]{2,1,0:T(8,128)(2,1)} %bitcast.6), calls=%async_computation | async-start | bytes 524288 | tf_op jit(solution)/shard_map/all_to_all | solution.py:475
  77.8 2.7 %collective-permute-start.25 = (bf16[2,16,2048]{2,1,0:T(8,128)(2,1)S(1)}, bf16[2,16,2048]{2,1,0:T(8,128)(2,1)S(1)}, u32[]{:S(2)}, u32[]{:S(2)}) collective-permute-start(bf16[2,16,2048]{2,1,0:T(8,128)(2,1)S(1)} %get-tuple-element.66), channel_id=1, source_target_pairs={{0,1},{1,0},{2,3},{3,2},{4,5},{5,4},{6,7},{7,6},{8,9},{9,8},{10,11... | collective-permute-start | bytes 393224 | tf_op jit(solution)/shard_map/ppermute | solution.py:330
  80.5 1.8 %collective-permute-start.26 = (bf16[2,16,2048]{2,1,0:T(8,128)(2,1)S(1)}, bf16[2,16,2048]{2,1,0:T(8,128)(2,1)S(1)}, u32[]{:S(2)}, u32[]{:S(2)}) collective-permute-start(bf16[2,16,2048]{2,1,0:T(8,128)(2,1)S(1)} %get-tuple-element.67), channel_id=1, source_target_pairs={{0,2},{1,3},{2,0},{3,1},{4,6},{5,7},{6,4},{7,5},{8,10},{9,11},{10,... | collective-permute-start | bytes 393224 | tf_op jit(solution)/shard_map/ppermute | solution.py:330
  82.4 5.2 %collective-permute-done.26.refs_2_ = bf16[2,16,2048]{2,1,0:T(8,128)(2,1)S(1)} collective-permute-done((bf16[2,16,2048]{2,1,0:T(8,128)(2,1)S(1)}, bf16[2,16,2048]{2,1,0:T(8,128)(2,1)S(1)}, u32[]{:S(2)}, u32[]{:S(2)}) %collective-permute-start.26) | collective-permute-done | bytes 131104 | tf_op jit(solution)/shard_map/ppermute | solution.py:330
  87.5 3.5 %collective-permute-done.27.refs_3_ = bf16[2,16,2048]{2,1,0:T(8,128)(2,1)S(1)} collective-permute-done((bf16[2,16,2048]{2,1,0:T(8,128)(2,1)S(1)}, bf16[2,16,2048]{2,1,0:T(8,128)(2,1)S(1)}, u32[]{:S(2)}, u32[]{:S(2)}) %collective-permute-start.27) | collective-permute-done | bytes 131104 | tf_op jit(solution)/shard_map/ppermute | solution.py:330
  91.0 1.0 %close.1 = (bf16[16,4,16,128]{3,2,1,0:T(8,128)(2,1)}, bf16[16,4,16,128]{3,2,1,0:T(8,128)(2,1)}) custom-call(s32[1]{0:T(128)} %bitcast.place_ref, bf16[2,16,2048]{2,1,0:T(8,128)(2,1)S(1)} %get-tuple-element.65.refs_0_, bf16[2,16,2048]{2,1,0:T(8,128)(2,1)S(1)} %collective-permute-done.25.refs_1_, bf16[2,16,2048]{2,1,0:T(8,128)(2,1)S(1)} %collective-permute-done.26.refs_2_, ...), custom_call_target="tpu_custom_call" | custom-call | flops 1 | bytes 1 | tf_op jit(solution)/shard_map/close/pallas_call | solution.py:81
  (51 shorter events, 12.9 us)
Async XLA Ops:
  0.6 1.0 %copy-start.1 = (bf16[1,16,4,16,128]{4,3,2,1,0:T(8,128)(2,1)S(1)}, bf16[1,16,4,16,128]{4,3,2,1,0:T(8,128)(2,1)}, u32[]{:S(2)}) copy-start(bf16[1,16,4,16,128]{4,3,2,1,0:T(8,128)(2,1)} %param.3) | copy-start | bytes 786436
  1.7 7.1 %collective-permute-start = (bf16[16,2048]{1,0:T(8,128)(2,1)S(1)}, bf16[16,2048]{1,0:T(8,128)(2,1)S(1)}, u32[]{:S(2)}, u32[]{:S(2)}) collective-permute-start(bf16[16,2048]{1,0:T(8,128)(2,1)S(1)} %get-tuple-element.38), channel_id=1, source_target_pairs={{0,1},{1,0},{2,3},{3,2},{4,5},{5,4},{6,7},{7,6},{8,9},{9,8},{10,11... | collective-permute-start | bytes 196616 | tf_op jit(solution)/shard_map/ppermute | solution.py:330
  5.0 3.8 %collective-permute-start.1 = (bf16[16,2048]{1,0:T(8,128)(2,1)S(1)}, bf16[16,2048]{1,0:T(8,128)(2,1)S(1)}, u32[]{:S(2)}, u32[]{:S(2)}) collective-permute-start(bf16[16,2048]{1,0:T(8,128)(2,1)S(1)} %get-tuple-element.39), channel_id=1, source_target_pairs={{0,2},{1,3},{2,0},{3,1},{4,6},{5,7},{6,4},{7,5},{8,10},{9,11},{10,... | collective-permute-start | bytes 196616 | tf_op jit(solution)/shard_map/ppermute | solution.py:330
  5.0 5.2 %collective-permute-start.2 = (bf16[16,2048]{1,0:T(8,128)(2,1)S(1)}, bf16[16,2048]{1,0:T(8,128)(2,1)S(1)}, u32[]{:S(2)}, u32[]{:S(2)}) collective-permute-start(bf16[16,2048]{1,0:T(8,128)(2,1)S(1)} %get-tuple-element.40), channel_id=1, source_target_pairs={{0,3},{1,2},{2,1},{3,0},{4,7},{5,6},{6,5},{7,4},{8,11},{9,10},{10,... | collective-permute-start | bytes 196616 | tf_op jit(solution)/shard_map/ppermute | solution.py:330
  6.8 0.9 %copy-start = (bf16[1,16,4,16,128]{4,3,2,1,0:T(8,128)(2,1)S(1)}, bf16[1,16,4,16,128]{4,3,2,1,0:T(8,128)(2,1)}, u32[]{:S(2)}) copy-start(bf16[1,16,4,16,128]{4,3,2,1,0:T(8,128)(2,1)} %param.5) | copy-start | bytes 786436
  10.3 9.0 %collective-permute-start.4 = (bf16[64,2048]{1,0:T(8,128)(2,1)S(1)}, bf16[64,2048]{1,0:T(8,128)(2,1)S(1)}, u32[]{:S(2)}, u32[]{:S(2)}) collective-permute-start(bf16[64,2048]{1,0:T(8,128)(2,1)S(1)} %order.1.refs_0_), channel_id=1, source_target_pairs={{0,12},{4,8},{8,4},{12,0},{1,13},{5,9},{9,5},{13,1},{2,14},{6,10},... | collective-permute-start | bytes 786440 | tf_op jit(solution)/shard_map/ppermute | solution.py:330
  11.4 7.9 %collective-permute-start.3 = (bf16[64,2048]{1,0:T(8,128)(2,1)S(1)}, bf16[64,2048]{1,0:T(8,128)(2,1)S(1)}, u32[]{:S(2)}, u32[]{:S(2)}) collective-permute-start(bf16[64,2048]{1,0:T(8,128)(2,1)S(1)} %order.1.refs_0_), channel_id=1, source_target_pairs={{0,4},{4,0},{8,12},{12,8},{1,5},{5,1},{9,13},{13,9},{2,6},{6,2},{1... | collective-permute-start | bytes 786440 | tf_op jit(solution)/shard_map/ppermute | solution.py:330
  11.4 9.1 %collective-permute-start.9 = (bf16[432,256]{1,0:T(8,128)(2,1)S(1)}, bf16[432,256]{1,0:T(8,128)(2,1)S(1)}, u32[]{:S(2)}, u32[]{:S(2)}) collective-permute-start(bf16[432,256]{1,0:T(8,128)(2,1)S(1)} %get-tuple-element.41.refs_4_.refs_5_.refs_1_.refs_3_), channel_id=1, source_target_pairs={{0,3},{1,2},{2,1},{3,0},{4,7},{5,6},{6,5},{7,4},{8,11},{9,10},{10,... | collective-permute-start | bytes 663560 | tf_op jit(solution)/shard_map/ppermute | solution.py:330
  13.1 11.0 %collective-permute-start.8 = (bf16[432,256]{1,0:T(8,128)(2,1)S(1)}, bf16[432,256]{1,0:T(8,128)(2,1)S(1)}, u32[]{:S(2)}, u32[]{:S(2)}) collective-permute-start(bf16[432,256]{1,0:T(8,128)(2,1)S(1)} %get-tuple-element.41.refs_4_.refs_5_.refs_1_.refs_3_), channel_id=1, source_target_pairs={{0,2},{1,3},{2,0},{3,1},{4,6},{5,7},{6,4},{7,5},{8,10},{9,11},{10,... | collective-permute-start | bytes 663560 | tf_op jit(solution)/shard_map/ppermute | solution.py:330
  13.6 11.7 %collective-permute-start.7 = (bf16[432,256]{1,0:T(8,128)(2,1)S(1)}, bf16[432,256]{1,0:T(8,128)(2,1)S(1)}, u32[]{:S(2)}, u32[]{:S(2)}) collective-permute-start(bf16[432,256]{1,0:T(8,128)(2,1)S(1)} %get-tuple-element.41.refs_4_.refs_5_.refs_1_.refs_3_), channel_id=1, source_target_pairs={{0,1},{1,0},{2,3},{3,2},{4,5},{5,4},{6,7},{7,6},{8,9},{9,8},{10,11... | collective-permute-start | bytes 663560 | tf_op jit(solution)/shard_map/ppermute | solution.py:330
  19.3 6.8 %collective-permute-start.5 = (bf16[32,2048]{1,0:T(8,128)(2,1)S(1)}, bf16[32,2048]{1,0:T(8,128)(2,1)S(1)}, u32[]{:S(2)}, u32[]{:S(2)}) collective-permute-start(bf16[32,2048]{1,0:T(8,128)(2,1)S(1)} %get-tuple-element.42), channel_id=1, source_target_pairs={{0,12},{4,8},{8,4},{12,0},{1,13},{5,9},{9,5},{13,1},{2,14},{6,10},... | collective-permute-start | bytes 393224 | tf_op jit(solution)/shard_map/ppermute | solution.py:330
  20.6 5.6 %collective-permute-start.6 = (bf16[32,2048]{1,0:T(8,128)(2,1)S(1)}, bf16[32,2048]{1,0:T(8,128)(2,1)S(1)}, u32[]{:S(2)}, u32[]{:S(2)}) collective-permute-start(bf16[32,2048]{1,0:T(8,128)(2,1)S(1)} %get-tuple-element.43), channel_id=1, source_target_pairs={{0,4},{4,0},{8,12},{12,8},{1,5},{5,1},{9,13},{13,9},{2,6},{6,2},{1... | collective-permute-start | bytes 393224 | tf_op jit(solution)/shard_map/ppermute | solution.py:330
  20.6 6.6 %collective-permute-start.10 = (bf16[16,2048]{1,0:T(8,128)(2,1)S(1)}, bf16[16,2048]{1,0:T(8,128)(2,1)S(1)}, u32[]{:S(2)}, u32[]{:S(2)}) collective-permute-start(bf16[16,2048]{1,0:T(8,128)(2,1)S(1)} %get-tuple-element.45), channel_id=1, source_target_pairs={{0,1},{1,0},{2,3},{3,2},{4,5},{5,4},{6,7},{7,6},{8,9},{9,8},{10,11... | collective-permute-start | bytes 196616 | tf_op jit(solution)/shard_map/ppermute | solution.py:330
  24.1 3.1 %collective-permute-start.11 = (bf16[16,2048]{1,0:T(8,128)(2,1)S(1)}, bf16[16,2048]{1,0:T(8,128)(2,1)S(1)}, u32[]{:S(2)}, u32[]{:S(2)}) collective-permute-start(bf16[16,2048]{1,0:T(8,128)(2,1)S(1)} %get-tuple-element.46), channel_id=1, source_target_pairs={{0,2},{1,3},{2,0},{3,1},{4,6},{5,7},{6,4},{7,5},{8,10},{9,11},{10,... | collective-permute-start | bytes 196616 | tf_op jit(solution)/shard_map/ppermute | solution.py:330
  25.2 4.6 %collective-permute-start.12 = (bf16[16,2048]{1,0:T(8,128)(2,1)S(1)}, bf16[16,2048]{1,0:T(8,128)(2,1)S(1)}, u32[]{:S(2)}, u32[]{:S(2)}) collective-permute-start(bf16[16,2048]{1,0:T(8,128)(2,1)S(1)} %get-tuple-element.47), channel_id=1, source_target_pairs={{0,3},{1,2},{2,1},{3,0},{4,7},{5,6},{6,5},{7,4},{8,11},{9,10},{10,... | collective-permute-start | bytes 196616 | tf_op jit(solution)/shard_map/ppermute | solution.py:330
  30.8 4.2 %collective-permute-start.13 = (bf16[64,2048]{1,0:T(8,128)(2,1)S(1)}, bf16[64,2048]{1,0:T(8,128)(2,1)S(1)}, u32[]{:S(2)}, u32[]{:S(2)}) collective-permute-start(bf16[64,2048]{1,0:T(8,128)(2,1)S(1)} %before.1.refs_5_), channel_id=1, source_target_pairs={{2,240},{3,2},{1,3},{0,1},{16,0},{17,16},{19,17},{18,19},{34,18},{... | collective-permute-start | bytes 786440 | tf_op jit(solution)/shard_map/ppermute | solution.py:326
  31.7 5.5 %collective-permute-start.14 = (bf16[64,2048]{1,0:T(8,128)(2,1)S(1)}, bf16[64,2048]{1,0:T(8,128)(2,1)S(1)}, u32[]{:S(2)}, u32[]{:S(2)}) collective-permute-start(bf16[64,2048]{1,0:T(8,128)(2,1)S(1)} %get-tuple-element.48), channel_id=1, source_target_pairs={{2,3},{3,1},{1,0},{0,16},{16,17},{17,19},{19,18},{18,34},{34,35},{... | collective-permute-start | bytes 786440 | tf_op jit(solution)/shard_map/ppermute | solution.py:326
  37.5 6.3 %collective-permute-start.16 = (bf16[64,2048]{1,0:T(8,128)(2,1)S(1)}, bf16[64,2048]{1,0:T(8,128)(2,1)S(1)}, u32[]{:S(2)}, u32[]{:S(2)}) collective-permute-start(bf16[64,2048]{1,0:T(8,128)(2,1)S(1)} %get-tuple-element.50.refs_0_.refs_1_), channel_id=1, source_target_pairs={{2,240},{3,2},{1,3},{0,1},{16,0},{17,16},{19,17},{18,19},{34,18},{... | collective-permute-start | bytes 786440 | tf_op jit(solution)/shard_map/ppermute | solution.py:326
  40.5 11.2 %collective-permute-start.15 = (bf16[64,2048]{1,0:T(8,128)(2,1)S(1)}, bf16[64,2048]{1,0:T(8,128)(2,1)S(1)}, u32[]{:S(2)}, u32[]{:S(2)}) collective-permute-start(bf16[64,2048]{1,0:T(8,128)(2,1)S(1)} %get-tuple-element.50.refs_0_.refs_1_), channel_id=1, source_target_pairs={{2,3},{3,1},{1,0},{0,16},{16,17},{17,19},{19,18},{18,34},{34,35},{... | collective-permute-start | bytes 786440 | tf_op jit(solution)/shard_map/ppermute | solution.py:326
  54.6 5.1 %collective-permute-start.20 = (bf16[256,432]{1,0:T(8,128)(2,1)S(1)}, bf16[256,432]{1,0:T(8,128)(2,1)S(1)}, u32[]{:S(2)}, u32[]{:S(2)}) collective-permute-start(bf16[256,432]{1,0:T(8,128)(2,1)S(1)} %get-tuple-element.59), channel_id=1, source_target_pairs={{0,1},{1,0},{2,3},{3,2},{4,5},{5,4},{6,7},{7,6},{8,9},{9,8},{10,11... | collective-permute-start | bytes 663560 | tf_op jit(solution)/shard_map/ppermute | solution.py:330
  54.7 5.0 %collective-permute-start.21 = (bf16[256,432]{1,0:T(8,128)(2,1)S(1)}, bf16[256,432]{1,0:T(8,128)(2,1)S(1)}, u32[]{:S(2)}, u32[]{:S(2)}) collective-permute-start(bf16[256,432]{1,0:T(8,128)(2,1)S(1)} %get-tuple-element.60), channel_id=1, source_target_pairs={{0,1},{1,0},{2,3},{3,2},{4,5},{5,4},{6,7},{7,6},{8,9},{9,8},{10,11... | collective-permute-start | bytes 663560 | tf_op jit(solution)/shard_map/ppermute | solution.py:330
  58.1 8.8 %collective-permute-start.18 = (bf16[32,2048]{1,0:T(8,128)(2,1)S(1)}, bf16[32,2048]{1,0:T(8,128)(2,1)S(1)}, u32[]{:S(2)}, u32[]{:S(2)}) collective-permute-start(bf16[32,2048]{1,0:T(8,128)(2,1)S(1)} %get-tuple-element.56), channel_id=1, source_target_pairs={{0,12},{4,8},{8,4},{12,0},{1,13},{5,9},{9,5},{13,1},{2,14},{6,10},... | collective-permute-start | bytes 393224 | tf_op jit(solution)/shard_map/ppermute | solution.py:330
  58.8 8.1 %collective-permute-start.19 = (bf16[32,2048]{1,0:T(8,128)(2,1)S(1)}, bf16[32,2048]{1,0:T(8,128)(2,1)S(1)}, u32[]{:S(2)}, u32[]{:S(2)}) collective-permute-start(bf16[32,2048]{1,0:T(8,128)(2,1)S(1)} %get-tuple-element.57), channel_id=1, source_target_pairs={{0,4},{4,0},{8,12},{12,8},{1,5},{5,1},{9,13},{13,9},{2,6},{6,2},{1... | collective-permute-start | bytes 393224 | tf_op jit(solution)/shard_map/ppermute | solution.py:330
  59.8 13.5 %collective-permute-start.28 = (bf16[256,432]{1,0:T(8,128)(2,1)S(1)}, bf16[256,432]{1,0:T(8,128)(2,1)S(1)}, u32[]{:S(2)}, u32[]{:S(2)}) collective-permute-start(bf16[256,432]{1,0:T(8,128)(2,1)S(1)} %lift.1.refs_4_), channel_id=1, source_target_pairs={{0,2},{1,3},{2,0},{3,1},{4,6},{5,7},{6,4},{7,5},{8,10},{9,11},{10,... | collective-permute-start | bytes 663560 | tf_op jit(solution)/shard_map/ppermute | solution.py:330
  64.3 4.1 %collective-permute-start.17 = (bf16[32,2048]{1,0:T(8,128)(2,1)S(1)}, bf16[32,2048]{1,0:T(8,128)(2,1)S(1)}, u32[]{:S(2)}, u32[]{:S(2)}) collective-permute-start(bf16[32,2048]{1,0:T(8,128)(2,1)S(1)} %get-tuple-element.53), channel_id=1, source_target_pairs={{0,4},{4,0},{8,12},{12,8},{1,5},{5,1},{9,13},{13,9},{2,6},{6,2},{1... | collective-permute-start | bytes 393224 | tf_op jit(solution)/shard_map/ppermute | solution.py:330
  64.9 5.0 %collective-permute-start.24 = (bf16[32,2048]{1,0:T(8,128)(2,1)S(1)}, bf16[32,2048]{1,0:T(8,128)(2,1)S(1)}, u32[]{:S(2)}, u32[]{:S(2)}) collective-permute-start(bf16[32,2048]{1,0:T(8,128)(2,1)S(1)} %get-tuple-element.63), channel_id=1, source_target_pairs={{0,12},{4,8},{8,4},{12,0},{1,13},{5,9},{9,5},{13,1},{2,14},{6,10},... | collective-permute-start | bytes 393224 | tf_op jit(solution)/shard_map/ppermute | solution.py:330
  67.0 4.4 %collective-permute-start.22 = (bf16[32,2048]{1,0:T(8,128)(2,1)S(1)}, bf16[32,2048]{1,0:T(8,128)(2,1)S(1)}, u32[]{:S(2)}, u32[]{:S(2)}) collective-permute-start(bf16[32,2048]{1,0:T(8,128)(2,1)S(1)} %get-tuple-element.61), channel_id=1, source_target_pairs={{0,4},{4,0},{8,12},{12,8},{1,5},{5,1},{9,13},{13,9},{2,6},{6,2},{1... | collective-permute-start | bytes 393224 | tf_op jit(solution)/shard_map/ppermute | solution.py:330
  67.5 5.8 %collective-permute-start.23 = (bf16[32,2048]{1,0:T(8,128)(2,1)S(1)}, bf16[32,2048]{1,0:T(8,128)(2,1)S(1)}, u32[]{:S(2)}, u32[]{:S(2)}) collective-permute-start(bf16[32,2048]{1,0:T(8,128)(2,1)S(1)} %get-tuple-element.62), channel_id=1, source_target_pairs={{0,12},{4,8},{8,4},{12,0},{1,13},{5,9},{9,5},{13,1},{2,14},{6,10},... | collective-permute-start | bytes 393224 | tf_op jit(solution)/shard_map/ppermute | solution.py:330
  74.1 17.9 %all-to-all-start = ((bf16[16,16,432]{2,1,0:T(8,128)(2,1)}), bf16[16,16,432]{2,1,0:T(8,128)(2,1)S(1)}, u32[]{:S(2)}, u32[]{:S(2)}) async-start(bf16[16,16,432]{2,1,0:T(8,128)(2,1)} %bitcast.6), calls=%async_computation | async-start | bytes 524288 | tf_op jit(solution)/shard_map/all_to_all | solution.py:475
  77.8 4.6 %collective-permute-start.25 = (bf16[2,16,2048]{2,1,0:T(8,128)(2,1)S(1)}, bf16[2,16,2048]{2,1,0:T(8,128)(2,1)S(1)}, u32[]{:S(2)}, u32[]{:S(2)}) collective-permute-start(bf16[2,16,2048]{2,1,0:T(8,128)(2,1)S(1)} %get-tuple-element.66), channel_id=1, source_target_pairs={{0,1},{1,0},{2,3},{3,2},{4,5},{5,4},{6,7},{7,6},{8,9},{9,8},{10,11... | collective-permute-start | bytes 393224 | tf_op jit(solution)/shard_map/ppermute | solution.py:330
  80.5 7.1 %collective-permute-start.26 = (bf16[2,16,2048]{2,1,0:T(8,128)(2,1)S(1)}, bf16[2,16,2048]{2,1,0:T(8,128)(2,1)S(1)}, u32[]{:S(2)}, u32[]{:S(2)}) collective-permute-start(bf16[2,16,2048]{2,1,0:T(8,128)(2,1)S(1)} %get-tuple-element.67), channel_id=1, source_target_pairs={{0,2},{1,3},{2,0},{3,1},{4,6},{5,7},{6,4},{7,5},{8,10},{9,11},{10,... | collective-permute-start | bytes 393224 | tf_op jit(solution)/shard_map/ppermute | solution.py:330
  82.3 8.7 %collective-permute-start.27 = (bf16[2,16,2048]{2,1,0:T(8,128)(2,1)S(1)}, bf16[2,16,2048]{2,1,0:T(8,128)(2,1)S(1)}, u32[]{:S(2)}, u32[]{:S(2)}) collective-permute-start(bf16[2,16,2048]{2,1,0:T(8,128)(2,1)S(1)} %get-tuple-element.68), channel_id=1, source_target_pairs={{0,3},{1,2},{2,1},{3,0},{4,7},{5,6},{6,5},{7,4},{8,11},{9,10},{10,... | collective-permute-start | bytes 393224 | tf_op jit(solution)/shard_map/ppermute | solution.py:330
  (1 other events, 0.9 us)

commit v6 on v5

--- a/solution.py
+++ b/solution.py
@@ -233,8 +233,11 @@
     return matrix_ref[a * rows : (a + 1) * rows]
 
 
-def middle_kernel(place_ref, grad_ref, *refs):
-    matrices, (sum_ref, moved_ref) = refs[:GROUP], refs[GROUP:]
+def middle_kernel(place_ref, grad_ref, active_ref, *refs):
+    matrices, sum_ref, actives = refs[:GROUP], refs[GROUP], refs[GROUP + 1 : 2 * GROUP + 1]
+    moved_ref = refs[2 * GROUP + 1]
+    for j, out_ref in enumerate(actives):
+        out_ref[...] = active_ref[block_rows(place_ref, "part", j, out_ref.shape[0]), :]
     fill_plane(moved_ref, 0, grad_ref[...])
     add_taps(place_ref, sum_ref, moved_ref, matrices, (0,), lambda ref: third(ref, 1))
 
@@ -280,7 +283,7 @@
 
 
 def pair_kernel(place_ref, own_ref, *refs):
-    halves, active_ref, outs, sum_ref = refs[:4], refs[4], refs[5 : 5 + GROUP], refs[5 + GROUP]
+    halves, outs, sum_ref = refs[:4], refs[4 : 4 + GROUP], refs[4 + GROUP]
     half = halves[0].shape[0]
     for k in range(2):
         rows = slice(k * half, (k + 1) * half)
@@ -290,18 +293,19 @@
             + halves[2 + k][...].astype(jnp.float32)
         )
     for j, out_ref in enumerate(outs):
-        block = block_rows(place_ref, "part", j, out_ref.shape[1])
-        out_ref[0] = active_ref[block, :]
-        out_ref[1] = sum_ref[block, :].astype(out_ref.dtype)
+        block = block_rows(place_ref, "part", j, out_ref.shape[0])
+        out_ref[...] = sum_ref[block, :].astype(out_ref.dtype)
 
 
 def close_kernel(place_ref, *refs):
-    pairs, outs = refs[:GROUP], refs[GROUP:]
-    for j, pair_ref in enumerate(pairs):
-        for k, out_ref in enumerate(outs):
-            channels, _, height, breadth = out_ref.shape
-            value = pair_ref[k].astype(jnp.float32).reshape(channels, height, breadth)
-            out_ref[:, partner_plane(place_ref, j)] = value.astype(out_ref.dtype)
+    pieces, outs = refs[: 2 * GROUP], refs[2 * GROUP :]
+    for k, out_ref in enumerate(outs):
+        channels, _, height, breadth = out_ref.shape
+        for j in range(GROUP):
+            value = pieces[k * GROUP + j][...].astype(jnp.float32)
+            out_ref[:, partner_plane(place_ref, j)] = value.reshape(
+                channels, height, breadth
+            ).astype(out_ref.dtype)
 
 
 def total_kernel(place_ref, parts_ref, out_ref, *, scale):
@@ -413,16 +417,18 @@
     def moved(planes):
         return pltpu.VMEM((3, rows, planes * (plane + 2 * BREADTH)), bf16)
 
-    (middle,) = call(
+    middle, *actives = call(
         middle_kernel,
-        [((in_total, plane), f32)],
+        [((in_total, plane), f32)] + [((out_local, plane), bf16)] * GROUP,
         "middle",
         place,
         grad,
+        active,
         *matrices,
         scratch=[moved(1)],
         flops=2 * 9 * rows * in_total * plane,
     )
+    actives = swapped(actives, "part")
     sums, sums_1, sums_2, sums_3 = call(
         functools.partial(filter_kernel, **ends),
         [((in_total, taps), bf16)] * GROUP,
@@ -431,7 +437,7 @@
         field,
         grad,
         *sides,
-        unread=[middle],
+        unread=[middle, *actives[1:]],
         scratch=[moved(3)],
     )
     sums_3, sums_1 = swap(sums_3, "part", 1), swap(sums_1, "part", 1)
@@ -481,11 +487,10 @@
     )
     pairs = call(
         pair_kernel,
-        [((2, in_local, plane), bf16)] * GROUP,
+        [((in_local, plane), bf16)] * GROUP,
         "pairs",
         place,
         *(own, low_1, high_1, low_3, high_3),
-        active,
         scratch=[pltpu.VMEM((depth, plane), f32)],
     )
     pairs = swapped(pairs, "part")
@@ -501,6 +506,7 @@
         [((in_local, planes, height, breadth), bf16)] * 2,
         "close",
         place,
+        *actives,
         *pairs,
     )
     return (

time: 93.1 us -> 92.8 us (level)
  waiting for transfers between devices: 40 us -> 30.8 us
  starting transfers between devices: 35.7 us -> 43.8 us
    ppermute x4, waiting for transfers between devices: 14.3 us -> 4.6 us  [shifted(): lax.ppermute(value, DEPTH, [(at[i], at[(i + by) % count]) for i in range(...]
    ppermute x25 -> x28, starting transfers between devices: 28.3 us -> 35 us  [swap(): lax.ppermute(value, axis, [(i, i ^ j) for i in range(lax.axis_size(axis))])]
    all_to_all x1, starting transfers between devices: 3.53 us -> 4.95 us  [body(): lax.all_to_all(sums.reshape(spaces, in_total // spaces, taps), 'space', s...]
    ppermute x25 -> x28, waiting for transfers between devices: 25.7 us -> 26.2 us  [swap(): lax.ppermute(value, axis, [(i, i ^ j) for i in range(lax.axis_size(axis))])]
  transfers between devices with their start and end apart: 30 -> 33, of which waited for: 15 -> 14; matrix products, arithmetic and copies ran while one was open for 0% -> 0% of each run, Pallas kernels for 8% -> 8%
where the time goes in v6:
time: 92.8 us; the launch traced here: 91.8 us
  starting transfers between devices  43.8 us (47%)
  waiting for transfers between devices  30.8 us (33%)
  Pallas kernels  13.6 us (15%)
  local copies, waits for them, and re-layouts  2.83 us (3%)
    ppermute x28, starting transfers between devices, swap(): lax.ppermute(value, axis, [(i, i ^ j) for i in range(lax.axis_size(axis))])  35 us
    ppermute x28, waiting for transfers between devices, swap(): lax.ppermute(value, axis, [(i, i ^ j) for i in range(lax.axis_size(axis))])  26.2 us
    pallas_call x17, Pallas kernels, call(): pl.pallas_call(run, in_specs=[pl.BlockSpec(memory_space=pltpu.SMEM)] + [p...  13.6 us
    all_to_all x1, starting transfers between devices, body(): lax.all_to_all(sums.reshape(spaces, in_total // spaces, taps), 'space', s...  4.95 us
    ppermute x4, waiting for transfers between devices, shifted(): lax.ppermute(value, DEPTH, [(at[i], at[(i + by) % count]) for i in range(...  4.6 us
    ppermute x4, starting transfers between devices, shifted(): lax.ppermute(value, DEPTH, [(at[i], at[(i + by) % count]) for i in range(...  3.85 us
    unnamed x6, local copies, waits for them, and re-layouts  2.83 us
  transfers between devices with their start and end apart: 33, of which 14 were waited for; matrix products, arithmetic and copies ran while one was open for 0% of the time, Pallas kernels for 8%

profile of v6, /device:TPU:1, one launch (start us, length us, event | category | flops | bytes accessed | tf_op | source)
XLA Modules:
  0.0 91.8 jit_solution(10417106761901382041)
XLA Ops:
  1.7 3.3 %collective-permute-start = (bf16[16,2048]{1,0:T(8,128)(2,1)S(1)}, bf16[16,2048]{1,0:T(8,128)(2,1)S(1)}, u32[]{:S(2)}, u32[]{:S(2)}) collective-permute-start(bf16[16,2048]{1,0:T(8,128)(2,1)S(1)} %get-tuple-element.43), channel_id=1, source_target_pairs={{0,1},{1,0},{2,3},{3,2},{4,5},{5,4},{6,7},{7,6},{8,9},{9,8},{10,11... | collective-permute-start | bytes 196616 | tf_op jit(solution)/shard_map/ppermute | solution.py:334
  5.0 1.7 %collective-permute-start.2 = (bf16[16,2048]{1,0:T(8,128)(2,1)S(1)}, bf16[16,2048]{1,0:T(8,128)(2,1)S(1)}, u32[]{:S(2)}, u32[]{:S(2)}) collective-permute-start(bf16[16,2048]{1,0:T(8,128)(2,1)S(1)} %get-tuple-element.45), channel_id=1, source_target_pairs={{0,3},{1,2},{2,1},{3,0},{4,7},{5,6},{6,5},{7,4},{8,11},{9,10},{10,... | collective-permute-start | bytes 196616 | tf_op jit(solution)/shard_map/ppermute | solution.py:334
  8.8 1.5 %collective-permute-done.2.refs_3_ = bf16[16,2048]{1,0:T(8,128)(2,1)S(1)} collective-permute-done((bf16[16,2048]{1,0:T(8,128)(2,1)S(1)}, bf16[16,2048]{1,0:T(8,128)(2,1)S(1)}, u32[]{:S(2)}, u32[]{:S(2)}) %collective-permute-start.2) | collective-permute-done | bytes 65568 | tf_op jit(solution)/shard_map/ppermute | solution.py:334
  10.3 1.1 %collective-permute-start.4 = (bf16[64,2048]{1,0:T(8,128)(2,1)S(1)}, bf16[64,2048]{1,0:T(8,128)(2,1)S(1)}, u32[]{:S(2)}, u32[]{:S(2)}) collective-permute-start(bf16[64,2048]{1,0:T(8,128)(2,1)S(1)} %order.1.refs_0_), channel_id=1, source_target_pairs={{0,12},{4,8},{8,4},{12,0},{1,13},{5,9},{9,5},{13,1},{2,14},{6,10},... | collective-permute-start | bytes 786440 | tf_op jit(solution)/shard_map/ppermute | solution.py:334
  11.4 1.7 %collective-permute-start.9 = (bf16[432,256]{1,0:T(8,128)(2,1)S(1)}, bf16[432,256]{1,0:T(8,128)(2,1)S(1)}, u32[]{:S(2)}, u32[]{:S(2)}) collective-permute-start(bf16[432,256]{1,0:T(8,128)(2,1)S(1)} %get-tuple-element.46.refs_4_.refs_5_.refs_1_.refs_2_.refs_3_), channel_id=1, source_target_pairs={{0,3},{1,2},{2,1},{3,0},{4,7},{5,6},{6,5},{7,4},{8,11},{9,10},{10,... | collective-permute-start | bytes 663560 | tf_op jit(solution)/shard_map/ppermute | solution.py:334
  13.6 5.7 %collective-permute-done.4.refs_1_.refs_2_ = bf16[64,2048]{1,0:T(8,128)(2,1)S(1)} collective-permute-done((bf16[64,2048]{1,0:T(8,128)(2,1)S(1)}, bf16[64,2048]{1,0:T(8,128)(2,1)S(1)}, u32[]{:S(2)}, u32[]{:S(2)}) %collective-permute-start.4) | collective-permute-done | bytes 262176 | tf_op jit(solution)/shard_map/ppermute | solution.py:334
  19.3 1.2 %collective-permute-start.5 = (bf16[32,2048]{1,0:T(8,128)(2,1)S(1)}, bf16[32,2048]{1,0:T(8,128)(2,1)S(1)}, u32[]{:S(2)}, u32[]{:S(2)}) collective-permute-start(bf16[32,2048]{1,0:T(8,128)(2,1)S(1)} %get-tuple-element.47), channel_id=1, source_target_pairs={{0,12},{4,8},{8,4},{12,0},{1,13},{5,9},{9,5},{13,1},{2,14},{6,10},... | collective-permute-start | bytes 393224 | tf_op jit(solution)/shard_map/ppermute | solution.py:334
  20.6 1.6 %collective-permute-start.10 = (bf16[16,2048]{1,0:T(8,128)(2,1)S(1)}, bf16[16,2048]{1,0:T(8,128)(2,1)S(1)}, u32[]{:S(2)}, u32[]{:S(2)}) collective-permute-start(bf16[16,2048]{1,0:T(8,128)(2,1)S(1)} %get-tuple-element.50), channel_id=1, source_target_pairs={{0,1},{1,0},{2,3},{3,2},{4,5},{5,4},{6,7},{7,6},{8,9},{9,8},{10,11... | collective-permute-start | bytes 196616 | tf_op jit(solution)/shard_map/ppermute | solution.py:334
  22.2 1.9 %collective-permute-done.8.refs_7_.refs_3_.refs_4_.refs_5_ = bf16[432,256]{1,0:T(8,128)(2,1)S(1)} collective-permute-done((bf16[432,256]{1,0:T(8,128)(2,1)S(1)}, bf16[432,256]{1,0:T(8,128)(2,1)S(1)}, u32[]{:S(2)}, u32[]{:S(2)}) %collective-permute-start.8) | collective-permute-done | bytes 221216 | tf_op jit(solution)/shard_map/ppermute | solution.py:334
  24.1 1.1 %collective-permute-start.11 = (bf16[16,2048]{1,0:T(8,128)(2,1)S(1)}, bf16[16,2048]{1,0:T(8,128)(2,1)S(1)}, u32[]{:S(2)}, u32[]{:S(2)}) collective-permute-start(bf16[16,2048]{1,0:T(8,128)(2,1)S(1)} %get-tuple-element.51), channel_id=1, source_target_pairs={{0,2},{1,3},{2,0},{3,1},{4,6},{5,7},{6,4},{7,5},{8,10},{9,11},{10,... | collective-permute-start | bytes 196616 | tf_op jit(solution)/shard_map/ppermute | solution.py:334
  26.2 1.0 %after.1 = (bf16[256,2048]{1,0:T(8,128)(2,1)S(1)}, bf16[64,2048]{1,0:T(8,128)(2,1)S(1)}) custom-call(s32[1]{0:T(128)} %bitcast.place_ref, bf16[64,2048]{1,0:T(8,128)(2,1)S(1)} %order.1.refs_0_, bf16[64,2048]{1,0:T(8,128)(2,1)S(1)} %collective-permute-done.3.refs_0_.refs_1_, bf16[64,2048]{1,0:T(8,128)(2,1)S(1)} %collective-permute-done.4.refs_1_.refs_2_, ...), custom_call_target="tpu_custom_call" | custom-call | flops 1 | bytes 1 | tf_op jit(solution)/shard_map/after/pallas_call | solution.py:81
  27.2 2.6 %collective-permute-done.12.refs_7_.refs_6_ = bf16[16,2048]{1,0:T(8,128)(2,1)S(1)} collective-permute-done((bf16[16,2048]{1,0:T(8,128)(2,1)S(1)}, bf16[16,2048]{1,0:T(8,128)(2,1)S(1)}, u32[]{:S(2)}, u32[]{:S(2)}) %collective-permute-start.12) | collective-permute-done | bytes 65568 | tf_op jit(solution)/shard_map/ppermute | solution.py:334
  32.6 2.4 %collective-permute-done.13.refs_1_ = bf16[64,2048]{1,0:T(8,128)(2,1)S(1)} collective-permute-done((bf16[64,2048]{1,0:T(8,128)(2,1)S(1)}, bf16[64,2048]{1,0:T(8,128)(2,1)S(1)}, u32[]{:S(2)}, u32[]{:S(2)}) %collective-permute-start.13) | collective-permute-done | bytes 262176 | tf_op jit(solution)/shard_map/ppermute | solution.py:330
  35.0 2.2 %collective-permute-done.14.refs_2_ = bf16[64,2048]{1,0:T(8,128)(2,1)S(1)} collective-permute-done((bf16[64,2048]{1,0:T(8,128)(2,1)S(1)}, bf16[64,2048]{1,0:T(8,128)(2,1)S(1)}, u32[]{:S(2)}, u32[]{:S(2)}) %collective-permute-start.14) | collective-permute-done | bytes 262176 | tf_op jit(solution)/shard_map/ppermute | solution.py:330
  37.5 3.0 %collective-permute-start.19 = (bf16[64,2048]{1,0:T(8,128)(2,1)S(1)}, bf16[64,2048]{1,0:T(8,128)(2,1)S(1)}, u32[]{:S(2)}, u32[]{:S(2)}) collective-permute-start(bf16[64,2048]{1,0:T(8,128)(2,1)S(1)} %get-tuple-element.55.refs_0_.refs_1_), channel_id=1, source_target_pairs={{2,240},{3,2},{1,3},{0,1},{16,0},{17,16},{19,17},{18,19},{34,18},{... | collective-permute-start | bytes 786440 | tf_op jit(solution)/shard_map/ppermute | solution.py:330
  40.5 1.5 %middle.1 = (f32[256,2048]{1,0:T(8,128)S(1)}, bf16[16,2048]{1,0:T(8,128)(2,1)S(1)}, bf16[16,2048]{1,0:T(8,128)(2,1)S(1)}, bf16[16,2048]{1,0:T(8,128)(2,1)S(1)}, bf16[16,2048]{1,0:T(8,128)(2,1)S(1)}) custom-call(s32[1]{0:T(128)} %bitcast.place_ref, bf16[64,2048]{1,0:T(8,128)(2,1)S(1)} %get-tuple-element.55.refs_0_.refs_1_, ...), custom_call_target="tpu_custom_call" | custom-call | flops 603979776 | bytes 1 | tf_op jit(solution)/shard_map/middle/pallas_call | solution.py:81
  42.1 8.0 %collective-permute-start.16 = (bf16[16,2048]{1,0:T(8,128)(2,1)S(1)}, bf16[16,2048]{1,0:T(8,128)(2,1)S(1)}, u32[]{:S(2)}, u32[]{:S(2)}) collective-permute-start(bf16[16,2048]{1,0:T(8,128)(2,1)S(1)} %get-tuple-element.59), channel_id=1, source_target_pairs={{0,2},{1,3},{2,0},{3,1},{4,6},{5,7},{6,4},{7,5},{8,10},{9,11},{10,... | collective-permute-start | bytes 196616 | tf_op jit(solution)/shard_map/ppermute | solution.py:334
  50.1 3.0 %collective-permute-done.16.refs_6_.refs_2_ = bf16[16,2048]{1,0:T(8,128)(2,1)S(1)} collective-permute-done((bf16[16,2048]{1,0:T(8,128)(2,1)S(1)}, bf16[16,2048]{1,0:T(8,128)(2,1)S(1)}, u32[]{:S(2)}, u32[]{:S(2)}) %collective-permute-start.16) | collective-permute-done | bytes 65568 | tf_op jit(solution)/shard_map/ppermute | solution.py:334
  53.1 1.7 %collective-permute-done.17.refs_7_.refs_3_ = bf16[16,2048]{1,0:T(8,128)(2,1)S(1)} collective-permute-done((bf16[16,2048]{1,0:T(8,128)(2,1)S(1)}, bf16[16,2048]{1,0:T(8,128)(2,1)S(1)}, u32[]{:S(2)}, u32[]{:S(2)}) %collective-permute-start.17) | collective-permute-done | bytes 65568 | tf_op jit(solution)/shard_map/ppermute | solution.py:334
  54.8 2.9 %filter_sums.1 = (bf16[256,432]{1,0:T(8,128)(2,1)S(1)}, bf16[256,432]{1,0:T(8,128)(2,1)S(1)}, bf16[256,432]{1,0:T(8,128)(2,1)S(1)}, bf16[256,432]{1,0:T(8,128)(2,1)S(1)}) custom-call(s32[1]{0:T(128)} %bitcast.place_ref, bf16[256,2048]{1,0:T(8,128)(2,1)S(1)} %get-tuple-element.49.refs_0_, bf16[64,2048]{1,0:T(8,128)(2,1)S(1)} %get-tuple-element.55.refs_0_.refs_1_, ...), custom_call_target="tpu_custom_call" | custom-call | flops 1 | bytes 1 | tf_op jit(solution)/shard_map/filter_sums/pallas_call | solution.py:81
  58.3 2.9 %input_sums.1 = (f32[64,2048]{1,0:T(8,128)S(1)}, bf16[32,2048]{1,0:T(8,128)(2,1)S(1)}, bf16[32,2048]{1,0:T(8,128)(2,1)S(1)}, bf16[32,2048]{1,0:T(8,128)(2,1)S(1)...) custom-call(s32[1]{0:T(128)} %bitcast.place_ref, ...), custom_call_target="tpu_custom_call" | custom-call | flops 1 | bytes 1 | tf_op jit(solution)/shard_map/input_sums/pallas_call | solution.py:81
  62.9 1.6 %collective-permute-start.31 = (bf16[256,432]{1,0:T(8,128)(2,1)S(1)}, bf16[256,432]{1,0:T(8,128)(2,1)S(1)}, u32[]{:S(2)}, u32[]{:S(2)}) collective-permute-start(bf16[256,432]{1,0:T(8,128)(2,1)S(1)} %lift.1.refs_4_), channel_id=1, source_target_pairs={{0,2},{1,3},{2,0},{3,1},{4,6},{5,7},{6,4},{7,5},{8,10},{9,11},{10,... | collective-permute-start | bytes 663560 | tf_op jit(solution)/shard_map/ppermute | solution.py:334
  65.1 2.0 %collective-permute-start.27 = (bf16[32,2048]{1,0:T(8,128)(2,1)S(1)}, bf16[32,2048]{1,0:T(8,128)(2,1)S(1)}, u32[]{:S(2)}, u32[]{:S(2)}) collective-permute-start(bf16[32,2048]{1,0:T(8,128)(2,1)S(1)} %get-tuple-element.74), channel_id=1, source_target_pairs={{0,12},{4,8},{8,4},{12,0},{1,13},{5,9},{9,5},{13,1},{2,14},{6,10},... | collective-permute-start | bytes 393224 | tf_op jit(solution)/shard_map/ppermute | solution.py:334
  67.6 1.7 %collective-permute-start.26 = (bf16[32,2048]{1,0:T(8,128)(2,1)S(1)}, bf16[32,2048]{1,0:T(8,128)(2,1)S(1)}, u32[]{:S(2)}, u32[]{:S(2)}) collective-permute-start(bf16[32,2048]{1,0:T(8,128)(2,1)S(1)} %get-tuple-element.73), channel_id=1, source_target_pairs={{0,12},{4,8},{8,4},{12,0},{1,13},{5,9},{9,5},{13,1},{2,14},{6,10},... | collective-permute-start | bytes 393224 | tf_op jit(solution)/shard_map/ppermute | solution.py:334
  70.1 1.5 %collective-permute-done.25.refs_2_.refs_4_ = bf16[32,2048]{1,0:T(8,128)(2,1)S(1)} collective-permute-done((bf16[32,2048]{1,0:T(8,128)(2,1)S(1)}, bf16[32,2048]{1,0:T(8,128)(2,1)S(1)}, u32[]{:S(2)}, u32[]{:S(2)}) %collective-permute-start.25) | collective-permute-done | bytes 131104 | tf_op jit(solution)/shard_map/ppermute | solution.py:334
  71.7 1.9 %collective-permute-done.26.refs_3_.refs_5_ = bf16[32,2048]{1,0:T(8,128)(2,1)S(1)} collective-permute-done((bf16[32,2048]{1,0:T(8,128)(2,1)S(1)}, bf16[32,2048]{1,0:T(8,128)(2,1)S(1)}, u32[]{:S(2)}, u32[]{:S(2)}) %collective-permute-start.26) | collective-permute-done | bytes 131104 | tf_op jit(solution)/shard_map/ppermute | solution.py:334
  74.3 5.0 %all-to-all-start = ((bf16[16,16,432]{2,1,0:T(8,128)(2,1)}), bf16[16,16,432]{2,1,0:T(8,128)(2,1)S(1)}, u32[]{:S(2)}, u32[]{:S(2)}) async-start(bf16[16,16,432]{2,1,0:T(8,128)(2,1)} %bitcast.6), calls=%async_computation | async-start | bytes 524288 | tf_op jit(solution)/shard_map/all_to_all | solution.py:481
  79.4 3.4 %collective-permute-start.28 = (bf16[16,2048]{1,0:T(8,128)(2,1)S(1)}, bf16[16,2048]{1,0:T(8,128)(2,1)S(1)}, u32[]{:S(2)}, u32[]{:S(2)}) collective-permute-start(bf16[16,2048]{1,0:T(8,128)(2,1)S(1)} %get-tuple-element.76), channel_id=1, source_target_pairs={{0,1},{1,0},{2,3},{3,2},{4,5},{5,4},{6,7},{7,6},{8,9},{9,8},{10,11... | collective-permute-start | bytes 196616 | tf_op jit(solution)/shard_map/ppermute | solution.py:334
  82.9 1.7 %collective-permute-start.30 = (bf16[16,2048]{1,0:T(8,128)(2,1)S(1)}, bf16[16,2048]{1,0:T(8,128)(2,1)S(1)}, u32[]{:S(2)}, u32[]{:S(2)}) collective-permute-start(bf16[16,2048]{1,0:T(8,128)(2,1)S(1)} %get-tuple-element.78), channel_id=1, source_target_pairs={{0,3},{1,2},{2,1},{3,0},{4,7},{5,6},{6,5},{7,4},{8,11},{9,10},{10,... | collective-permute-start | bytes 196616 | tf_op jit(solution)/shard_map/ppermute | solution.py:334
  84.6 3.0 %collective-permute-done.29.refs_6_ = bf16[16,2048]{1,0:T(8,128)(2,1)S(1)} collective-permute-done((bf16[16,2048]{1,0:T(8,128)(2,1)S(1)}, bf16[16,2048]{1,0:T(8,128)(2,1)S(1)}, u32[]{:S(2)}, u32[]{:S(2)}) %collective-permute-start.29) | collective-permute-done | bytes 65568 | tf_op jit(solution)/shard_map/ppermute | solution.py:334
  87.6 2.4 %collective-permute-done.30.refs_7_ = bf16[16,2048]{1,0:T(8,128)(2,1)S(1)} collective-permute-done((bf16[16,2048]{1,0:T(8,128)(2,1)S(1)}, bf16[16,2048]{1,0:T(8,128)(2,1)S(1)}, u32[]{:S(2)}, u32[]{:S(2)}) %collective-permute-start.30) | collective-permute-done | bytes 65568 | tf_op jit(solution)/shard_map/ppermute | solution.py:334
  90.0 1.0 %close.1 = (bf16[16,4,16,128]{3,2,1,0:T(8,128)(2,1)}, bf16[16,4,16,128]{3,2,1,0:T(8,128)(2,1)}) custom-call(s32[1]{0:T(128)} %bitcast.place_ref, bf16[16,2048]{1,0:T(8,128)(2,1)S(1)} %get-tuple-element.57.refs_0_, bf16[16,2048]{1,0:T(8,128)(2,1)S(1)} %collective-permute-done.15.refs_5_.refs_1_, bf16[16,2048]{1,0:T(8,128)(2,1)S(1)} %collective-permute-done.16.refs_6_.refs_2_, ...), custom_call_target="tpu_custom_call" | custom-call | flops 1 | bytes 1 | tf_op jit(solution)/shard_map/close/pallas_call | solution.py:81
  (57 shorter events, 13.8 us)
Async XLA Ops:
  1.7 7.1 %collective-permute-start = (bf16[16,2048]{1,0:T(8,128)(2,1)S(1)}, bf16[16,2048]{1,0:T(8,128)(2,1)S(1)}, u32[]{:S(2)}, u32[]{:S(2)}) collective-permute-start(bf16[16,2048]{1,0:T(8,128)(2,1)S(1)} %get-tuple-element.43), channel_id=1, source_target_pairs={{0,1},{1,0},{2,3},{3,2},{4,5},{5,4},{6,7},{7,6},{8,9},{9,8},{10,11... | collective-permute-start | bytes 196616 | tf_op jit(solution)/shard_map/ppermute | solution.py:334
  5.0 3.8 %collective-permute-start.1 = (bf16[16,2048]{1,0:T(8,128)(2,1)S(1)}, bf16[16,2048]{1,0:T(8,128)(2,1)S(1)}, u32[]{:S(2)}, u32[]{:S(2)}) collective-permute-start(bf16[16,2048]{1,0:T(8,128)(2,1)S(1)} %get-tuple-element.44), channel_id=1, source_target_pairs={{0,2},{1,3},{2,0},{3,1},{4,6},{5,7},{6,4},{7,5},{8,10},{9,11},{10,... | collective-permute-start | bytes 196616 | tf_op jit(solution)/shard_map/ppermute | solution.py:334
  5.0 5.2 %collective-permute-start.2 = (bf16[16,2048]{1,0:T(8,128)(2,1)S(1)}, bf16[16,2048]{1,0:T(8,128)(2,1)S(1)}, u32[]{:S(2)}, u32[]{:S(2)}) collective-permute-start(bf16[16,2048]{1,0:T(8,128)(2,1)S(1)} %get-tuple-element.45), channel_id=1, source_target_pairs={{0,3},{1,2},{2,1},{3,0},{4,7},{5,6},{6,5},{7,4},{8,11},{9,10},{10,... | collective-permute-start | bytes 196616 | tf_op jit(solution)/shard_map/ppermute | solution.py:334
  10.3 9.0 %collective-permute-start.4 = (bf16[64,2048]{1,0:T(8,128)(2,1)S(1)}, bf16[64,2048]{1,0:T(8,128)(2,1)S(1)}, u32[]{:S(2)}, u32[]{:S(2)}) collective-permute-start(bf16[64,2048]{1,0:T(8,128)(2,1)S(1)} %order.1.refs_0_), channel_id=1, source_target_pairs={{0,12},{4,8},{8,4},{12,0},{1,13},{5,9},{9,5},{13,1},{2,14},{6,10},... | collective-permute-start | bytes 786440 | tf_op jit(solution)/shard_map/ppermute | solution.py:334
  11.4 7.9 %collective-permute-start.3 = (bf16[64,2048]{1,0:T(8,128)(2,1)S(1)}, bf16[64,2048]{1,0:T(8,128)(2,1)S(1)}, u32[]{:S(2)}, u32[]{:S(2)}) collective-permute-start(bf16[64,2048]{1,0:T(8,128)(2,1)S(1)} %order.1.refs_0_), channel_id=1, source_target_pairs={{0,4},{4,0},{8,12},{12,8},{1,5},{5,1},{9,13},{13,9},{2,6},{6,2},{1... | collective-permute-start | bytes 786440 | tf_op jit(solution)/shard_map/ppermute | solution.py:334
  11.4 9.1 %collective-permute-start.9 = (bf16[432,256]{1,0:T(8,128)(2,1)S(1)}, bf16[432,256]{1,0:T(8,128)(2,1)S(1)}, u32[]{:S(2)}, u32[]{:S(2)}) collective-permute-start(bf16[432,256]{1,0:T(8,128)(2,1)S(1)} %get-tuple-element.46.refs_4_.refs_5_.refs_1_.refs_2_.refs_3_), channel_id=1, source_target_pairs={{0,3},{1,2},{2,1},{3,0},{4,7},{5,6},{6,5},{7,4},{8,11},{9,10},{10,... | collective-permute-start | bytes 663560 | tf_op jit(solution)/shard_map/ppermute | solution.py:334
  13.1 11.0 %collective-permute-start.8 = (bf16[432,256]{1,0:T(8,128)(2,1)S(1)}, bf16[432,256]{1,0:T(8,128)(2,1)S(1)}, u32[]{:S(2)}, u32[]{:S(2)}) collective-permute-start(bf16[432,256]{1,0:T(8,128)(2,1)S(1)} %get-tuple-element.46.refs_4_.refs_5_.refs_1_.refs_2_.refs_3_), channel_id=1, source_target_pairs={{0,2},{1,3},{2,0},{3,1},{4,6},{5,7},{6,4},{7,5},{8,10},{9,11},{10,... | collective-permute-start | bytes 663560 | tf_op jit(solution)/shard_map/ppermute | solution.py:334
  13.6 11.7 %collective-permute-start.7 = (bf16[432,256]{1,0:T(8,128)(2,1)S(1)}, bf16[432,256]{1,0:T(8,128)(2,1)S(1)}, u32[]{:S(2)}, u32[]{:S(2)}) collective-permute-start(bf16[432,256]{1,0:T(8,128)(2,1)S(1)} %get-tuple-element.46.refs_4_.refs_5_.refs_1_.refs_2_.refs_3_), channel_id=1, source_target_pairs={{0,1},{1,0},{2,3},{3,2},{4,5},{5,4},{6,7},{7,6},{8,9},{9,8},{10,11... | collective-permute-start | bytes 663560 | tf_op jit(solution)/shard_map/ppermute | solution.py:334
  19.3 6.8 %collective-permute-start.5 = (bf16[32,2048]{1,0:T(8,128)(2,1)S(1)}, bf16[32,2048]{1,0:T(8,128)(2,1)S(1)}, u32[]{:S(2)}, u32[]{:S(2)}) collective-permute-start(bf16[32,2048]{1,0:T(8,128)(2,1)S(1)} %get-tuple-element.47), channel_id=1, source_target_pairs={{0,12},{4,8},{8,4},{12,0},{1,13},{5,9},{9,5},{13,1},{2,14},{6,10},... | collective-permute-start | bytes 393224 | tf_op jit(solution)/shard_map/ppermute | solution.py:334
  20.6 5.6 %collective-permute-start.6 = (bf16[32,2048]{1,0:T(8,128)(2,1)S(1)}, bf16[32,2048]{1,0:T(8,128)(2,1)S(1)}, u32[]{:S(2)}, u32[]{:S(2)}) collective-permute-start(bf16[32,2048]{1,0:T(8,128)(2,1)S(1)} %get-tuple-element.48), channel_id=1, source_target_pairs={{0,4},{4,0},{8,12},{12,8},{1,5},{5,1},{9,13},{13,9},{2,6},{6,2},{1... | collective-permute-start | bytes 393224 | tf_op jit(solution)/shard_map/ppermute | solution.py:334
  20.6 6.6 %collective-permute-start.10 = (bf16[16,2048]{1,0:T(8,128)(2,1)S(1)}, bf16[16,2048]{1,0:T(8,128)(2,1)S(1)}, u32[]{:S(2)}, u32[]{:S(2)}) collective-permute-start(bf16[16,2048]{1,0:T(8,128)(2,1)S(1)} %get-tuple-element.50), channel_id=1, source_target_pairs={{0,1},{1,0},{2,3},{3,2},{4,5},{5,4},{6,7},{7,6},{8,9},{9,8},{10,11... | collective-permute-start | bytes 196616 | tf_op jit(solution)/shard_map/ppermute | solution.py:334
  25.2 4.6 %collective-permute-start.12 = (bf16[16,2048]{1,0:T(8,128)(2,1)S(1)}, bf16[16,2048]{1,0:T(8,128)(2,1)S(1)}, u32[]{:S(2)}, u32[]{:S(2)}) collective-permute-start(bf16[16,2048]{1,0:T(8,128)(2,1)S(1)} %get-tuple-element.52), channel_id=1, source_target_pairs={{0,3},{1,2},{2,1},{3,0},{4,7},{5,6},{6,5},{7,4},{8,11},{9,10},{10,... | collective-permute-start | bytes 196616 | tf_op jit(solution)/shard_map/ppermute | solution.py:334
  30.8 4.2 %collective-permute-start.13 = (bf16[64,2048]{1,0:T(8,128)(2,1)S(1)}, bf16[64,2048]{1,0:T(8,128)(2,1)S(1)}, u32[]{:S(2)}, u32[]{:S(2)}) collective-permute-start(bf16[64,2048]{1,0:T(8,128)(2,1)S(1)} %before.1.refs_5_), channel_id=1, source_target_pairs={{2,240},{3,2},{1,3},{0,1},{16,0},{17,16},{19,17},{18,19},{34,18},{... | collective-permute-start | bytes 786440 | tf_op jit(solution)/shard_map/ppermute | solution.py:330
  31.7 5.5 %collective-permute-start.14 = (bf16[64,2048]{1,0:T(8,128)(2,1)S(1)}, bf16[64,2048]{1,0:T(8,128)(2,1)S(1)}, u32[]{:S(2)}, u32[]{:S(2)}) collective-permute-start(bf16[64,2048]{1,0:T(8,128)(2,1)S(1)} %get-tuple-element.53), channel_id=1, source_target_pairs={{2,3},{3,1},{1,0},{0,16},{16,17},{17,19},{19,18},{18,34},{34,35},{... | collective-permute-start | bytes 786440 | tf_op jit(solution)/shard_map/ppermute | solution.py:330
  37.5 17.3 %collective-permute-start.19 = (bf16[64,2048]{1,0:T(8,128)(2,1)S(1)}, bf16[64,2048]{1,0:T(8,128)(2,1)S(1)}, u32[]{:S(2)}, u32[]{:S(2)}) collective-permute-start(bf16[64,2048]{1,0:T(8,128)(2,1)S(1)} %get-tuple-element.55.refs_0_.refs_1_), channel_id=1, source_target_pairs={{2,240},{3,2},{1,3},{0,1},{16,0},{17,16},{19,17},{18,19},{34,18},{... | collective-permute-start | bytes 786440 | tf_op jit(solution)/shard_map/ppermute | solution.py:330
  40.5 14.3 %collective-permute-start.18 = (bf16[64,2048]{1,0:T(8,128)(2,1)S(1)}, bf16[64,2048]{1,0:T(8,128)(2,1)S(1)}, u32[]{:S(2)}, u32[]{:S(2)}) collective-permute-start(bf16[64,2048]{1,0:T(8,128)(2,1)S(1)} %get-tuple-element.55.refs_0_.refs_1_), channel_id=1, source_target_pairs={{2,3},{3,1},{1,0},{0,16},{16,17},{17,19},{19,18},{18,34},{34,35},{... | collective-permute-start | bytes 786440 | tf_op jit(solution)/shard_map/ppermute | solution.py:330
  42.0 8.1 %collective-permute-start.15 = (bf16[16,2048]{1,0:T(8,128)(2,1)S(1)}, bf16[16,2048]{1,0:T(8,128)(2,1)S(1)}, u32[]{:S(2)}, u32[]{:S(2)}) collective-permute-start(bf16[16,2048]{1,0:T(8,128)(2,1)S(1)} %get-tuple-element.58), channel_id=1, source_target_pairs={{0,1},{1,0},{2,3},{3,2},{4,5},{5,4},{6,7},{7,6},{8,9},{9,8},{10,11... | collective-permute-start | bytes 196616 | tf_op jit(solution)/shard_map/ppermute | solution.py:334
  42.1 11.1 %collective-permute-start.16 = (bf16[16,2048]{1,0:T(8,128)(2,1)S(1)}, bf16[16,2048]{1,0:T(8,128)(2,1)S(1)}, u32[]{:S(2)}, u32[]{:S(2)}) collective-permute-start(bf16[16,2048]{1,0:T(8,128)(2,1)S(1)} %get-tuple-element.59), channel_id=1, source_target_pairs={{0,2},{1,3},{2,0},{3,1},{4,6},{5,7},{6,4},{7,5},{8,10},{9,11},{10,... | collective-permute-start | bytes 196616 | tf_op jit(solution)/shard_map/ppermute | solution.py:334
  50.0 4.7 %collective-permute-start.17 = (bf16[16,2048]{1,0:T(8,128)(2,1)S(1)}, bf16[16,2048]{1,0:T(8,128)(2,1)S(1)}, u32[]{:S(2)}, u32[]{:S(2)}) collective-permute-start(bf16[16,2048]{1,0:T(8,128)(2,1)S(1)} %get-tuple-element.60), channel_id=1, source_target_pairs={{0,3},{1,2},{2,1},{3,0},{4,7},{5,6},{6,5},{7,4},{8,11},{9,10},{10,... | collective-permute-start | bytes 196616 | tf_op jit(solution)/shard_map/ppermute | solution.py:334
  57.7 5.1 %collective-permute-start.23 = (bf16[256,432]{1,0:T(8,128)(2,1)S(1)}, bf16[256,432]{1,0:T(8,128)(2,1)S(1)}, u32[]{:S(2)}, u32[]{:S(2)}) collective-permute-start(bf16[256,432]{1,0:T(8,128)(2,1)S(1)} %get-tuple-element.70), channel_id=1, source_target_pairs={{0,1},{1,0},{2,3},{3,2},{4,5},{5,4},{6,7},{7,6},{8,9},{9,8},{10,11... | collective-permute-start | bytes 663560 | tf_op jit(solution)/shard_map/ppermute | solution.py:334
  58.2 4.6 %collective-permute-start.24 = (bf16[256,432]{1,0:T(8,128)(2,1)S(1)}, bf16[256,432]{1,0:T(8,128)(2,1)S(1)}, u32[]{:S(2)}, u32[]{:S(2)}) collective-permute-start(bf16[256,432]{1,0:T(8,128)(2,1)S(1)} %get-tuple-element.71), channel_id=1, source_target_pairs={{0,1},{1,0},{2,3},{3,2},{4,5},{5,4},{6,7},{7,6},{8,9},{9,8},{10,11... | collective-permute-start | bytes 663560 | tf_op jit(solution)/shard_map/ppermute | solution.py:334
  61.2 6.0 %collective-permute-start.21 = (bf16[32,2048]{1,0:T(8,128)(2,1)S(1)}, bf16[32,2048]{1,0:T(8,128)(2,1)S(1)}, u32[]{:S(2)}, u32[]{:S(2)}) collective-permute-start(bf16[32,2048]{1,0:T(8,128)(2,1)S(1)} %get-tuple-element.67), channel_id=1, source_target_pairs={{0,12},{4,8},{8,4},{12,0},{1,13},{5,9},{9,5},{13,1},{2,14},{6,10},... | collective-permute-start | bytes 393224 | tf_op jit(solution)/shard_map/ppermute | solution.py:334
  61.9 5.2 %collective-permute-start.22 = (bf16[32,2048]{1,0:T(8,128)(2,1)S(1)}, bf16[32,2048]{1,0:T(8,128)(2,1)S(1)}, u32[]{:S(2)}, u32[]{:S(2)}) collective-permute-start(bf16[32,2048]{1,0:T(8,128)(2,1)S(1)} %get-tuple-element.68), channel_id=1, source_target_pairs={{0,4},{4,0},{8,12},{12,8},{1,5},{5,1},{9,13},{13,9},{2,6},{6,2},{1... | collective-permute-start | bytes 393224 | tf_op jit(solution)/shard_map/ppermute | solution.py:334
  62.9 10.7 %collective-permute-start.31 = (bf16[256,432]{1,0:T(8,128)(2,1)S(1)}, bf16[256,432]{1,0:T(8,128)(2,1)S(1)}, u32[]{:S(2)}, u32[]{:S(2)}) collective-permute-start(bf16[256,432]{1,0:T(8,128)(2,1)S(1)} %lift.1.refs_4_), channel_id=1, source_target_pairs={{0,2},{1,3},{2,0},{3,1},{4,6},{5,7},{6,4},{7,5},{8,10},{9,11},{10,... | collective-permute-start | bytes 663560 | tf_op jit(solution)/shard_map/ppermute | solution.py:334
  64.5 4.8 %collective-permute-start.20 = (bf16[32,2048]{1,0:T(8,128)(2,1)S(1)}, bf16[32,2048]{1,0:T(8,128)(2,1)S(1)}, u32[]{:S(2)}, u32[]{:S(2)}) collective-permute-start(bf16[32,2048]{1,0:T(8,128)(2,1)S(1)} %get-tuple-element.64), channel_id=1, source_target_pairs={{0,4},{4,0},{8,12},{12,8},{1,5},{5,1},{9,13},{13,9},{2,6},{6,2},{1... | collective-permute-start | bytes 393224 | tf_op jit(solution)/shard_map/ppermute | solution.py:334
  65.1 5.0 %collective-permute-start.27 = (bf16[32,2048]{1,0:T(8,128)(2,1)S(1)}, bf16[32,2048]{1,0:T(8,128)(2,1)S(1)}, u32[]{:S(2)}, u32[]{:S(2)}) collective-permute-start(bf16[32,2048]{1,0:T(8,128)(2,1)S(1)} %get-tuple-element.74), channel_id=1, source_target_pairs={{0,12},{4,8},{8,4},{12,0},{1,13},{5,9},{9,5},{13,1},{2,14},{6,10},... | collective-permute-start | bytes 393224 | tf_op jit(solution)/shard_map/ppermute | solution.py:334
  67.2 4.4 %collective-permute-start.25 = (bf16[32,2048]{1,0:T(8,128)(2,1)S(1)}, bf16[32,2048]{1,0:T(8,128)(2,1)S(1)}, u32[]{:S(2)}, u32[]{:S(2)}) collective-permute-start(bf16[32,2048]{1,0:T(8,128)(2,1)S(1)} %get-tuple-element.72), channel_id=1, source_target_pairs={{0,4},{4,0},{8,12},{12,8},{1,5},{5,1},{9,13},{13,9},{2,6},{6,2},{1... | collective-permute-start | bytes 393224 | tf_op jit(solution)/shard_map/ppermute | solution.py:334
  67.6 5.9 %collective-permute-start.26 = (bf16[32,2048]{1,0:T(8,128)(2,1)S(1)}, bf16[32,2048]{1,0:T(8,128)(2,1)S(1)}, u32[]{:S(2)}, u32[]{:S(2)}) collective-permute-start(bf16[32,2048]{1,0:T(8,128)(2,1)S(1)} %get-tuple-element.73), channel_id=1, source_target_pairs={{0,12},{4,8},{8,4},{12,0},{1,13},{5,9},{9,5},{13,1},{2,14},{6,10},... | collective-permute-start | bytes 393224 | tf_op jit(solution)/shard_map/ppermute | solution.py:334
  74.3 16.6 %all-to-all-start = ((bf16[16,16,432]{2,1,0:T(8,128)(2,1)}), bf16[16,16,432]{2,1,0:T(8,128)(2,1)S(1)}, u32[]{:S(2)}, u32[]{:S(2)}) async-start(bf16[16,16,432]{2,1,0:T(8,128)(2,1)} %bitcast.6), calls=%async_computation | async-start | bytes 524288 | tf_op jit(solution)/shard_map/all_to_all | solution.py:481
  79.4 5.2 %collective-permute-start.28 = (bf16[16,2048]{1,0:T(8,128)(2,1)S(1)}, bf16[16,2048]{1,0:T(8,128)(2,1)S(1)}, u32[]{:S(2)}, u32[]{:S(2)}) collective-permute-start(bf16[16,2048]{1,0:T(8,128)(2,1)S(1)} %get-tuple-element.76), channel_id=1, source_target_pairs={{0,1},{1,0},{2,3},{3,2},{4,5},{5,4},{6,7},{7,6},{8,9},{9,8},{10,11... | collective-permute-start | bytes 196616 | tf_op jit(solution)/shard_map/ppermute | solution.py:334
  82.9 4.7 %collective-permute-start.29 = (bf16[16,2048]{1,0:T(8,128)(2,1)S(1)}, bf16[16,2048]{1,0:T(8,128)(2,1)S(1)}, u32[]{:S(2)}, u32[]{:S(2)}) collective-permute-start(bf16[16,2048]{1,0:T(8,128)(2,1)S(1)} %get-tuple-element.77), channel_id=1, source_target_pairs={{0,2},{1,3},{2,0},{3,1},{4,6},{5,7},{6,4},{7,5},{8,10},{9,11},{10,... | collective-permute-start | bytes 196616 | tf_op jit(solution)/shard_map/ppermute | solution.py:334
  82.9 7.1 %collective-permute-start.30 = (bf16[16,2048]{1,0:T(8,128)(2,1)S(1)}, bf16[16,2048]{1,0:T(8,128)(2,1)S(1)}, u32[]{:S(2)}, u32[]{:S(2)}) collective-permute-start(bf16[16,2048]{1,0:T(8,128)(2,1)S(1)} %get-tuple-element.78), channel_id=1, source_target_pairs={{0,3},{1,2},{2,1},{3,0},{4,7},{5,6},{6,5},{7,4},{8,11},{9,10},{10,... | collective-permute-start | bytes 196616 | tf_op jit(solution)/shard_map/ppermute | solution.py:334
  (4 other events, 6.0 us)

commit v7 on v6

--- a/solution.py
+++ b/solution.py
@@ -437,7 +437,7 @@
         field,
         grad,
         *sides,
-        unread=[middle, *actives[1:]],
+        unread=[middle],
         scratch=[moved(3)],
     )
     sums_3, sums_1 = swap(sums_3, "part", 1), swap(sums_1, "part", 1)
@@ -449,7 +449,7 @@
         middle,
         *sides,
         *matrices,
-        unread=[sums],
+        unread=[sums, *actives[1:]],
         scratch=[moved(2), pltpu.VMEM((in_total, plane), f32)],
     )
     far_low, far_high = swap(far_low, "run", 1), swap(far_high, "run", 3)

time: 92.8 us -> 96.3 us (1.038)
  waiting for transfers between devices: 30.8 us -> 39.4 us
  starting transfers between devices: 43.8 us -> 38.4 us
    ppermute x4, waiting for transfers between devices: 4.6 us -> 14.3 us  [shifted(): lax.ppermute(value, DEPTH, [(at[i], at[(i + by) % count]) for i in range(...]
    ppermute x28, starting transfers between devices: 35 us -> 31 us  [swap(): lax.ppermute(value, axis, [(i, i ^ j) for i in range(lax.axis_size(axis))])]
    all_to_all x1, starting transfers between devices: 4.95 us -> 3.53 us  [body(): lax.all_to_all(sums.reshape(spaces, in_total // spaces, taps), 'space', s...]
    ppermute x28, waiting for transfers between devices: 26.2 us -> 25.1 us  [swap(): lax.ppermute(value, axis, [(i, i ^ j) for i in range(lax.axis_size(axis))])]
  transfers between devices with their start and end apart: 33 -> 33, of which waited for: 14 -> 18; matrix products, arithmetic and copies ran while one was open for 0% -> 0% of each run, Pallas kernels for 8% -> 8%
where the time goes in v7:
time: 96.3 us; the launch traced here: 95 us
  waiting for transfers between devices  39.4 us (41%)
  starting transfers between devices  38.4 us (40%)
  Pallas kernels  13.6 us (14%)
  local copies, waits for them, and re-layouts  2.83 us (3%)
    ppermute x28, starting transfers between devices, swap(): lax.ppermute(value, axis, [(i, i ^ j) for i in range(lax.axis_size(axis))])  31 us
    ppermute x28, waiting for transfers between devices, swap(): lax.ppermute(value, axis, [(i, i ^ j) for i in range(lax.axis_size(axis))])  25.1 us
    ppermute x4, waiting for transfers between devices, shifted(): lax.ppermute(value, DEPTH, [(at[i], at[(i + by) % count]) for i in range(...  14.3 us
    pallas_call x17, Pallas kernels, call(): pl.pallas_call(run, in_specs=[pl.BlockSpec(memory_space=pltpu.SMEM)] + [p...  13.6 us
    ppermute x4, starting transfers between devices, shifted(): lax.ppermute(value, DEPTH, [(at[i], at[(i + by) % count]) for i in range(...  3.85 us
    all_to_all x1, starting transfers between devices, body(): lax.all_to_all(sums.reshape(spaces, in_total // spaces, taps), 'space', s...  3.53 us
    unnamed x6, local copies, waits for them, and re-layouts  2.83 us
  transfers between devices with their start and end apart: 33, of which 18 were waited for; matrix products, arithmetic and copies ran while one was open for 0% of the time, Pallas kernels for 8%

profile of v7, /device:TPU:1, one launch (start us, length us, event | category | flops | bytes accessed | tf_op | source)
XLA Modules:
  0.0 95.0 jit_solution(8712569204303505234)
XLA Ops:
  1.7 3.3 %collective-permute-start = (bf16[16,2048]{1,0:T(8,128)(2,1)S(1)}, bf16[16,2048]{1,0:T(8,128)(2,1)S(1)}, u32[]{:S(2)}, u32[]{:S(2)}) collective-permute-start(bf16[16,2048]{1,0:T(8,128)(2,1)S(1)} %get-tuple-element.43), channel_id=1, source_target_pairs={{0,1},{1,0},{2,3},{3,2},{4,5},{5,4},{6,7},{7,6},{8,9},{9,8},{10,11... | collective-permute-start | bytes 196616 | tf_op jit(solution)/shard_map/ppermute | solution.py:334
  5.0 1.7 %collective-permute-start.2 = (bf16[16,2048]{1,0:T(8,128)(2,1)S(1)}, bf16[16,2048]{1,0:T(8,128)(2,1)S(1)}, u32[]{:S(2)}, u32[]{:S(2)}) collective-permute-start(bf16[16,2048]{1,0:T(8,128)(2,1)S(1)} %get-tuple-element.45), channel_id=1, source_target_pairs={{0,3},{1,2},{2,1},{3,0},{4,7},{5,6},{6,5},{7,4},{8,11},{9,10},{10,... | collective-permute-start | bytes 196616 | tf_op jit(solution)/shard_map/ppermute | solution.py:334
  8.8 1.5 %collective-permute-done.2.refs_3_ = bf16[16,2048]{1,0:T(8,128)(2,1)S(1)} collective-permute-done((bf16[16,2048]{1,0:T(8,128)(2,1)S(1)}, bf16[16,2048]{1,0:T(8,128)(2,1)S(1)}, u32[]{:S(2)}, u32[]{:S(2)}) %collective-permute-start.2) | collective-permute-done | bytes 65568 | tf_op jit(solution)/shard_map/ppermute | solution.py:334
  10.3 1.1 %collective-permute-start.4 = (bf16[64,2048]{1,0:T(8,128)(2,1)S(1)}, bf16[64,2048]{1,0:T(8,128)(2,1)S(1)}, u32[]{:S(2)}, u32[]{:S(2)}) collective-permute-start(bf16[64,2048]{1,0:T(8,128)(2,1)S(1)} %order.1.refs_0_), channel_id=1, source_target_pairs={{0,12},{4,8},{8,4},{12,0},{1,13},{5,9},{9,5},{13,1},{2,14},{6,10},... | collective-permute-start | bytes 786440 | tf_op jit(solution)/shard_map/ppermute | solution.py:334
  11.4 1.7 %collective-permute-start.9 = (bf16[432,256]{1,0:T(8,128)(2,1)S(1)}, bf16[432,256]{1,0:T(8,128)(2,1)S(1)}, u32[]{:S(2)}, u32[]{:S(2)}) collective-permute-start(bf16[432,256]{1,0:T(8,128)(2,1)S(1)} %get-tuple-element.46.refs_4_.refs_5_.refs_1_.refs_2_.refs_3_), channel_id=1, source_target_pairs={{0,3},{1,2},{2,1},{3,0},{4,7},{5,6},{6,5},{7,4},{8,11},{9,10},{10,... | collective-permute-start | bytes 663560 | tf_op jit(solution)/shard_map/ppermute | solution.py:334
  13.6 5.7 %collective-permute-done.4.refs_1_.refs_2_ = bf16[64,2048]{1,0:T(8,128)(2,1)S(1)} collective-permute-done((bf16[64,2048]{1,0:T(8,128)(2,1)S(1)}, bf16[64,2048]{1,0:T(8,128)(2,1)S(1)}, u32[]{:S(2)}, u32[]{:S(2)}) %collective-permute-start.4) | collective-permute-done | bytes 262176 | tf_op jit(solution)/shard_map/ppermute | solution.py:334
  19.3 1.2 %collective-permute-start.5 = (bf16[32,2048]{1,0:T(8,128)(2,1)S(1)}, bf16[32,2048]{1,0:T(8,128)(2,1)S(1)}, u32[]{:S(2)}, u32[]{:S(2)}) collective-permute-start(bf16[32,2048]{1,0:T(8,128)(2,1)S(1)} %get-tuple-element.47), channel_id=1, source_target_pairs={{0,12},{4,8},{8,4},{12,0},{1,13},{5,9},{9,5},{13,1},{2,14},{6,10},... | collective-permute-start | bytes 393224 | tf_op jit(solution)/shard_map/ppermute | solution.py:334
  20.6 1.6 %collective-permute-start.10 = (bf16[16,2048]{1,0:T(8,128)(2,1)S(1)}, bf16[16,2048]{1,0:T(8,128)(2,1)S(1)}, u32[]{:S(2)}, u32[]{:S(2)}) collective-permute-start(bf16[16,2048]{1,0:T(8,128)(2,1)S(1)} %get-tuple-element.50), channel_id=1, source_target_pairs={{0,1},{1,0},{2,3},{3,2},{4,5},{5,4},{6,7},{7,6},{8,9},{9,8},{10,11... | collective-permute-start | bytes 196616 | tf_op jit(solution)/shard_map/ppermute | solution.py:334
  22.2 1.9 %collective-permute-done.8.refs_7_.refs_3_.refs_4_.refs_5_ = bf16[432,256]{1,0:T(8,128)(2,1)S(1)} collective-permute-done((bf16[432,256]{1,0:T(8,128)(2,1)S(1)}, bf16[432,256]{1,0:T(8,128)(2,1)S(1)}, u32[]{:S(2)}, u32[]{:S(2)}) %collective-permute-start.8) | collective-permute-done | bytes 221216 | tf_op jit(solution)/shard_map/ppermute | solution.py:334
  24.1 1.1 %collective-permute-start.11 = (bf16[16,2048]{1,0:T(8,128)(2,1)S(1)}, bf16[16,2048]{1,0:T(8,128)(2,1)S(1)}, u32[]{:S(2)}, u32[]{:S(2)}) collective-permute-start(bf16[16,2048]{1,0:T(8,128)(2,1)S(1)} %get-tuple-element.51), channel_id=1, source_target_pairs={{0,2},{1,3},{2,0},{3,1},{4,6},{5,7},{6,4},{7,5},{8,10},{9,11},{10,... | collective-permute-start | bytes 196616 | tf_op jit(solution)/shard_map/ppermute | solution.py:334
  27.2 2.6 %collective-permute-done.12.refs_7_.refs_6_ = bf16[16,2048]{1,0:T(8,128)(2,1)S(1)} collective-permute-done((bf16[16,2048]{1,0:T(8,128)(2,1)S(1)}, bf16[16,2048]{1,0:T(8,128)(2,1)S(1)}, u32[]{:S(2)}, u32[]{:S(2)}) %collective-permute-start.12) | collective-permute-done | bytes 65568 | tf_op jit(solution)/shard_map/ppermute | solution.py:334
  32.6 2.4 %collective-permute-done.13.refs_1_ = bf16[64,2048]{1,0:T(8,128)(2,1)S(1)} collective-permute-done((bf16[64,2048]{1,0:T(8,128)(2,1)S(1)}, bf16[64,2048]{1,0:T(8,128)(2,1)S(1)}, u32[]{:S(2)}, u32[]{:S(2)}) %collective-permute-start.13) | collective-permute-done | bytes 262176 | tf_op jit(solution)/shard_map/ppermute | solution.py:330
  35.0 2.2 %collective-permute-done.14.refs_2_ = bf16[64,2048]{1,0:T(8,128)(2,1)S(1)} collective-permute-done((bf16[64,2048]{1,0:T(8,128)(2,1)S(1)}, bf16[64,2048]{1,0:T(8,128)(2,1)S(1)}, u32[]{:S(2)}, u32[]{:S(2)}) %collective-permute-start.14) | collective-permute-done | bytes 262176 | tf_op jit(solution)/shard_map/ppermute | solution.py:330
  37.5 3.0 %collective-permute-start.19 = (bf16[64,2048]{1,0:T(8,128)(2,1)S(1)}, bf16[64,2048]{1,0:T(8,128)(2,1)S(1)}, u32[]{:S(2)}, u32[]{:S(2)}) collective-permute-start(bf16[64,2048]{1,0:T(8,128)(2,1)S(1)} %get-tuple-element.55.refs_0_.refs_1_), channel_id=1, source_target_pairs={{2,240},{3,2},{1,3},{0,1},{16,0},{17,16},{19,17},{18,19},{34,18},{... | collective-permute-start | bytes 786440 | tf_op jit(solution)/shard_map/ppermute | solution.py:330
  40.5 1.5 %middle.1 = (f32[256,2048]{1,0:T(8,128)S(1)}, bf16[16,2048]{1,0:T(8,128)(2,1)S(1)}, bf16[16,2048]{1,0:T(8,128)(2,1)S(1)}, bf16[16,2048]{1,0:T(8,128)(2,1)S(1)}, bf16[16,2048]{1,0:T(8,128)(2,1)S(1)}) custom-call(s32[1]{0:T(128)} %bitcast.place_ref, bf16[64,2048]{1,0:T(8,128)(2,1)S(1)} %get-tuple-element.55.refs_0_.refs_1_, ...), custom_call_target="tpu_custom_call" | custom-call | flops 603979776 | bytes 1 | tf_op jit(solution)/shard_map/middle/pallas_call | solution.py:81
  42.0 1.8 %collective-permute-done.19.refs_3_.refs_2_ = bf16[64,2048]{1,0:T(8,128)(2,1)S(1)} collective-permute-done((bf16[64,2048]{1,0:T(8,128)(2,1)S(1)}, bf16[64,2048]{1,0:T(8,128)(2,1)S(1)}, u32[]{:S(2)}, u32[]{:S(2)}) %collective-permute-start.19) | collective-permute-done | bytes 262176 | tf_op jit(solution)/shard_map/ppermute | solution.py:330
  43.8 7.9 %collective-permute-done.18.refs_2_.refs_1_ = bf16[64,2048]{1,0:T(8,128)(2,1)S(1)} collective-permute-done((bf16[64,2048]{1,0:T(8,128)(2,1)S(1)}, bf16[64,2048]{1,0:T(8,128)(2,1)S(1)}, u32[]{:S(2)}, u32[]{:S(2)}) %collective-permute-start.18) | collective-permute-done | bytes 262176 | tf_op jit(solution)/shard_map/ppermute | solution.py:330
  51.7 2.9 %filter_sums.1 = (bf16[256,432]{1,0:T(8,128)(2,1)S(1)}, bf16[256,432]{1,0:T(8,128)(2,1)S(1)}, bf16[256,432]{1,0:T(8,128)(2,1)S(1)}, bf16[256,432]{1,0:T(8,128)(2,1)S(1)}) custom-call(s32[1]{0:T(128)} %bitcast.place_ref, bf16[256,2048]{1,0:T(8,128)(2,1)S(1)} %get-tuple-element.49.refs_0_, bf16[64,2048]{1,0:T(8,128)(2,1)S(1)} %get-tuple-element.55.refs_0_.refs_1_, ...), custom_call_target="tpu_custom_call" | custom-call | flops 1 | bytes 1 | tf_op jit(solution)/shard_map/filter_sums/pallas_call | solution.py:81
  55.3 4.8 %collective-permute-start.16 = (bf16[16,2048]{1,0:T(8,128)(2,1)S(1)}, bf16[16,2048]{1,0:T(8,128)(2,1)S(1)}, u32[]{:S(2)}, u32[]{:S(2)}) collective-permute-start(bf16[16,2048]{1,0:T(8,128)(2,1)S(1)} %get-tuple-element.59), channel_id=1, source_target_pairs={{0,2},{1,3},{2,0},{3,1},{4,6},{5,7},{6,4},{7,5},{8,10},{9,11},{10,... | collective-permute-start | bytes 196616 | tf_op jit(solution)/shard_map/ppermute | solution.py:334
  60.1 2.3 %collective-permute-done.16.refs_9_.refs_2_ = bf16[16,2048]{1,0:T(8,128)(2,1)S(1)} collective-permute-done((bf16[16,2048]{1,0:T(8,128)(2,1)S(1)}, bf16[16,2048]{1,0:T(8,128)(2,1)S(1)}, u32[]{:S(2)}, u32[]{:S(2)}) %collective-permute-start.16) | collective-permute-done | bytes 65568 | tf_op jit(solution)/shard_map/ppermute | solution.py:334
  62.4 1.8 %collective-permute-done.17.refs_10_.refs_3_ = bf16[16,2048]{1,0:T(8,128)(2,1)S(1)} collective-permute-done((bf16[16,2048]{1,0:T(8,128)(2,1)S(1)}, bf16[16,2048]{1,0:T(8,128)(2,1)S(1)}, u32[]{:S(2)}, u32[]{:S(2)}) %collective-permute-start.17) | collective-permute-done | bytes 65568 | tf_op jit(solution)/shard_map/ppermute | solution.py:334
  64.2 2.9 %input_sums.1 = (f32[64,2048]{1,0:T(8,128)S(1)}, bf16[32,2048]{1,0:T(8,128)(2,1)S(1)}, bf16[32,2048]{1,0:T(8,128)(2,1)S(1)}, bf16[32,2048]{1,0:T(8,128)(2,1)S(1)...) custom-call(s32[1]{0:T(128)} %bitcast.place_ref, ...), custom_call_target="tpu_custom_call" | custom-call | flops 1 | bytes 1 | tf_op jit(solution)/shard_map/input_sums/pallas_call | solution.py:81
  68.7 1.5 %collective-permute-start.31 = (bf16[256,432]{1,0:T(8,128)(2,1)S(1)}, bf16[256,432]{1,0:T(8,128)(2,1)S(1)}, u32[]{:S(2)}, u32[]{:S(2)}) collective-permute-start(bf16[256,432]{1,0:T(8,128)(2,1)S(1)} %lift.1.refs_4_), channel_id=1, source_target_pairs={{0,2},{1,3},{2,0},{3,1},{4,6},{5,7},{6,4},{7,5},{8,10},{9,11},{10,... | collective-permute-start | bytes 663560 | tf_op jit(solution)/shard_map/ppermute | solution.py:334
  70.8 2.0 %collective-permute-start.27 = (bf16[32,2048]{1,0:T(8,128)(2,1)S(1)}, bf16[32,2048]{1,0:T(8,128)(2,1)S(1)}, u32[]{:S(2)}, u32[]{:S(2)}) collective-permute-start(bf16[32,2048]{1,0:T(8,128)(2,1)S(1)} %get-tuple-element.74), channel_id=1, source_target_pairs={{0,12},{4,8},{8,4},{12,0},{1,13},{5,9},{9,5},{13,1},{2,14},{6,10},... | collective-permute-start | bytes 393224 | tf_op jit(solution)/shard_map/ppermute | solution.py:334
  73.5 1.7 %collective-permute-start.26 = (bf16[32,2048]{1,0:T(8,128)(2,1)S(1)}, bf16[32,2048]{1,0:T(8,128)(2,1)S(1)}, u32[]{:S(2)}, u32[]{:S(2)}) collective-permute-start(bf16[32,2048]{1,0:T(8,128)(2,1)S(1)} %get-tuple-element.73), channel_id=1, source_target_pairs={{0,12},{4,8},{8,4},{12,0},{1,13},{5,9},{9,5},{13,1},{2,14},{6,10},... | collective-permute-start | bytes 393224 | tf_op jit(solution)/shard_map/ppermute | solution.py:334
  75.8 1.7 %collective-permute-done.25.refs_2_.refs_4_ = bf16[32,2048]{1,0:T(8,128)(2,1)S(1)} collective-permute-done((bf16[32,2048]{1,0:T(8,128)(2,1)S(1)}, bf16[32,2048]{1,0:T(8,128)(2,1)S(1)}, u32[]{:S(2)}, u32[]{:S(2)}) %collective-permute-start.25) | collective-permute-done | bytes 131104 | tf_op jit(solution)/shard_map/ppermute | solution.py:334
  77.5 1.5 %collective-permute-done.26.refs_3_.refs_5_ = bf16[32,2048]{1,0:T(8,128)(2,1)S(1)} collective-permute-done((bf16[32,2048]{1,0:T(8,128)(2,1)S(1)}, bf16[32,2048]{1,0:T(8,128)(2,1)S(1)}, u32[]{:S(2)}, u32[]{:S(2)}) %collective-permute-start.26) | collective-permute-done | bytes 131104 | tf_op jit(solution)/shard_map/ppermute | solution.py:334
  79.8 3.5 %all-to-all-start = ((bf16[16,16,432]{2,1,0:T(8,128)(2,1)}), bf16[16,16,432]{2,1,0:T(8,128)(2,1)S(1)}, u32[]{:S(2)}, u32[]{:S(2)}) async-start(bf16[16,16,432]{2,1,0:T(8,128)(2,1)} %bitcast.6), calls=%async_computation | async-start | bytes 524288 | tf_op jit(solution)/shard_map/all_to_all | solution.py:481
  83.5 2.9 %collective-permute-start.28 = (bf16[16,2048]{1,0:T(8,128)(2,1)S(1)}, bf16[16,2048]{1,0:T(8,128)(2,1)S(1)}, u32[]{:S(2)}, u32[]{:S(2)}) collective-permute-start(bf16[16,2048]{1,0:T(8,128)(2,1)S(1)} %get-tuple-element.76), channel_id=1, source_target_pairs={{0,1},{1,0},{2,3},{3,2},{4,5},{5,4},{6,7},{7,6},{8,9},{9,8},{10,11... | collective-permute-start | bytes 196616 | tf_op jit(solution)/shard_map/ppermute | solution.py:334
  86.4 1.2 %collective-permute-start.29 = (bf16[16,2048]{1,0:T(8,128)(2,1)S(1)}, bf16[16,2048]{1,0:T(8,128)(2,1)S(1)}, u32[]{:S(2)}, u32[]{:S(2)}) collective-permute-start(bf16[16,2048]{1,0:T(8,128)(2,1)S(1)} %get-tuple-element.77), channel_id=1, source_target_pairs={{0,2},{1,3},{2,0},{3,1},{4,6},{5,7},{6,4},{7,5},{8,10},{9,11},{10,... | collective-permute-start | bytes 196616 | tf_op jit(solution)/shard_map/ppermute | solution.py:334
  88.1 2.5 %collective-permute-done.29.refs_6_ = bf16[16,2048]{1,0:T(8,128)(2,1)S(1)} collective-permute-done((bf16[16,2048]{1,0:T(8,128)(2,1)S(1)}, bf16[16,2048]{1,0:T(8,128)(2,1)S(1)}, u32[]{:S(2)}, u32[]{:S(2)}) %collective-permute-start.29) | collective-permute-done | bytes 65568 | tf_op jit(solution)/shard_map/ppermute | solution.py:334
  90.6 2.6 %collective-permute-done.30.refs_7_ = bf16[16,2048]{1,0:T(8,128)(2,1)S(1)} collective-permute-done((bf16[16,2048]{1,0:T(8,128)(2,1)S(1)}, bf16[16,2048]{1,0:T(8,128)(2,1)S(1)}, u32[]{:S(2)}, u32[]{:S(2)}) %collective-permute-start.30) | collective-permute-done | bytes 65568 | tf_op jit(solution)/shard_map/ppermute | solution.py:334
  (57 shorter events, 16.2 us)
Async XLA Ops:
  1.7 7.1 %collective-permute-start = (bf16[16,2048]{1,0:T(8,128)(2,1)S(1)}, bf16[16,2048]{1,0:T(8,128)(2,1)S(1)}, u32[]{:S(2)}, u32[]{:S(2)}) collective-permute-start(bf16[16,2048]{1,0:T(8,128)(2,1)S(1)} %get-tuple-element.43), channel_id=1, source_target_pairs={{0,1},{1,0},{2,3},{3,2},{4,5},{5,4},{6,7},{7,6},{8,9},{9,8},{10,11... | collective-permute-start | bytes 196616 | tf_op jit(solution)/shard_map/ppermute | solution.py:334
  5.0 3.8 %collective-permute-start.1 = (bf16[16,2048]{1,0:T(8,128)(2,1)S(1)}, bf16[16,2048]{1,0:T(8,128)(2,1)S(1)}, u32[]{:S(2)}, u32[]{:S(2)}) collective-permute-start(bf16[16,2048]{1,0:T(8,128)(2,1)S(1)} %get-tuple-element.44), channel_id=1, source_target_pairs={{0,2},{1,3},{2,0},{3,1},{4,6},{5,7},{6,4},{7,5},{8,10},{9,11},{10,... | collective-permute-start | bytes 196616 | tf_op jit(solution)/shard_map/ppermute | solution.py:334
  5.0 5.2 %collective-permute-start.2 = (bf16[16,2048]{1,0:T(8,128)(2,1)S(1)}, bf16[16,2048]{1,0:T(8,128)(2,1)S(1)}, u32[]{:S(2)}, u32[]{:S(2)}) collective-permute-start(bf16[16,2048]{1,0:T(8,128)(2,1)S(1)} %get-tuple-element.45), channel_id=1, source_target_pairs={{0,3},{1,2},{2,1},{3,0},{4,7},{5,6},{6,5},{7,4},{8,11},{9,10},{10,... | collective-permute-start | bytes 196616 | tf_op jit(solution)/shard_map/ppermute | solution.py:334
  10.3 9.0 %collective-permute-start.4 = (bf16[64,2048]{1,0:T(8,128)(2,1)S(1)}, bf16[64,2048]{1,0:T(8,128)(2,1)S(1)}, u32[]{:S(2)}, u32[]{:S(2)}) collective-permute-start(bf16[64,2048]{1,0:T(8,128)(2,1)S(1)} %order.1.refs_0_), channel_id=1, source_target_pairs={{0,12},{4,8},{8,4},{12,0},{1,13},{5,9},{9,5},{13,1},{2,14},{6,10},... | collective-permute-start | bytes 786440 | tf_op jit(solution)/shard_map/ppermute | solution.py:334
  11.4 7.9 %collective-permute-start.3 = (bf16[64,2048]{1,0:T(8,128)(2,1)S(1)}, bf16[64,2048]{1,0:T(8,128)(2,1)S(1)}, u32[]{:S(2)}, u32[]{:S(2)}) collective-permute-start(bf16[64,2048]{1,0:T(8,128)(2,1)S(1)} %order.1.refs_0_), channel_id=1, source_target_pairs={{0,4},{4,0},{8,12},{12,8},{1,5},{5,1},{9,13},{13,9},{2,6},{6,2},{1... | collective-permute-start | bytes 786440 | tf_op jit(solution)/shard_map/ppermute | solution.py:334
  11.4 9.1 %collective-permute-start.9 = (bf16[432,256]{1,0:T(8,128)(2,1)S(1)}, bf16[432,256]{1,0:T(8,128)(2,1)S(1)}, u32[]{:S(2)}, u32[]{:S(2)}) collective-permute-start(bf16[432,256]{1,0:T(8,128)(2,1)S(1)} %get-tuple-element.46.refs_4_.refs_5_.refs_1_.refs_2_.refs_3_), channel_id=1, source_target_pairs={{0,3},{1,2},{2,1},{3,0},{4,7},{5,6},{6,5},{7,4},{8,11},{9,10},{10,... | collective-permute-start | bytes 663560 | tf_op jit(solution)/shard_map/ppermute | solution.py:334
  13.1 11.0 %collective-permute-start.8 = (bf16[432,256]{1,0:T(8,128)(2,1)S(1)}, bf16[432,256]{1,0:T(8,128)(2,1)S(1)}, u32[]{:S(2)}, u32[]{:S(2)}) collective-permute-start(bf16[432,256]{1,0:T(8,128)(2,1)S(1)} %get-tuple-element.46.refs_4_.refs_5_.refs_1_.refs_2_.refs_3_), channel_id=1, source_target_pairs={{0,2},{1,3},{2,0},{3,1},{4,6},{5,7},{6,4},{7,5},{8,10},{9,11},{10,... | collective-permute-start | bytes 663560 | tf_op jit(solution)/shard_map/ppermute | solution.py:334
  13.6 11.7 %collective-permute-start.7 = (bf16[432,256]{1,0:T(8,128)(2,1)S(1)}, bf16[432,256]{1,0:T(8,128)(2,1)S(1)}, u32[]{:S(2)}, u32[]{:S(2)}) collective-permute-start(bf16[432,256]{1,0:T(8,128)(2,1)S(1)} %get-tuple-element.46.refs_4_.refs_5_.refs_1_.refs_2_.refs_3_), channel_id=1, source_target_pairs={{0,1},{1,0},{2,3},{3,2},{4,5},{5,4},{6,7},{7,6},{8,9},{9,8},{10,11... | collective-permute-start | bytes 663560 | tf_op jit(solution)/shard_map/ppermute | solution.py:334
  19.3 6.8 %collective-permute-start.5 = (bf16[32,2048]{1,0:T(8,128)(2,1)S(1)}, bf16[32,2048]{1,0:T(8,128)(2,1)S(1)}, u32[]{:S(2)}, u32[]{:S(2)}) collective-permute-start(bf16[32,2048]{1,0:T(8,128)(2,1)S(1)} %get-tuple-element.47), channel_id=1, source_target_pairs={{0,12},{4,8},{8,4},{12,0},{1,13},{5,9},{9,5},{13,1},{2,14},{6,10},... | collective-permute-start | bytes 393224 | tf_op jit(solution)/shard_map/ppermute | solution.py:334
  20.6 5.6 %collective-permute-start.6 = (bf16[32,2048]{1,0:T(8,128)(2,1)S(1)}, bf16[32,2048]{1,0:T(8,128)(2,1)S(1)}, u32[]{:S(2)}, u32[]{:S(2)}) collective-permute-start(bf16[32,2048]{1,0:T(8,128)(2,1)S(1)} %get-tuple-element.48), channel_id=1, source_target_pairs={{0,4},{4,0},{8,12},{12,8},{1,5},{5,1},{9,13},{13,9},{2,6},{6,2},{1... | collective-permute-start | bytes 393224 | tf_op jit(solution)/shard_map/ppermute | solution.py:334
  20.6 6.6 %collective-permute-start.10 = (bf16[16,2048]{1,0:T(8,128)(2,1)S(1)}, bf16[16,2048]{1,0:T(8,128)(2,1)S(1)}, u32[]{:S(2)}, u32[]{:S(2)}) collective-permute-start(bf16[16,2048]{1,0:T(8,128)(2,1)S(1)} %get-tuple-element.50), channel_id=1, source_target_pairs={{0,1},{1,0},{2,3},{3,2},{4,5},{5,4},{6,7},{7,6},{8,9},{9,8},{10,11... | collective-permute-start | bytes 196616 | tf_op jit(solution)/shard_map/ppermute | solution.py:334
  25.2 4.6 %collective-permute-start.12 = (bf16[16,2048]{1,0:T(8,128)(2,1)S(1)}, bf16[16,2048]{1,0:T(8,128)(2,1)S(1)}, u32[]{:S(2)}, u32[]{:S(2)}) collective-permute-start(bf16[16,2048]{1,0:T(8,128)(2,1)S(1)} %get-tuple-element.52), channel_id=1, source_target_pairs={{0,3},{1,2},{2,1},{3,0},{4,7},{5,6},{6,5},{7,4},{8,11},{9,10},{10,... | collective-permute-start | bytes 196616 | tf_op jit(solution)/shard_map/ppermute | solution.py:334
  30.8 4.2 %collective-permute-start.13 = (bf16[64,2048]{1,0:T(8,128)(2,1)S(1)}, bf16[64,2048]{1,0:T(8,128)(2,1)S(1)}, u32[]{:S(2)}, u32[]{:S(2)}) collective-permute-start(bf16[64,2048]{1,0:T(8,128)(2,1)S(1)} %before.1.refs_5_), channel_id=1, source_target_pairs={{2,240},{3,2},{1,3},{0,1},{16,0},{17,16},{19,17},{18,19},{34,18},{... | collective-permute-start | bytes 786440 | tf_op jit(solution)/shard_map/ppermute | solution.py:330
  31.7 5.5 %collective-permute-start.14 = (bf16[64,2048]{1,0:T(8,128)(2,1)S(1)}, bf16[64,2048]{1,0:T(8,128)(2,1)S(1)}, u32[]{:S(2)}, u32[]{:S(2)}) collective-permute-start(bf16[64,2048]{1,0:T(8,128)(2,1)S(1)} %get-tuple-element.53), channel_id=1, source_target_pairs={{2,3},{3,1},{1,0},{0,16},{16,17},{17,19},{19,18},{18,34},{34,35},{... | collective-permute-start | bytes 786440 | tf_op jit(solution)/shard_map/ppermute | solution.py:330
  37.5 6.3 %collective-permute-start.19 = (bf16[64,2048]{1,0:T(8,128)(2,1)S(1)}, bf16[64,2048]{1,0:T(8,128)(2,1)S(1)}, u32[]{:S(2)}, u32[]{:S(2)}) collective-permute-start(bf16[64,2048]{1,0:T(8,128)(2,1)S(1)} %get-tuple-element.55.refs_0_.refs_1_), channel_id=1, source_target_pairs={{2,240},{3,2},{1,3},{0,1},{16,0},{17,16},{19,17},{18,19},{34,18},{... | collective-permute-start | bytes 786440 | tf_op jit(solution)/shard_map/ppermute | solution.py:330
  40.5 11.2 %collective-permute-start.18 = (bf16[64,2048]{1,0:T(8,128)(2,1)S(1)}, bf16[64,2048]{1,0:T(8,128)(2,1)S(1)}, u32[]{:S(2)}, u32[]{:S(2)}) collective-permute-start(bf16[64,2048]{1,0:T(8,128)(2,1)S(1)} %get-tuple-element.55.refs_0_.refs_1_), channel_id=1, source_target_pairs={{2,3},{3,1},{1,0},{0,16},{16,17},{17,19},{19,18},{18,34},{34,35},{... | collective-permute-start | bytes 786440 | tf_op jit(solution)/shard_map/ppermute | solution.py:330
  54.6 14.0 %collective-permute-start.23 = (bf16[256,432]{1,0:T(8,128)(2,1)S(1)}, bf16[256,432]{1,0:T(8,128)(2,1)S(1)}, u32[]{:S(2)}, u32[]{:S(2)}) collective-permute-start(bf16[256,432]{1,0:T(8,128)(2,1)S(1)} %get-tuple-element.70), channel_id=1, source_target_pairs={{0,1},{1,0},{2,3},{3,2},{4,5},{5,4},{6,7},{7,6},{8,9},{9,8},{10,11... | collective-permute-start | bytes 663560 | tf_op jit(solution)/shard_map/ppermute | solution.py:334
  54.7 13.9 %collective-permute-start.24 = (bf16[256,432]{1,0:T(8,128)(2,1)S(1)}, bf16[256,432]{1,0:T(8,128)(2,1)S(1)}, u32[]{:S(2)}, u32[]{:S(2)}) collective-permute-start(bf16[256,432]{1,0:T(8,128)(2,1)S(1)} %get-tuple-element.71), channel_id=1, source_target_pairs={{0,1},{1,0},{2,3},{3,2},{4,5},{5,4},{6,7},{7,6},{8,9},{9,8},{10,11... | collective-permute-start | bytes 663560 | tf_op jit(solution)/shard_map/ppermute | solution.py:334
  55.2 4.9 %collective-permute-start.15 = (bf16[16,2048]{1,0:T(8,128)(2,1)S(1)}, bf16[16,2048]{1,0:T(8,128)(2,1)S(1)}, u32[]{:S(2)}, u32[]{:S(2)}) collective-permute-start(bf16[16,2048]{1,0:T(8,128)(2,1)S(1)} %get-tuple-element.58), channel_id=1, source_target_pairs={{0,1},{1,0},{2,3},{3,2},{4,5},{5,4},{6,7},{7,6},{8,9},{9,8},{10,11... | collective-permute-start | bytes 196616 | tf_op jit(solution)/shard_map/ppermute | solution.py:334
  55.3 7.1 %collective-permute-start.16 = (bf16[16,2048]{1,0:T(8,128)(2,1)S(1)}, bf16[16,2048]{1,0:T(8,128)(2,1)S(1)}, u32[]{:S(2)}, u32[]{:S(2)}) collective-permute-start(bf16[16,2048]{1,0:T(8,128)(2,1)S(1)} %get-tuple-element.59), channel_id=1, source_target_pairs={{0,2},{1,3},{2,0},{3,1},{4,6},{5,7},{6,4},{7,5},{8,10},{9,11},{10,... | collective-permute-start | bytes 196616 | tf_op jit(solution)/shard_map/ppermute | solution.py:334
  60.1 4.1 %collective-permute-start.17 = (bf16[16,2048]{1,0:T(8,128)(2,1)S(1)}, bf16[16,2048]{1,0:T(8,128)(2,1)S(1)}, u32[]{:S(2)}, u32[]{:S(2)}) collective-permute-start(bf16[16,2048]{1,0:T(8,128)(2,1)S(1)} %get-tuple-element.60), channel_id=1, source_target_pairs={{0,3},{1,2},{2,1},{3,0},{4,7},{5,6},{6,5},{7,4},{8,11},{9,10},{10,... | collective-permute-start | bytes 196616 | tf_op jit(solution)/shard_map/ppermute | solution.py:334
  67.1 6.0 %collective-permute-start.21 = (bf16[32,2048]{1,0:T(8,128)(2,1)S(1)}, bf16[32,2048]{1,0:T(8,128)(2,1)S(1)}, u32[]{:S(2)}, u32[]{:S(2)}) collective-permute-start(bf16[32,2048]{1,0:T(8,128)(2,1)S(1)} %get-tuple-element.67), channel_id=1, source_target_pairs={{0,12},{4,8},{8,4},{12,0},{1,13},{5,9},{9,5},{13,1},{2,14},{6,10},... | collective-permute-start | bytes 393224 | tf_op jit(solution)/shard_map/ppermute | solution.py:334
  67.8 5.3 %collective-permute-start.22 = (bf16[32,2048]{1,0:T(8,128)(2,1)S(1)}, bf16[32,2048]{1,0:T(8,128)(2,1)S(1)}, u32[]{:S(2)}, u32[]{:S(2)}) collective-permute-start(bf16[32,2048]{1,0:T(8,128)(2,1)S(1)} %get-tuple-element.68), channel_id=1, source_target_pairs={{0,4},{4,0},{8,12},{12,8},{1,5},{5,1},{9,13},{13,9},{2,6},{6,2},{1... | collective-permute-start | bytes 393224 | tf_op jit(solution)/shard_map/ppermute | solution.py:334
  68.7 10.3 %collective-permute-start.31 = (bf16[256,432]{1,0:T(8,128)(2,1)S(1)}, bf16[256,432]{1,0:T(8,128)(2,1)S(1)}, u32[]{:S(2)}, u32[]{:S(2)}) collective-permute-start(bf16[256,432]{1,0:T(8,128)(2,1)S(1)} %lift.1.refs_4_), channel_id=1, source_target_pairs={{0,2},{1,3},{2,0},{3,1},{4,6},{5,7},{6,4},{7,5},{8,10},{9,11},{10,... | collective-permute-start | bytes 663560 | tf_op jit(solution)/shard_map/ppermute | solution.py:334
  70.2 5.1 %collective-permute-start.20 = (bf16[32,2048]{1,0:T(8,128)(2,1)S(1)}, bf16[32,2048]{1,0:T(8,128)(2,1)S(1)}, u32[]{:S(2)}, u32[]{:S(2)}) collective-permute-start(bf16[32,2048]{1,0:T(8,128)(2,1)S(1)} %get-tuple-element.64), channel_id=1, source_target_pairs={{0,4},{4,0},{8,12},{12,8},{1,5},{5,1},{9,13},{13,9},{2,6},{6,2},{1... | collective-permute-start | bytes 393224 | tf_op jit(solution)/shard_map/ppermute | solution.py:334
  70.8 5.0 %collective-permute-start.27 = (bf16[32,2048]{1,0:T(8,128)(2,1)S(1)}, bf16[32,2048]{1,0:T(8,128)(2,1)S(1)}, u32[]{:S(2)}, u32[]{:S(2)}) collective-permute-start(bf16[32,2048]{1,0:T(8,128)(2,1)S(1)} %get-tuple-element.74), channel_id=1, source_target_pairs={{0,12},{4,8},{8,4},{12,0},{1,13},{5,9},{9,5},{13,1},{2,14},{6,10},... | collective-permute-start | bytes 393224 | tf_op jit(solution)/shard_map/ppermute | solution.py:334
  73.1 4.4 %collective-permute-start.25 = (bf16[32,2048]{1,0:T(8,128)(2,1)S(1)}, bf16[32,2048]{1,0:T(8,128)(2,1)S(1)}, u32[]{:S(2)}, u32[]{:S(2)}) collective-permute-start(bf16[32,2048]{1,0:T(8,128)(2,1)S(1)} %get-tuple-element.72), channel_id=1, source_target_pairs={{0,4},{4,0},{8,12},{12,8},{1,5},{5,1},{9,13},{13,9},{2,6},{6,2},{1... | collective-permute-start | bytes 393224 | tf_op jit(solution)/shard_map/ppermute | solution.py:334
  73.5 5.5 %collective-permute-start.26 = (bf16[32,2048]{1,0:T(8,128)(2,1)S(1)}, bf16[32,2048]{1,0:T(8,128)(2,1)S(1)}, u32[]{:S(2)}, u32[]{:S(2)}) collective-permute-start(bf16[32,2048]{1,0:T(8,128)(2,1)S(1)} %get-tuple-element.73), channel_id=1, source_target_pairs={{0,12},{4,8},{8,4},{12,0},{1,13},{5,9},{9,5},{13,1},{2,14},{6,10},... | collective-permute-start | bytes 393224 | tf_op jit(solution)/shard_map/ppermute | solution.py:334
  79.8 14.3 %all-to-all-start = ((bf16[16,16,432]{2,1,0:T(8,128)(2,1)}), bf16[16,16,432]{2,1,0:T(8,128)(2,1)S(1)}, u32[]{:S(2)}, u32[]{:S(2)}) async-start(bf16[16,16,432]{2,1,0:T(8,128)(2,1)} %bitcast.6), calls=%async_computation | async-start | bytes 524288 | tf_op jit(solution)/shard_map/all_to_all | solution.py:481
  83.5 4.6 %collective-permute-start.28 = (bf16[16,2048]{1,0:T(8,128)(2,1)S(1)}, bf16[16,2048]{1,0:T(8,128)(2,1)S(1)}, u32[]{:S(2)}, u32[]{:S(2)}) collective-permute-start(bf16[16,2048]{1,0:T(8,128)(2,1)S(1)} %get-tuple-element.76), channel_id=1, source_target_pairs={{0,1},{1,0},{2,3},{3,2},{4,5},{5,4},{6,7},{7,6},{8,9},{9,8},{10,11... | collective-permute-start | bytes 196616 | tf_op jit(solution)/shard_map/ppermute | solution.py:334
  86.4 4.2 %collective-permute-start.29 = (bf16[16,2048]{1,0:T(8,128)(2,1)S(1)}, bf16[16,2048]{1,0:T(8,128)(2,1)S(1)}, u32[]{:S(2)}, u32[]{:S(2)}) collective-permute-start(bf16[16,2048]{1,0:T(8,128)(2,1)S(1)} %get-tuple-element.77), channel_id=1, source_target_pairs={{0,2},{1,3},{2,0},{3,1},{4,6},{5,7},{6,4},{7,5},{8,10},{9,11},{10,... | collective-permute-start | bytes 196616 | tf_op jit(solution)/shard_map/ppermute | solution.py:334
  87.5 5.6 %collective-permute-start.30 = (bf16[16,2048]{1,0:T(8,128)(2,1)S(1)}, bf16[16,2048]{1,0:T(8,128)(2,1)S(1)}, u32[]{:S(2)}, u32[]{:S(2)}) collective-permute-start(bf16[16,2048]{1,0:T(8,128)(2,1)S(1)} %get-tuple-element.78), channel_id=1, source_target_pairs={{0,3},{1,2},{2,1},{3,0},{4,7},{5,6},{6,5},{7,4},{8,11},{9,10},{10,... | collective-permute-start | bytes 196616 | tf_op jit(solution)/shard_map/ppermute | solution.py:334
  (4 other events, 6.0 us)
